TPU v7x, 512 devices: a whole 4x8x8 slice. The times are simulated.
512 devices in a mesh: dp: 32 (over y, x), seq: 16 (over z, core).
Axes of the slice: x: 4, y: 8, z: 8, core: 2. Of those that a mesh axis runs over, the one named last changes fastest.
Arguments:
- patches: bfloat16 [32, 768, 1408], P('dp', 'seq'), may hold values from -6 to 6
- keep_pos: int32 [32, 768], P('dp', 'seq'), may hold values from -1 to 4095, as said below
- kept_counts: int32 [32, 16], P('dp'), may hold values from 16 to 48, as said below
- enc_gain: float32 [1408], replicated, may hold values from 0.25 to 1.75
- w_qkv: bfloat16 [3, 1408, 1408], P(None, None, 'seq'), may hold values from -2 to 2
- w_out: bfloat16 [1408, 1408], P('seq'), may hold values from -12 to 12
- w_e2d: bfloat16 [1408, 512], replicated, may hold values from -0.15625 to 0.15625
- mask_token: bfloat16 [512], replicated, may hold values from -4 to 4
- dec_gain: float32 [512], replicated, may hold values from 0.25 to 1.75
- fc_in: bfloat16 [2048, 512], P('seq'), may hold values from -0.25 to 0.25
- fc_out: bfloat16 [2048, 512], P('seq'), may hold values from -0.125 to 0.125
- cotangent: bfloat16 [32, 4096, 512], P('dp', 'seq'), may hold values from -6 to 6
Outputs:
- recon: bfloat16 [32, 4096, 512], P('dp', 'seq')
- grad_qkv: bfloat16 [3, 1408, 1408], P(None, None, 'seq')
- grad_out: bfloat16 [1408, 1408], P('seq')
Inputs may be any that keep to these rules, and one draw needn't show every extreme that they name: `keep_pos`: rows j < kept_counts[s] of device s's block hold distinct tube positions of the clip, the other rows -1; no device's block holds more than 3 positions of one range of 256 positions; in every clip some device holds exactly 3 in every range, and some range receives exactly 3 from every device. `kept_counts`: the counts of a clip sum to 430; some device holds exactly 48.
All inputs are finite; a program needn't handle non-finite values.
Results may differ from a plain program's by a relative error of at most 0.03.
Values may be sent and summed in bfloat16 or wider, within the bound.
No kernel may reach another device: no remote copies, remote signals or barrier semaphores. Data moves between devices by JAX's collectives and lax.ppermute only.
A program may use at most 64 MiB of HBM per device.

v0:
```python
import jax
import jax.numpy as jnp
from jax import lax
from jax.sharding import PartitionSpec as P

HD = 88
DD = 512


def layer_norm(values, gain):
    mean = jnp.mean(values, axis=-1, keepdims=True)
    centred = values - mean
    var = jnp.mean(centred * centred, axis=-1, keepdims=True)
    return centred * lax.rsqrt(var + 1e-06) * gain


def layer_norm_back(values, gain, upstream):
    mean = jnp.mean(values, axis=-1, keepdims=True)
    centred = values - mean
    var = jnp.mean(centred * centred, axis=-1, keepdims=True)
    inv_std = lax.rsqrt(var + 1e-06)
    normed = centred * inv_std
    scaled = upstream * gain
    first = jnp.mean(scaled, axis=-1, keepdims=True)
    second = jnp.mean(scaled * normed, axis=-1, keepdims=True)
    return inv_std * (scaled - first - normed * second)


def gelu_slope(h):
    cdf = 0.5 * (1.0 + jax.scipy.special.erf(h * 0.7071067811865476))
    pdf = jnp.exp(-0.5 * h * h) * 0.3989422804014327
    return cdf + h * pdf


def position_table(positions, width):
    half = width // 2
    freq = 10000.0 ** (-(jnp.arange(half, dtype=jnp.float32) * 2.0 / width))
    angle = positions[:, None] * freq[None, :]
    return jnp.concatenate([jnp.sin(angle), jnp.cos(angle)], axis=1)


def local(
    patches,
    keep_pos,
    kept_counts,
    enc_gain,
    w_qkv,
    w_out,
    w_e2d,
    mask_token,
    dec_gain,
    fc_in,
    fc_out,
    cotangent,
):
    slots_each = patches.shape[1]
    groups = lax.axis_size("seq")
    me = lax.axis_index("seq")
    fdev = cotangent.shape[1]
    local_width = w_out.shape[0]
    heads_here = local_width // HD
    scale = HD ** (-0.5)
    x_rows = patches[0]
    counts = kept_counts[0]
    own_keep = keep_pos[0]
    cot = cotangent[0]
    every = groups * slots_each
    index = jnp.arange(every, dtype=jnp.int32)
    live = index % slots_each < counts[index // slots_each]
    own_count = lax.dynamic_index_in_dim(counts, me, keepdims=False)
    own_live = jnp.arange(slots_each, dtype=jnp.int32) < own_count
    gathered = lax.all_gather(x_rows, "seq", axis=0, tiled=True)
    count = gathered.shape[0]
    xn = layer_norm(gathered.astype(jnp.float32), enc_gain).astype(jnp.bfloat16)
    query = (
        (jnp.dot(xn, w_qkv[0], preferred_element_type=jnp.float32) * scale)
        .astype(jnp.bfloat16)
        .reshape(count, heads_here, HD)
    )
    keys = (
        jnp.dot(xn, w_qkv[1], preferred_element_type=jnp.float32)
        .astype(jnp.bfloat16)
        .reshape(count, heads_here, HD)
    )
    values = (
        jnp.dot(xn, w_qkv[2], preferred_element_type=jnp.float32)
        .astype(jnp.bfloat16)
        .reshape(count, heads_here, HD)
    )
    scores = jnp.einsum("qhd,khd->hqk", query, keys, preferred_element_type=jnp.float32)
    scores = jnp.where(live[None, None, :], scores, -jnp.inf)
    top = jnp.max(scores, axis=-1, keepdims=True)
    expo = jnp.exp(scores - top)
    probs = expo / jnp.sum(expo, axis=-1, keepdims=True)
    probs_b = probs.astype(jnp.bfloat16)
    ctx = (
        jnp.einsum("hqk,khd->qhd", probs_b, values, preferred_element_type=jnp.float32)
        .astype(jnp.bfloat16)
        .reshape(count, local_width)
    )
    part = (
        jnp.dot(ctx, w_out, preferred_element_type=jnp.float32)
        .astype(jnp.bfloat16)
        .astype(jnp.float32)
    )
    part = jnp.where(live[:, None], part, 0.0)
    summed = lax.psum_scatter(
        part.astype(jnp.bfloat16), "seq", scatter_dimension=0, tiled=True
    ).astype(jnp.float32)
    enc = x_rows.astype(jnp.float32) + summed
    vis = jnp.dot(enc.astype(jnp.bfloat16), w_e2d, preferred_element_type=jnp.float32).astype(
        jnp.bfloat16
    )
    incoming, incoming_pos = (
        lax.all_gather(vis, "seq", axis=0, tiled=True),
        lax.all_gather(own_keep, "seq", axis=0, tiled=True),
    )
    incoming_pos = jnp.where(incoming_pos >= 0, incoming_pos - me * fdev, -1)
    placer = (incoming_pos[None, :] == jnp.arange(fdev, dtype=jnp.int32)[:, None]).astype(
        jnp.bfloat16
    )
    dec_vis = jnp.dot(placer, incoming, preferred_element_type=jnp.float32)
    seen = jnp.sum(placer.astype(jnp.float32), axis=1)
    table = position_table((me * fdev + jnp.arange(fdev, dtype=jnp.int32)).astype(jnp.float32), DD)
    dec_x = jnp.where(seen[:, None] > 0.5, dec_vis, mask_token.astype(jnp.float32)[None, :]) + table
    dn = layer_norm(dec_x, dec_gain).astype(jnp.bfloat16)
    pieces = (
        lax.all_gather(fc_in, "seq", axis=0, tiled=True),
        lax.all_gather(fc_out, "seq", axis=0, tiled=True),
    )
    hidden = jnp.einsum("fd,hd->fh", dn, pieces[0], preferred_element_type=jnp.float32)
    act = jax.nn.gelu(hidden, approximate=False).astype(jnp.bfloat16)
    dact = jnp.einsum("fd,hd->fh", cot, pieces[1], preferred_element_type=jnp.float32)
    dhidden = (dact * gelu_slope(hidden)).astype(jnp.bfloat16)
    mixed_part = jnp.dot(act, pieces[1], preferred_element_type=jnp.float32)
    grad_part = jnp.dot(dhidden, pieces[0], preferred_element_type=jnp.float32)
    recon = (dec_x + mixed_part).astype(jnp.bfloat16)
    ddec = cot.astype(jnp.float32) + layer_norm_back(dec_x, dec_gain, grad_part)
    ddec_b = ddec.astype(jnp.bfloat16)
    back_terms = jnp.dot(placer.T, ddec_b, preferred_element_type=jnp.float32)
    dvis = lax.psum_scatter(back_terms.astype(jnp.bfloat16), "seq", scatter_dimension=0, tiled=True)
    denc = jnp.dot(dvis, w_e2d.T, preferred_element_type=jnp.float32)
    dy_own = jnp.where(own_live[:, None], denc, 0.0).astype(jnp.bfloat16)
    dy_all = lax.all_gather(dy_own, "seq", axis=0, tiled=True)
    dctx = jnp.dot(dy_all, w_out.T, preferred_element_type=jnp.float32).astype(jnp.bfloat16)
    grad_o = jnp.dot(ctx.T, dy_all, preferred_element_type=jnp.float32)
    dctx3 = dctx.reshape(count, heads_here, HD)
    dprob = jnp.einsum("qhd,khd->hqk", dctx3, values, preferred_element_type=jnp.float32)
    inner = jnp.sum(probs * dprob, axis=-1, keepdims=True)
    dscore = (probs * (dprob - inner)).astype(jnp.bfloat16)
    dq = (
        jnp.einsum("hqk,khd->qhd", dscore, keys, preferred_element_type=jnp.float32) * scale
    ).astype(jnp.bfloat16)
    dk = jnp.einsum("hqk,qhd->khd", dscore, query, preferred_element_type=jnp.float32).astype(
        jnp.bfloat16
    )
    dv = jnp.einsum("hqk,qhd->khd", probs_b, dctx3, preferred_element_type=jnp.float32).astype(
        jnp.bfloat16
    )
    grad_q = jnp.stack(
        [
            jnp.dot(xn.T, term.reshape(count, local_width), preferred_element_type=jnp.float32)
            for term in (dq, dk, dv)
        ]
    )
    grad_q, grad_o = (
        lax.psum(grad_q.astype(jnp.bfloat16), "dp").astype(jnp.float32),
        lax.psum(grad_o.astype(jnp.bfloat16), "dp").astype(jnp.float32),
    )
    return (recon[None], grad_q.astype(jnp.bfloat16), grad_o.astype(jnp.bfloat16))


def solution(mesh):
    placed = (
        P("dp", "seq", None),
        P("dp", "seq"),
        P("dp", None),
        P(),
        P(None, None, "seq"),
        P("seq", None),
        P(),
        P(),
        P(),
        P("seq", None),
        P("seq", None),
        P("dp", "seq", None),
    )
    return jax.shard_map(
        local,
        mesh=mesh,
        in_specs=placed,
        out_specs=(P("dp", "seq", None), P(None, None, "seq"), P("seq", None)),
        check_vma=False,
    )
```

profile of v0, /device:TPU:8, one launch (start us, length us, event | category | flops | bytes accessed | tf_op | source)
XLA Modules:
  0.0 516.4 jit_solution(5313282981564815130)
XLA Ops:
  7.2 0.0 copy-start
  7.2 0.0 all-gather.13.cloned.1.call-start
  7.2 0.7 all-gather.13.cloned.1.call-update
  7.9 0.0 reduce-scatter.3.cloned.1.call-start
  8.3 2.0 constant_dynamic-slice_fusion
  10.3 4.4 fusion.102
  14.7 5.6 %fusion.98 = pred[768]{0:T(1024)(128)(4,1)S(1)} fusion(pred[768]{0:T(1024)(128)(4,1)S(1)} %compare_reduce_fusion, pred[768]{0:T(1024)(128)(4,1)S(1)} %compare_reduce_fusion.1, pred[768]{0:T(1024)(128)(4,1)S(1)} %compare_reduce_fusion.2, pred[768]{0:T(1024)(128)(4,1)S(1)} %compare_reduce_fusion.3, pred[768]{0:T(1024)(128)(4,1)S(1)} %compare_reduce_fusion.4, ...), kind=kLoop, calls=%fused_computation.162 | loop fusion | flops 12288 | bytes 10788 | tf_op jit(solution)/shard_map/lt | solution.py:69
  20.4 37.7 %all-gather.13.cloned.1.call-done = bf16[1,768,1408]{2,1,0:T(8,128)(2,1)} async-done(((bf16[1,48,1408]{2,1,0:T(8,128)(2,1)}), bf16[1,768,1408]{2,1,0:T(8,128)(2,1)}) %all-gather.13.cloned.1.call-update) | async-done | bytes 2162704 | tf_op jit(solution)/shard_map/all_gather | solution.py:72
  58.1 2.1 convert_reduce_fusion
  60.2 0.1 copy-done.4
  60.4 0.7 fusion.3
  61.1 0.7 fusion.5
  61.8 0.4 copy-done.6
  62.2 0.8 convolution_convert_fusion.10
  63.0 0.8 fusion.31
  63.9 0.8 convolution_convert_fusion.11
  64.7 0.5 select_reduce_fusion
  65.3 0.5 fusion.26
  65.8 0.7 fusion.32
  66.5 0.2 copy-done.2
  66.7 0.3 copy-done.9
  67.0 2.1 select_convert_fusion
  69.2 0.0 reduce-scatter.3.cloned.1.call-update
  69.2 0.0 all-gather.7.cloned.1.call-start
  69.3 0.7 all-gather.7.cloned.1.call-update
  69.9 0.0 all-gather.9.cloned.1.call-start
  70.0 0.5 all-gather.9.cloned.1.call-update
  70.5 0.0 reduce-scatter.5.cloned.1.call-start
  70.6 1.3 dynamic-slice.1
  72.6 0.1 bitcast_dynamic-update-slice_fusion
  72.7 11.6 %all-reduce = s32[768]{0:T(1024)S(1)} all-reduce(s32[768]{0:T(1024)S(1)} %bitcast_dynamic-update-slice_fusion), channel_id=2, replica_groups=mesh['dp'=32,'seq'=16] {'seq'}, use_global_device_ids=true, to_apply=%add | all-reduce | flops 768 | bytes 6144
  84.3 0.2 convert_reduce_fusion.1
  84.5 1.0 multiply_sine_fusion
  85.5 44.9 %reduce-scatter.3.cloned.1.call-done = bf16[48,1408]{1,0:T(8,128)(2,1)} async-done(((bf16[768,1408]{1,0:T(8,128)(2,1)}), bf16[48,1408]{1,0:T(8,128)(2,1)}) %reduce-scatter.3.cloned.1.call-update) | async-done | bytes 135184 | tf_op jit(solution)/shard_map/reduce_scatter | solution.py:107
  130.4 1.2 convolution_convert_fusion.12
  131.7 16.6 %all_gather.20 = bf16[768,512]{1,0:T(8,128)(2,1)S(1)} all-gather(bf16[48,512]{1,0:T(8,128)(2,1)S(1)} %convolution_convert_fusion.12), channel_id=1, replica_groups=mesh['dp'=32,'seq'=16] {'seq'}, dimensions={0}, use_global_device_ids=true | all-gather | bytes 835584 | tf_op jit(solution)/shard_map/all_gather | solution.py:115
  148.3 0.5 fusion.143
  148.8 0.2 multiply_reduce_fusion.2
  149.0 24.8 %all-gather.7.cloned.1.call-done = bf16[2048,512]{1,0:T(8,128)(2,1)} async-done(((bf16[128,512]{1,0:T(8,128)(2,1)}), bf16[2048,512]{1,0:T(8,128)(2,1)}) %all-gather.7.cloned.1.call-update) | async-done | bytes 2097168 | tf_op jit(solution)/shard_map/all_gather | solution.py:128
  173.8 3.7 fusion.78
  177.6 39.8 %all-gather.9.cloned.1.call-done = bf16[2048,512]{1,0:T(8,128)(2,1)} async-done(((bf16[128,512]{1,0:T(8,128)(2,1)}), bf16[2048,512]{1,0:T(8,128)(2,1)}) %all-gather.9.cloned.1.call-update) | async-done | bytes 2097168 | tf_op jit(solution)/shard_map/all_gather | solution.py:129
  217.3 4.7 fusion.142
  222.1 1.5 convolution_convert_fusion.5
  223.6 0.0 reduce-scatter.5.cloned.1.call-update
  223.6 0.0 all-gather.11.cloned.1.call-start
  223.7 0.7 iota_compare_fusion.3
  224.3 57.8 %reduce-scatter.5.cloned.1.call-done = bf16[48,512]{1,0:T(8,128)(2,1)} async-done(((bf16[768,512]{1,0:T(8,128)(2,1)}), bf16[48,512]{1,0:T(8,128)(2,1)}) %reduce-scatter.5.cloned.1.call-update) | async-done | bytes 49168 | tf_op jit(solution)/shard_map/reduce_scatter | solution.py:141
  282.1 2.0 fusion.10
  284.2 0.0 all-gather.11.cloned.1.call-update
  284.2 0.2 all-reduce.4.cloned.1.call-start
  284.4 41.5 %all-gather.11.cloned.1.call-done = bf16[768,1408]{1,0:T(8,128)(2,1)} async-done(((bf16[48,1408]{1,0:T(8,128)(2,1)}), bf16[768,1408]{1,0:T(8,128)(2,1)}) %all-gather.11.cloned.1.call-update) | async-done | bytes 2162704 | tf_op jit(solution)/shard_map/all_gather | solution.py:144
  325.9 2.4 convolution_convert_fusion.9
  328.4 4.2 fusion.9
  332.6 2.6 multiply_reduce_fusion
  335.2 1.4 multiply_convert_fusion
  336.6 3.3 fusion.8
  339.9 3.1 fusion.7
  343.0 2.0 pad_maximum_fusion
  345.0 2.9 convolution_convert_fusion.1
  347.9 0.0 all-reduce.4.cloned.1.call-update
  347.9 7.5 %fusion.29 = bf16[1,256,512]{2,1,0:T(8,128)(2,1)} fusion(f32[256,512]{1,0:T(8,128)S(1)} %get-tuple-element.29, bf16[2048,512]{1,0:T(8,128)(2,1)} %all-gather.9.cloned.1.call-done, f32[256,2048]{1,0:T(8,128)} %fusion.78), kind=kOutput, calls=%fused_computation.59 | convolution fusion | flops 571211776 | bytes 4980736 | tf_op jit(solution)/shard_map/dot_general | solution.py:135
  355.4 150.4 %all-reduce.4.cloned.1.call-done = (bf16[3,1408,88]{1,2,0:T(8,128)(2,1)}, bf16[88,1408]{1,0:T(8,128)(2,1)}) async-done(((bf16[3,1408,88]{1,2,0:T(8,128)(2,1)}, bf16[88,1408]{1,0:T(8,128)(2,1)}), (bf16[3,1408,88]{1,2,0:T(8,128)(2,1)}, bf16[88,1408]{1,0:T(8,128)(2,1)})) %all-reduce.4.cloned.1.call-update) | async-done | bytes 991248 | tf_op jit(solution)/shard_map/psum | solution.py:167
  505.8 2.0 copy.18
  507.9 1.7 copy.19
  (49 shorter events, 0.5 us)
Async XLA Ops:
  7.2 123.3 %copy-start = (bf16[1408,512]{1,0:T(8,128)(2,1)S(1)}, bf16[1408,512]{1,0:T(8,128)(2,1)}, u32[]{:S(2)}) copy-start(bf16[1408,512]{1,0:T(8,128)(2,1)} %param.18) | copy-start | bytes 4325380
  7.2 50.9 %all-gather.13.cloned.1.call-start = ((), (), s32[]{:S(2)}) async-start(), calls=%async_computation.7 | async-start | bytes 2297856 | tf_op jit(solution)/shard_map/all_gather | solution.py:72
  7.9 122.5 %reduce-scatter.3.cloned.1.call-start = ((), (), s32[]{:S(2)}) async-start(), calls=%async_computation.2 | async-start | bytes 2297856 | tf_op jit(solution)/shard_map/reduce_scatter | solution.py:107
  20.3 312.2 %copy-start.12 = (pred[768]{0:T(1024)(128)(4,1)}, pred[768]{0:T(1024)(128)(4,1)S(1)}, u32[]{:S(2)}) copy-start(pred[768]{0:T(1024)(128)(4,1)S(1)} %fusion.98) | copy-start | bytes 2308
  20.4 40.7 %copy-start.13 = (f32[1408]{0:T(1024)S(1)}, f32[1408]{0:T(1024)}, u32[]{:S(2)}) copy-start(f32[1408]{0:T(1024)} %param.15) | copy-start | bytes 16900
  58.1 2.3 copy-start.4
  61.1 1.1 copy-start.6
  62.2 1.7 copy-start.1
  65.3 1.4 copy-start.2
  65.8 266.8 %copy-start.11 = (f32[768]{0:T(1024)}, f32[768]{0:T(1024)S(1)}, u32[]{:S(2)}) copy-start(f32[768]{0:T(1024)S(1)} %fusion.26) | copy-start | bytes 9220
  65.8 1.2 copy-start.9
  67.0 2.2 copy-start.10
  67.0 3.5 copy-start.15
  67.0 5.5 %copy-start.16 = (s32[1,48]{1,0:T(1,128)S(1)}, s32[1,48]{1,0:T(1,128)}, u32[]{:S(2)}) copy-start(s32[1,48]{1,0:T(1,128)} %param.13) | copy-start | bytes 580
  69.2 61.3 %copy-start.7 = (bf16[1,48,1408]{2,1,0:T(8,128)(2,1)S(1)}, bf16[1,48,1408]{2,1,0:T(8,128)(2,1)}, u32[]{:S(2)}) copy-start(bf16[1,48,1408]{2,1,0:T(8,128)(2,1)} %param.12) | copy-start | bytes 405508
  69.2 104.6 %all-gather.7.cloned.1.call-start = ((), (), s32[]{:S(2)}) async-start(), calls=%async_computation.3 | async-start | bytes 2228224 | tf_op jit(solution)/shard_map/all_gather | solution.py:128
  69.9 147.4 %all-gather.9.cloned.1.call-start = ((), (), s32[]{:S(2)}) async-start(), calls=%async_computation.4 | async-start | bytes 2228224 | tf_op jit(solution)/shard_map/all_gather | solution.py:129
  70.5 211.6 %reduce-scatter.5.cloned.1.call-start = ((), (), s32[]{:S(2)}) async-start(), calls=%async_computation.5 | async-start | bytes 835584 | tf_op jit(solution)/shard_map/reduce_scatter | solution.py:141
  131.7 42.2 %copy-start.14 = (f32[512]{0:T(512)S(1)}, f32[512]{0:T(512)}, u32[]{:S(2)}) copy-start(f32[512]{0:T(512)} %param.20) | copy-start | bytes 6148
  149.0 68.3 %copy-start.8 = (bf16[1,256,512]{2,1,0:T(8,128)(2,1)S(1)}, bf16[1,256,512]{2,1,0:T(8,128)(2,1)}, u32[]{:S(2)}) copy-start(bf16[1,256,512]{2,1,0:T(8,128)(2,1)} %param.23) | copy-start | bytes 786436
  223.6 102.3 %all-gather.11.cloned.1.call-start = ((), (), s32[]{:S(2)}) async-start(), calls=%async_computation.6 | async-start | bytes 2297856 | tf_op jit(solution)/shard_map/all_gather | solution.py:144
  284.2 221.6 %all-reduce.4.cloned.1.call-start = ((), (), s32[]{:S(2)}) async-start(), calls=%async_computation.8 | async-start | bytes 1982464 | tf_op jit(solution)/shard_map/psum | solution.py:167
  332.6 2.7 copy-start.3
  339.9 3.1 copy-start.5
Sparse Core Ops, SparseCore 0:
  10.1 47.9 all-gather.12
  69.3 61.0 reduce-scatter.2
  132.8 41.0 all-gather.6
  176.0 41.2 all-gather.8
  223.7 58.3 reduce-scatter.4
  284.7 41.1 all-gather.10
  348.0 157.7 all-reduce.3
where the time goes:
time: 517 us; the launch traced here: 516 us
  waiting for transfers between devices  399 us (77%)
  matrix products  45.7 us (9%)
  blocking collectives  28.2 us (5%)
  other arithmetic  19.8 us (4%)
  between operations  15.1 us (3%)
  local copies, waits for them, and re-layouts  8.21 us (2%)
    psum x1, waiting for transfers between devices, local(): lax.psum(grad_q.astype(jnp.bfloat16), 'dp').astype(jnp.float32)  150 us
    reduce_scatter x1, waiting for transfers between devices, local(): lax.psum_scatter(back_terms.astype(jnp.bfloat16), 'seq', scatter_dimensio...  57.8 us
    reduce_scatter x1, waiting for transfers between devices, local(): lax.psum_scatter(part.astype(jnp.bfloat16), 'seq', scatter_dimension=0, t...  44.9 us
    all_gather x1, waiting for transfers between devices, local(): dy_all = lax.all_gather(dy_own, 'seq', axis=0, tiled=True)  41.5 us
    all_gather x1, waiting for transfers between devices, local(): lax.all_gather(fc_out, 'seq', axis=0, tiled=True)  39.8 us
    all_gather x1, waiting for transfers between devices, local(): gathered = lax.all_gather(x_rows, 'seq', axis=0, tiled=True)  37.7 us
    all_gather x1, waiting for transfers between devices, local(): lax.all_gather(fc_in, 'seq', axis=0, tiled=True)  24.8 us
    all_gather x1, blocking collectives, local(): lax.all_gather(vis, 'seq', axis=0, tiled=True)  16.6 us
  transfers between devices with their start and end apart: 7, of which 7 were waited for; matrix products, arithmetic and copies ran while one was open for 6% of the time, Pallas kernels for 0%

commit v1 on v0

v1 whole, which is shorter than its diff:
```python
import jax
import jax.numpy as jnp
from jax import lax
from jax.experimental import pallas as pl
from jax.experimental.pallas import tpu as pltpu
from jax.sharding import PartitionSpec as P

HD = 88
HP = 96
DD = 512
NZ = 8
NX = 4
NY = 8
CAP = 48
ROWS = 768
SLOTS = 3
HID = 128
FDEV = 256
DEAD = 1024.0
GRAD_ROWS = 3328
SCALE = HD ** (-0.5)
F32 = jnp.float32
BF16 = jnp.bfloat16


def dot(a, b):
    return jnp.dot(a, b, preferred_element_type=F32)


def dot_nt(a, b):
    return lax.dot_general(a, b, (((1,), (1,)), ((), ())), preferred_element_type=F32)


def layer_norm(values, gain):
    mean = jnp.mean(values, axis=-1, keepdims=True)
    centred = values - mean
    var = jnp.mean(centred * centred, axis=-1, keepdims=True)
    return centred * lax.rsqrt(var + 1e-06) * gain


def call(body, outs, scratch, cost, grant, *args):
    return pl.pallas_call(
        body,
        out_shape=[jax.ShapeDtypeStruct(shape, dtype) for shape, dtype in outs],
        in_specs=[pl.BlockSpec(memory_space=pltpu.VMEM)] * len(args),
        out_specs=[pl.BlockSpec(memory_space=pltpu.VMEM)] * len(outs),
        scratch_shapes=scratch,
        compiler_params=pltpu.CompilerParams(vmem_limit_bytes=grant << 20),
        cost_estimate=pl.CostEstimate(flops=cost, bytes_accessed=8 << 20, transcendentals=1 << 20),
    )(*args)


def prep_body(keep, patches, gain, xn, x_slot, offsets):
    at_row = lax.broadcasted_iota(jnp.int32, (CAP, CAP), 0)
    at_col = lax.broadcasted_iota(jnp.int32, (CAP, CAP), 1)
    own = jnp.broadcast_to(keep[...], (CAP, CAP))
    owner = lax.shift_right_arithmetic(own, 8)
    owner_col = jnp.sum(jnp.where(at_row == at_col, owner, 0), axis=1, keepdims=True)
    same = (owner_col == owner) & (at_row < at_col)
    rank = jnp.sum(same.astype(jnp.int32), axis=0, keepdims=True)
    slot = jnp.where(own >= 0, owner * SLOTS + rank, -1)
    pick = at_row == slot
    live = jnp.sum(pick.astype(F32), axis=1, keepdims=True) > 0.5
    spot = jnp.sum(jnp.where(pick, own - owner * FDEV, 0).astype(F32), axis=1, keepdims=True)
    rows = dot(pick.astype(F32).astype(BF16), patches[...])
    x_slot[...] = rows.astype(BF16)
    lane = lax.broadcasted_iota(jnp.int32, rows.shape, 1)
    dead_row = jnp.where(lane == 0, DEAD, 0.0)
    xn[...] = jnp.where(live, layer_norm(rows, gain[...]), dead_row).astype(BF16)
    offsets[...] = jnp.broadcast_to(jnp.where(live, spot, -1.0), (CAP, 128)).astype(BF16)


def prep(keep, patches, gain):
    return call(
        prep_body, [((CAP, patches.shape[1]), BF16), ((CAP, patches.shape[1]), BF16), ((CAP, 128), BF16)],
        [], 1 << 20, 8, keep, patches, gain)


def join_body(*refs):
    blocks, out, sems = refs[:NZ], refs[NZ], refs[NZ + 1]
    copies = [pltpu.make_async_copy(blocks[k], out.at[pl.ds(CAP * k, CAP)], sems.at[k]) for k in range(NZ)]
    for copy in copies:
        copy.start()
    for copy in copies:
        copy.wait()


def join(blocks):
    rows, width = blocks[0].shape
    return pl.pallas_call(
        join_body,
        out_shape=jax.ShapeDtypeStruct((NZ * rows, width), blocks[0].dtype),
        in_specs=[pl.BlockSpec(memory_space=pl.ANY)] * NZ,
        out_specs=pl.BlockSpec(memory_space=pl.ANY),
        scratch_shapes=[pltpu.SemaphoreType.DMA((NZ,))],
        compiler_params=pltpu.CompilerParams(vmem_limit_bytes=4 << 20),
        cost_estimate=pl.CostEstimate(flops=0, bytes_accessed=4 << 20, transcendentals=0),
    )(*blocks)


def attend_body(mine, other, w_t, swap, extra, sent, q_out, k_out, kt_out, v_out, stats, live_out, ctx_out):
    def heads(x):
        qkv = dot_nt(w_t[...], x[...])
        pad = jnp.zeros((HP - HD, qkv.shape[1]), F32)
        return [jnp.concatenate([qkv[i * HD:(i + 1) * HD], pad], axis=0) for i in range(3)]

    q, k, v = [jnp.concatenate(pair, axis=1) for pair in zip(heads(mine), heads(other))]
    q = (q * SCALE).astype(BF16)
    vt = v.astype(BF16)
    k_rows = k.T.astype(BF16)
    live = jnp.concatenate([mine[:, 0:128], other[:, 0:128]], axis=0).astype(F32)[:, 0:1] < 0.5 * DEAD
    q_out[...] = q
    k_out[...] = k_rows
    kt_out[...] = k.astype(BF16)
    v_out[...] = v.T.astype(BF16)
    live_out[...] = jnp.where(live, 0.0, -jnp.inf).astype(F32)
    ctx = []
    for i in range(3):
        cols = slice(256 * i, 256 * (i + 1))
        scores = jnp.where(live, dot(k_rows, q[:, cols]), -jnp.inf)
        top = jnp.max(scores, axis=0, keepdims=True)
        expo = jnp.exp(scores - top)
        total = jnp.sum(expo, axis=0, keepdims=True)
        stats[0:1, cols] = top
        stats[1:2, cols] = total
        ctx.append(dot(vt, (expo / total).astype(BF16)))
    ctx = jnp.concatenate(ctx, axis=1)
    ctx = jnp.concatenate([ctx, jnp.zeros((128 - HP, ROWS), F32)], axis=0).astype(BF16)
    sent[:, 0:CAP, :] = dot_nt(swap[...], ctx).astype(BF16).reshape(16, CAP, 128)
    sent[:, CAP:, :] = extra[...]
    ctx_out[...] = dot_nt(ctx, swap[...])[0:HP].astype(BF16)


def attend(mine, other, w_t, swap, extra):
    return call(
        attend_body,
        [((16, 64, 128), BF16), ((HP, ROWS), BF16), ((ROWS, HP), BF16), ((HP, ROWS), BF16), ((ROWS, HP), BF16),
         ((8, ROWS), F32), ((ROWS, 1), F32), ((HP, ROWS), BF16)],
        [], 1700 << 20, 20, mine, other, w_t, swap, extra)


def decode_body(came, weights, mask, gain, cot, table, recon, dvis, mixed, grad):
    flat = came[...].reshape(16 * 64, 128)
    vis = jnp.zeros((CAP, DD), F32)
    for g in range(16):
        vis += dot(came[g, 0:CAP, 0:HP], weights[g, 2 * HID:2 * HID + HP, :])
    row = lax.broadcasted_iota(jnp.int32, (CAP, 1024), 0)
    col = lax.broadcasted_iota(jnp.int32, (CAP, 1024), 1)
    source = jnp.zeros((CAP, 1024), jnp.int32)
    for g in range(1, 16):
        source += (row >= SLOTS * g).astype(jnp.int32)
    slot = row - SLOTS * source
    base = 64 * source + CAP
    x_part = jnp.concatenate(
        [dot((col == base + 4 * slot + i).astype(F32).astype(BF16), flat) for i in range(4)], axis=1)
    vis = (vis + x_part).astype(BF16)
    spots = dot((col == base + 12).astype(F32).astype(BF16), flat)
    lane = lax.broadcasted_iota(jnp.int32, (CAP, 128), 1)
    spot = jnp.sum(jnp.where(lane == slot[:, 0:128], spots, 0.0), axis=1, keepdims=True)
    spot = jnp.concatenate([spot, jnp.full((128 - CAP, 1), -1.0, F32)], axis=0)
    vis = jnp.concatenate([vis.astype(F32), jnp.zeros((128 - CAP, DD), F32)], axis=0).astype(BF16)
    where_col = lax.broadcasted_iota(jnp.int32, (128, FDEV), 1).astype(F32)
    picker = (spot == where_col).astype(F32)
    placer = picker.T
    seen = jnp.sum(placer, axis=1, keepdims=True)
    dec_vis = dot(placer.astype(BF16), vis)
    dec_x = jnp.where(seen > 0.5, dec_vis, mask[...].astype(F32)) + table[...]
    mean = jnp.mean(dec_x, axis=-1, keepdims=True)
    centred = dec_x - mean
    var = jnp.mean(centred * centred, axis=-1, keepdims=True)
    inv_std = lax.rsqrt(var + 1e-06)
    normed = centred * inv_std
    dn = (normed * gain[...]).astype(BF16)
    cot_b = cot[...]
    mixed[...] = dec_x
    for i in range(8):
        fin = jnp.concatenate([weights[2 * i, 0:HID, :], weights[2 * i + 1, 0:HID, :]], axis=0)
        fout = jnp.concatenate([weights[2 * i, HID:2 * HID, :], weights[2 * i + 1, HID:2 * HID, :]], axis=0)
        hidden = dot_nt(dn, fin)
        dact = dot_nt(cot_b, fout)
        cdf = 0.5 * (1.0 + lax.erf(hidden * 0.7071067811865476))
        pdf = jnp.exp(-0.5 * hidden * hidden) * 0.3989422804014327
        act = (hidden * cdf).astype(BF16)
        dhidden = (dact * (cdf + hidden * pdf)).astype(BF16)
        mixed[...] += dot(act, fout)
        if i == 0:
            grad[...] = dot(dhidden, fin)
        else:
            grad[...] += dot(dhidden, fin)
    recon[...] = mixed[...].astype(BF16)
    scaled = grad[...] * gain[...]
    first = jnp.mean(scaled, axis=-1, keepdims=True)
    second = jnp.mean(scaled * normed, axis=-1, keepdims=True)
    ddec = (cot_b.astype(F32) + inv_std * (scaled - first - normed * second)).astype(BF16)
    dvis[...] = dot(picker[0:CAP].astype(BF16), ddec).astype(BF16)


def decode(came, weights, mask, gain, cot, table):
    return call(
        decode_body, [((FDEV, DD), BF16), ((CAP, DD), BF16)],
        [pltpu.VMEM((FDEV, DD), F32), pltpu.VMEM((FDEV, DD), F32)], 2300 << 20, 20,
        came, weights, mask, gain, cot, table)


def back_body(dvis, w_oe, swap, q, k, kt, v, stats, dead, ctx, mine, other, parts, ds_all, pb_all):
    dctx = dot(dot_nt(w_oe[...], dvis[...]).astype(BF16), swap[...]).astype(BF16)
    grad_oe = dot(ctx[...], dvis[...])[0:HD]
    dq = []
    for i in range(3):
        cols = slice(256 * i, 256 * (i + 1))
        scores = dot(k[...], q[:, cols]) + dead[...]
        probs = jnp.exp(scores - stats[0:1, cols]) / stats[1:2, cols]
        dprob = dot(v[...], dctx[:, cols])
        inner = jnp.sum(probs * dprob, axis=0, keepdims=True)
        ds = (probs * (dprob - inner)).astype(BF16)
        ds_all[:, cols] = ds
        pb_all[:, cols] = probs.astype(BF16)
        dq.append(dot(kt[...], ds) * SCALE)
    dq = jnp.concatenate(dq, axis=1)[0:HD]
    dk = dot_nt(q[...], ds_all[...])[0:HD]
    dv = dot_nt(dctx, pb_all[...])[0:HD]
    dqkv = jnp.concatenate([dq, dk, dv], axis=0).astype(BF16)
    grad = dot(dqkv[:, 0:ROWS // 2], mine[...]) + dot(dqkv[:, ROWS // 2:], other[...])
    wide = grad.shape[1] // 128
    pieces = [grad[:, 128 * j:128 * (j + 1)] for j in range(wide)]
    pieces += [grad_oe[:, 128 * j:128 * (j + 1)] for j in range(DD // 128)]
    done = sum(p.shape[0] for p in pieces)
    pieces.append(jnp.zeros((GRAD_ROWS - done, 128), F32))
    parts[...] = jnp.concatenate(pieces, axis=0).astype(BF16)


def back(*args):
    return call(
        back_body, [((GRAD_ROWS, 128), BF16)],
        [pltpu.VMEM((ROWS, ROWS), BF16), pltpu.VMEM((ROWS, ROWS), BF16)], 2500 << 20, 20, *args)[0]


def position_table(positions, width):
    half = width // 2
    freq = 10000.0 ** (-(jnp.arange(half, dtype=F32) * 2.0 / width))
    angle = positions[:, None] * freq[None, :]
    return jnp.concatenate([jnp.sin(angle), jnp.cos(angle)], axis=1)


Z_GROUPS = [[2 * z + c for z in range(NZ)] for c in range(2)]
X_GROUPS = [[NX * y + x for x in range(NX)] for y in range(NY)]
Y_GROUPS = [[NX * y + x for y in range(NY)] for x in range(NX)]


def exchange(block, axis, groups):
    return lax.all_to_all(block, axis, 0, 0, axis_index_groups=groups, tiled=True)


def spread(block, axis, groups):
    count = len(groups[0])
    copies = jnp.broadcast_to(block[None], (count,) + block.shape)
    return exchange(copies, axis, groups)


def z_shift(block, step):
    return lax.ppermute(block, "seq", [(s, (s + 2 * step) % 16) for s in range(16)])


def ring(block):
    got = {0: block, 8: block}
    for step in range(1, 5):
        got[step] = z_shift(got[step - 1], 1)
        if step < 4:
            got[8 - step] = z_shift(got[9 - step], -1)
    return [got[k] for k in range(NZ)]


def swap_core(block):
    return lax.ppermute(block, "seq", [(s, s ^ 1) for s in range(16)])


def local(
    patches,
    keep_pos,
    kept_counts,
    enc_gain,
    w_qkv,
    w_out,
    w_e2d,
    mask_token,
    dec_gain,
    fc_in,
    fc_out,
    cotangent,
):
    me = lax.axis_index("seq")
    my_c = me % 2
    fdev = cotangent.shape[1]
    my_z = me // 2
    cot = cotangent[0]
    cap = keep_pos.shape[1]
    rows = 16 * cap

    xn_own, x_slot, offsets = prep(keep_pos, patches[0], enc_gain[None])
    mine = join(ring(xn_own))
    other = swap_core(mine)

    x_vis = dot(x_slot, w_e2d).astype(BF16)
    places = jnp.pad(offsets[:, 0].reshape(16, 1, SLOTS), ((0, 0), (0, 0), (0, 128 - SLOTS)))
    extra = jnp.concatenate(
        [x_vis.reshape(16, 12, 128), places, jnp.zeros((16, 3, 128), BF16)], axis=1)

    w_oe_own = jnp.pad(dot(w_out, w_e2d).astype(BF16), ((0, HP - HD), (0, 0)))
    weights = lax.all_gather(jnp.concatenate([fc_in, fc_out, w_oe_own], axis=0), "seq", axis=0)

    tok = jnp.arange(rows, dtype=jnp.int32)
    block = tok // cap
    source = (my_z - block % NZ) % NZ * 2 + (my_c ^ (block // NZ))
    inside = tok % cap
    dest = inside // SLOTS * cap + source * SLOTS + inside % SLOTS
    swap = (dest[None, :] == tok[:, None]).astype(BF16)
    table = position_table((me * fdev + jnp.arange(fdev, dtype=jnp.int32)).astype(F32), DD)

    w_t = w_qkv.transpose(0, 2, 1).reshape(3 * HD, -1)
    sent, q, k, k_t, v, stats, dead, ctx = attend(mine, other, w_t, swap, extra)
    came = lax.all_to_all(sent, "seq", 0, 0, tiled=True)
    recon, dvis_own = decode(came, weights, mask_token[None], dec_gain[None], cot, table)
    dvis = lax.all_gather(dvis_own, "seq", axis=0, tiled=True)
    parts = back(dvis, w_oe_own, swap, q, k, k_t, v, stats, dead, ctx, mine, other)

    parts = jnp.sum(exchange(parts.reshape(NX, 832, 128), "dp", X_GROUPS).astype(F32), axis=0).astype(BF16)
    parts = jnp.sum(exchange(parts.reshape(NY, 104, 128), "dp", Y_GROUPS).astype(F32), axis=0).astype(BF16)
    parts = spread(parts, "dp", Y_GROUPS).reshape(832, 128)
    total = spread(parts, "dp", X_GROUPS).reshape(GRAD_ROWS, 128)
    wide = w_qkv.shape[1] // 128
    cut = 3 * HD * wide
    grad_q = total[:cut].reshape(wide, 3 * HD, 128).transpose(1, 0, 2).reshape(3, HD, wide * 128).transpose(0, 2, 1)
    grad_oe = total[cut:cut + 4 * HD].reshape(4, HD, 128).transpose(1, 0, 2).reshape(HD, DD)
    grad_o = dot_nt(grad_oe, w_e2d).astype(BF16)
    return (recon[None], grad_q, grad_o)


def solution(mesh):
    placed = (
        P("dp", "seq", None),
        P("dp", "seq"),
        P("dp", None),
        P(),
        P(None, None, "seq"),
        P("seq", None),
        P(),
        P(),
        P(),
        P("seq", None),
        P("seq", None),
        P("dp", "seq", None),
    )
    return jax.shard_map(
        local,
        mesh=mesh,
        in_specs=placed,
        out_specs=(P("dp", "seq", None), P(None, None, "seq"), P("seq", None)),
        check_vma=False,
    )
```

time: 517 us -> 190 us (0.37)
  the two profiles are of different devices: /device:TPU:8 before, /device:TPU:64 now
where the time goes in v1:
time: 190 us; the launch traced here: 189 us
  blocking collectives  78.8 us (41%)
  starting transfers between devices  34.8 us (18%)
  waiting for transfers between devices  26.2 us (14%)
  Pallas kernels  18 us (9%)
  between operations  14.4 us (8%)
  local copies, waits for them, and re-layouts  11.6 us (6%)
  matrix products  2.95 us (2%)
  other arithmetic  2.61 us (1%)
    all_to_all x4, blocking collectives, exchange(): lax.all_to_all(block, axis, 0, 0, axis_index_groups=groups, tiled=True)  60.2 us
    ppermute x7, starting transfers between devices, z_shift(): lax.ppermute(block, 'seq', [(s, (s + 2 * step) % 16) for s in range(16)])  25.6 us
    all_gather x1, blocking collectives, local(): dvis = lax.all_gather(dvis_own, 'seq', axis=0, tiled=True)  18.6 us
    pallas_call x4, Pallas kernels, call(): pl.pallas_call(body, out_shape=[jax.ShapeDtypeStruct(shape, dtype) for sh...  17 us
    ppermute x7, waiting for transfers between devices, z_shift(): lax.ppermute(block, 'seq', [(s, (s + 2 * step) % 16) for s in range(16)])  16 us
    unnamed x46, local copies, waits for them, and re-layouts  9.45 us
    all_to_all x1, waiting for transfers between devices, local(): came = lax.all_to_all(sent, 'seq', 0, 0, tiled=True)  8.54 us
    all_to_all x1, starting transfers between devices, local(): came = lax.all_to_all(sent, 'seq', 0, 0, tiled=True)  7.24 us
  transfers between devices with their start and end apart: 10, of which 8 were waited for; matrix products, arithmetic and copies ran while one was open for 1% of the time, Pallas kernels for 4%

profile of v1, /device:TPU:64, one launch (start us, length us, event | category | flops | bytes accessed | tf_op | source)
XLA Modules:
  0.0 189.5 jit_solution(16465234696664236238)
XLA Ops:
  7.2 0.0 copy-start
  7.2 0.0 copy-start.19
  7.2 0.0 copy-start.20
  7.2 0.0 copy-start.21
  7.2 0.0 copy-start.6
  7.2 0.0 copy-start.4
  7.2 0.0 all-gather.3.cloned.1.call-start
  7.3 1.3 copy-done
  8.5 1.3 convolution_convert_fusion.1
  9.9 0.8 pad_maximum_fusion.1
  10.7 0.0 all-gather.3.cloned.1.call-update
  10.7 0.0 copy-done.6
  10.8 0.0 copy-done.4
  10.8 0.5 shard_map.130
  11.2 4.3 %collective-permute-start = (bf16[48,1408]{1,0:T(8,128)(2,1)S(1)}, bf16[48,1408]{1,0:T(8,128)(2,1)S(1)}, u32[]{:S(2)}, u32[]{:S(2)}) collective-permute-start(bf16[48,1408]{1,0:T(8,128)(2,1)S(1)} %get-tuple-element.16.refs_0_), channel_id=1, source_target_pairs={{0,2},{1,3},{2,4},{3,5},{4,6},{5,7},{6,8},{7,9},{8,10},{9,11},{10,... | collective-permute-start | bytes 405512 | tf_op jit(solution)/shard_map/ppermute | solution.py:261
  15.5 4.6 %collective-permute-start.4 = (bf16[48,1408]{1,0:T(8,128)(2,1)S(1)}, bf16[48,1408]{1,0:T(8,128)(2,1)S(1)}, u32[]{:S(2)}, u32[]{:S(2)}) collective-permute-start(bf16[48,1408]{1,0:T(8,128)(2,1)S(1)} %get-tuple-element.16.refs_0_), channel_id=1, source_target_pairs={{0,14},{1,15},{2,0},{3,1},{4,2},{5,3},{6,4},{7,5},{8,6},{9,7},{10,... | collective-permute-start | bytes 405512 | tf_op jit(solution)/shard_map/ppermute | solution.py:261
  20.1 1.0 collective-permute-done.refs_1_
  21.2 1.9 %collective-permute-start.1 = (bf16[48,1408]{1,0:T(8,128)(2,1)S(1)}, bf16[48,1408]{1,0:T(8,128)(2,1)S(1)}, u32[]{:S(2)}, u32[]{:S(2)}) collective-permute-start(bf16[48,1408]{1,0:T(8,128)(2,1)S(1)} %collective-permute-done.refs_1_), channel_id=1, source_target_pairs={{0,2},{1,3},{2,4},{3,5},{4,6},{5,7},{6,8},{7,9},{8,10},{9,11},{10,... | collective-permute-start | bytes 405512 | tf_op jit(solution)/shard_map/ppermute | solution.py:261
  23.1 0.0 collective-permute-done.4.refs_7_
  23.1 6.1 %collective-permute-start.5 = (bf16[48,1408]{1,0:T(8,128)(2,1)S(1)}, bf16[48,1408]{1,0:T(8,128)(2,1)S(1)}, u32[]{:S(2)}, u32[]{:S(2)}) collective-permute-start(bf16[48,1408]{1,0:T(8,128)(2,1)S(1)} %collective-permute-done.4.refs_7_), channel_id=1, source_target_pairs={{0,14},{1,15},{2,0},{3,1},{4,2},{5,3},{6,4},{7,5},{8,6},{9,7},{10,... | collective-permute-start | bytes 405512 | tf_op jit(solution)/shard_map/ppermute | solution.py:261
  29.3 2.5 %collective-permute-done.1.refs_2_ = bf16[48,1408]{1,0:T(8,128)(2,1)S(1)} collective-permute-done((bf16[48,1408]{1,0:T(8,128)(2,1)S(1)}, bf16[48,1408]{1,0:T(8,128)(2,1)S(1)}, u32[]{:S(2)}, u32[]{:S(2)}) %collective-permute-start.1) | collective-permute-done | bytes 135200 | tf_op jit(solution)/shard_map/ppermute | solution.py:261
  31.7 1.9 %collective-permute-start.2 = (bf16[48,1408]{1,0:T(8,128)(2,1)S(1)}, bf16[48,1408]{1,0:T(8,128)(2,1)S(1)}, u32[]{:S(2)}, u32[]{:S(2)}) collective-permute-start(bf16[48,1408]{1,0:T(8,128)(2,1)S(1)} %collective-permute-done.1.refs_2_), channel_id=1, source_target_pairs={{0,2},{1,3},{2,4},{3,5},{4,6},{5,7},{6,8},{7,9},{8,10},{9,11},{10,... | collective-permute-start | bytes 405512 | tf_op jit(solution)/shard_map/ppermute | solution.py:261
  33.6 1.7 collective-permute-done.5.refs_6_
  35.3 4.4 %collective-permute-start.6 = (bf16[48,1408]{1,0:T(8,128)(2,1)S(1)}, bf16[48,1408]{1,0:T(8,128)(2,1)S(1)}, u32[]{:S(2)}, u32[]{:S(2)}) collective-permute-start(bf16[48,1408]{1,0:T(8,128)(2,1)S(1)} %collective-permute-done.5.refs_6_), channel_id=1, source_target_pairs={{0,14},{1,15},{2,0},{3,1},{4,2},{5,3},{6,4},{7,5},{8,6},{9,7},{10,... | collective-permute-start | bytes 405512 | tf_op jit(solution)/shard_map/ppermute | solution.py:261
  39.7 1.5 collective-permute-done.2.refs_3_
  41.2 2.4 %collective-permute-start.3 = (bf16[48,1408]{1,0:T(8,128)(2,1)S(1)}, bf16[48,1408]{1,0:T(8,128)(2,1)S(1)}, u32[]{:S(2)}, u32[]{:S(2)}) collective-permute-start(bf16[48,1408]{1,0:T(8,128)(2,1)S(1)} %collective-permute-done.2.refs_3_), channel_id=1, source_target_pairs={{0,2},{1,3},{2,4},{3,5},{4,6},{5,7},{6,8},{7,9},{8,10},{9,11},{10,... | collective-permute-start | bytes 405512 | tf_op jit(solution)/shard_map/ppermute | solution.py:261
  43.6 2.1 %collective-permute-done.6.refs_5_ = bf16[48,1408]{1,0:T(8,128)(2,1)S(1)} collective-permute-done((bf16[48,1408]{1,0:T(8,128)(2,1)S(1)}, bf16[48,1408]{1,0:T(8,128)(2,1)S(1)}, u32[]{:S(2)}, u32[]{:S(2)}) %collective-permute-start.6) | collective-permute-done | bytes 135200 | tf_op jit(solution)/shard_map/ppermute | solution.py:261
  45.7 7.1 %collective-permute-done.3.refs_4_ = bf16[48,1408]{1,0:T(8,128)(2,1)S(1)} collective-permute-done((bf16[48,1408]{1,0:T(8,128)(2,1)S(1)}, bf16[48,1408]{1,0:T(8,128)(2,1)S(1)}, u32[]{:S(2)}, u32[]{:S(2)}) %collective-permute-start.3) | collective-permute-done | bytes 135200 | tf_op jit(solution)/shard_map/ppermute | solution.py:261
  52.9 1.1 shard_map.131.mine
  54.0 1.9 %collective-permute-start.7 = (bf16[384,1408]{1,0:T(8,128)(2,1)}, bf16[384,1408]{1,0:T(8,128)(2,1)}, u32[]{:S(2)}, u32[]{:S(2)}) collective-permute-start(bf16[384,1408]{1,0:T(8,128)(2,1)} %shard_map.131.mine), channel_id=1, source_target_pairs={{0,1},{1,0},{2,3},{3,2},{4,5},{5,4},{6,7},{7,6},{8,9},{9,8},{10,11... | collective-permute-start | bytes 3244040 | tf_op jit(solution)/shard_map/ppermute | solution.py:274
  55.9 0.1 slice_reduce_fusion
  56.0 0.1 reshape_squeeze.4
  56.1 0.4 convolution_convert_fusion.2
  56.5 0.1 reshape.121
  56.6 0.1 pad.17.clone
  56.7 0.1 fusion.6.extra
  56.8 0.4 fusion.swap
  57.2 1.7 collective-permute-done.7.other
  58.9 1.1 copy-done.2
  60.0 6.0 %shard_map.132 = (bf16[16,64,128]{2,1,0:T(8,128)(2,1)}, bf16[96,768]{1,0:T(8,128)(2,1)S(1)}, bf16[768,96]{1,0:T(8,128)(2,1)S(1)}, bf16[96,768]{1,0:T(8,128)(2,1)...) custom-call(bf16[384,1408]{1,0:T(8,128)(2,1)} %shard_map.131.mine, ...), custom_call_target="tpu_custom_call" | custom-call | flops 1782579200 | bytes 8388608 | tf_op jit(solution)/shard_map/pallas_call | solution.py:42
  66.0 0.7 copy-done.7
  66.7 0.7 copy-done.9
  67.4 0.7 copy-done.11
  68.1 0.7 copy-done.13
  68.8 0.7 copy-done.15
  69.4 7.2 %all-to-all-start = ((bf16[16,64,128]{2,1,0:T(8,128)(2,1)}), bf16[16,64,128]{2,1,0:T(8,128)(2,1)S(1)}, u32[]{:S(2)}, u32[]{:S(2)}) async-start(bf16[16,64,128]{2,1,0:T(8,128)(2,1)} %get-tuple-element.19), calls=%async_computation | async-start | bytes 524288 | tf_op jit(solution)/shard_map/all_to_all | solution.py:321
  76.7 1.0 multiply_sine_fusion
  77.7 0.0 copy-done.17
  77.7 0.1 pad_maximum_fusion.table
  77.8 8.5 %all-to-all-done.came = bf16[16,64,128]{2,1,0:T(8,128)(2,1)S(1)} async-done(((bf16[16,64,128]{2,1,0:T(8,128)(2,1)}), bf16[16,64,128]{2,1,0:T(8,128)(2,1)S(1)}, u32[]{:S(2)}, u32[]{:S(2)}) %all-to-all-start) | async-done | bytes 262176 | tf_op jit(solution)/shard_map/all_to_all | solution.py:321
  86.3 2.6 %copy-done.1 = bf16[5632,512]{1,0:T(8,128)(2,1)S(1)} copy-done((bf16[5632,512]{1,0:T(8,128)(2,1)S(1)}, bf16[5632,512]{1,0:T(8,128)(2,1)}, u32[]{:S(2)}) %copy-start.1) | copy-done | bytes 5767192
  89.0 0.9 copy-done.3
  89.9 5.2 %shard_map.133 = (bf16[256,512]{1,0:T(8,128)(2,1)}, bf16[48,512]{1,0:T(8,128)(2,1)S(1)}) custom-call(bf16[16,64,128]{2,1,0:T(8,128)(2,1)S(1)} %all-to-all-done.came, bf16[16,352,512]{2,1,0:T(8,128)(2,1)S(1)} %bitcast.28, bf16[1,512]{1,0:T(2,128)(2,1)S(1)} %broadcast_in_dim.34.mask, f32[1,512]{1,0:T(1,128)S(1)} %bitcast.32, bf16[256,512]{1,0:T(8,128)(2,1)S(1)} %bitcast.30, ...), custom_call_target="tpu_custom_call" | custom-call | flops 2411724800 | bytes 8388608 | tf_op jit(solution)/shard_map/pallas_call | solution.py:42
  95.1 18.6 %all_gather.11.dvis = bf16[768,512]{1,0:T(8,128)(2,1)S(1)} all-gather(bf16[48,512]{1,0:T(8,128)(2,1)S(1)} %get-tuple-element.21), channel_id=1, replica_groups=mesh['dp'=32,'seq'=16] {'seq'}, dimensions={0}, use_global_device_ids=true | all-gather | bytes 835584 | tf_op jit(solution)/shard_map/all_gather | solution.py:323
  113.7 5.3 %shard_map.134 = bf16[3328,128]{1,0:T(8,128)(2,1)S(1)} custom-call(bf16[768,512]{1,0:T(8,128)(2,1)S(1)} %all_gather.11.dvis, bf16[96,512]{1,0:T(8,128)(2,1)S(1)} %pad.9.w_oe, bf16[768,768]{1,0:T(8,128)(2,1)S(1)} %fusion.swap, bf16[96,768]{1,0:T(8,128)(2,1)S(1)} %copy-done.14, bf16[768,96]{1,0:T(8,128)(2,1)S(1)} %copy-done.10, ...), custom_call_target="tpu_custom_call" | custom-call | flops 2621440000 | bytes 8388608 | tf_op jit(solution)/shard_map/pallas_call | solution.py:42
  119.1 18.0 %all_to_all.25 = bf16[4,832,128]{2,1,0:T(8,128)(2,1)S(1)} all-to-all(bf16[4,832,128]{2,1,0:T(8,128)(2,1)S(1)} %bitcast.27), channel_id=1, replica_groups={{0,16,32,48},{64,80,96,112},{128,144,160,176},{192,208,224,240},{256,27..., dimensions={0} | all-to-all | bytes 1703936 | tf_op jit(solution)/shard_map/all_to_all | solution.py:251
  137.1 0.2 reduce_sum.24
  137.3 17.6 %all_to_all.26 = bf16[8,104,128]{2,1,0:T(8,128)(2,1)S(1)} all-to-all(bf16[8,104,128]{2,1,0:T(8,128)(2,1)S(1)} %bitcast.36), channel_id=1, replica_groups={{0,64,128,192,256,320,384,448},{16,80,144,208,272,336,400,464},{32,96,1..., dimensions={0} | all-to-all | bytes 425984 | tf_op jit(solution)/shard_map/all_to_all | solution.py:251
  155.0 12.4 %all_to_all.27 = bf16[8,104,128]{2,1,0:T(8,128)(2,1)S(1)} all-to-all(bf16[8,104,128]{2,1,0:T(8,128)(2,1)S(1)} %broadcast_in_dim.37), channel_id=1, replica_groups={{0,64,128,192,256,320,384,448},{16,80,144,208,272,336,400,464},{32,96,1..., dimensions={0} | all-to-all | bytes 425984 | tf_op jit(solution)/shard_map/all_to_all | solution.py:251
  167.4 0.1 broadcast_in_dim.39
  167.5 12.2 %all_to_all.28 = bf16[4,832,128]{2,1,0:T(8,128)(2,1)S(1)} all-to-all(bf16[4,832,128]{2,1,0:T(8,128)(2,1)S(1)} %broadcast_in_dim.39), channel_id=1, replica_groups={{0,16,32,48},{64,80,96,112},{128,144,160,176},{192,208,224,240},{256,27..., dimensions={0} | all-to-all | bytes 1703936 | tf_op jit(solution)/shard_map/all_to_all | solution.py:251
  179.8 1.3 convolution_convert_fusion
  181.1 0.2 copy.19
  181.3 1.3 reshape.126
  (41 shorter events, 0.3 us)
Async XLA Ops:
  7.2 1.4 copy-start
  7.2 2.7 %copy-start.19 = (bf16[128,512]{1,0:T(8,128)(2,1)S(1)}, bf16[128,512]{1,0:T(8,128)(2,1)}, u32[]{:S(2)}) copy-start(bf16[128,512]{1,0:T(8,128)(2,1)} %param.21) | copy-start | bytes 393220
  7.2 2.7 %copy-start.20 = (bf16[128,512]{1,0:T(8,128)(2,1)S(1)}, bf16[128,512]{1,0:T(8,128)(2,1)}, u32[]{:S(2)}) copy-start(bf16[128,512]{1,0:T(8,128)(2,1)} %param.20) | copy-start | bytes 393220
  7.2 3.5 %copy-start.21 = (f32[1408]{0:T(1024)S(1)}, f32[1408]{0:T(1024)}, u32[]{:S(2)}) copy-start(f32[1408]{0:T(1024)} %param.14) | copy-start | bytes 16900
  7.2 3.5 %copy-start.6 = (s32[1,48]{1,0:T(1,128)S(1)}, s32[1,48]{1,0:T(1,128)}, u32[]{:S(2)}) copy-start(s32[1,48]{1,0:T(1,128)} %keep.1) | copy-start | bytes 580
  7.2 3.5 %copy-start.4 = (bf16[1,48,1408]{2,1,0:T(8,128)(2,1)S(1)}, bf16[1,48,1408]{2,1,0:T(8,128)(2,1)}, u32[]{:S(2)}) copy-start(bf16[1,48,1408]{2,1,0:T(8,128)(2,1)} %param.12) | copy-start | bytes 405508
  7.2 79.1 %all-gather.3.cloned.1.call-start = ((), (), s32[]{:S(2)}) async-start(), calls=%async_computation.5 | async-start | bytes 6127616 | tf_op jit(solution)/shard_map/all_gather | solution.py:309
  11.2 9.9 %collective-permute-start = (bf16[48,1408]{1,0:T(8,128)(2,1)S(1)}, bf16[48,1408]{1,0:T(8,128)(2,1)S(1)}, u32[]{:S(2)}, u32[]{:S(2)}) collective-permute-start(bf16[48,1408]{1,0:T(8,128)(2,1)S(1)} %get-tuple-element.16.refs_0_), channel_id=1, source_target_pairs={{0,2},{1,3},{2,4},{3,5},{4,6},{5,7},{6,8},{7,9},{8,10},{9,11},{10,... | collective-permute-start | bytes 405512 | tf_op jit(solution)/shard_map/ppermute | solution.py:261
  15.5 7.6 %collective-permute-start.4 = (bf16[48,1408]{1,0:T(8,128)(2,1)S(1)}, bf16[48,1408]{1,0:T(8,128)(2,1)S(1)}, u32[]{:S(2)}, u32[]{:S(2)}) collective-permute-start(bf16[48,1408]{1,0:T(8,128)(2,1)S(1)} %get-tuple-element.16.refs_0_), channel_id=1, source_target_pairs={{0,14},{1,15},{2,0},{3,1},{4,2},{5,3},{6,4},{7,5},{8,6},{9,7},{10,... | collective-permute-start | bytes 405512 | tf_op jit(solution)/shard_map/ppermute | solution.py:261
  21.2 10.6 %collective-permute-start.1 = (bf16[48,1408]{1,0:T(8,128)(2,1)S(1)}, bf16[48,1408]{1,0:T(8,128)(2,1)S(1)}, u32[]{:S(2)}, u32[]{:S(2)}) collective-permute-start(bf16[48,1408]{1,0:T(8,128)(2,1)S(1)} %collective-permute-done.refs_1_), channel_id=1, source_target_pairs={{0,2},{1,3},{2,4},{3,5},{4,6},{5,7},{6,8},{7,9},{8,10},{9,11},{10,... | collective-permute-start | bytes 405512 | tf_op jit(solution)/shard_map/ppermute | solution.py:261
  23.1 12.2 %collective-permute-start.5 = (bf16[48,1408]{1,0:T(8,128)(2,1)S(1)}, bf16[48,1408]{1,0:T(8,128)(2,1)S(1)}, u32[]{:S(2)}, u32[]{:S(2)}) collective-permute-start(bf16[48,1408]{1,0:T(8,128)(2,1)S(1)} %collective-permute-done.4.refs_7_), channel_id=1, source_target_pairs={{0,14},{1,15},{2,0},{3,1},{4,2},{5,3},{6,4},{7,5},{8,6},{9,7},{10,... | collective-permute-start | bytes 405512 | tf_op jit(solution)/shard_map/ppermute | solution.py:261
  31.7 9.5 %collective-permute-start.2 = (bf16[48,1408]{1,0:T(8,128)(2,1)S(1)}, bf16[48,1408]{1,0:T(8,128)(2,1)S(1)}, u32[]{:S(2)}, u32[]{:S(2)}) collective-permute-start(bf16[48,1408]{1,0:T(8,128)(2,1)S(1)} %collective-permute-done.1.refs_2_), channel_id=1, source_target_pairs={{0,2},{1,3},{2,4},{3,5},{4,6},{5,7},{6,8},{7,9},{8,10},{9,11},{10,... | collective-permute-start | bytes 405512 | tf_op jit(solution)/shard_map/ppermute | solution.py:261
  35.3 10.4 %collective-permute-start.6 = (bf16[48,1408]{1,0:T(8,128)(2,1)S(1)}, bf16[48,1408]{1,0:T(8,128)(2,1)S(1)}, u32[]{:S(2)}, u32[]{:S(2)}) collective-permute-start(bf16[48,1408]{1,0:T(8,128)(2,1)S(1)} %collective-permute-done.5.refs_6_), channel_id=1, source_target_pairs={{0,14},{1,15},{2,0},{3,1},{4,2},{5,3},{6,4},{7,5},{8,6},{9,7},{10,... | collective-permute-start | bytes 405512 | tf_op jit(solution)/shard_map/ppermute | solution.py:261
  41.2 11.7 %collective-permute-start.3 = (bf16[48,1408]{1,0:T(8,128)(2,1)S(1)}, bf16[48,1408]{1,0:T(8,128)(2,1)S(1)}, u32[]{:S(2)}, u32[]{:S(2)}) collective-permute-start(bf16[48,1408]{1,0:T(8,128)(2,1)S(1)} %collective-permute-done.2.refs_3_), channel_id=1, source_target_pairs={{0,2},{1,3},{2,4},{3,5},{4,6},{5,7},{6,8},{7,9},{8,10},{9,11},{10,... | collective-permute-start | bytes 405512 | tf_op jit(solution)/shard_map/ppermute | solution.py:261
  54.0 5.0 %collective-permute-start.7 = (bf16[384,1408]{1,0:T(8,128)(2,1)}, bf16[384,1408]{1,0:T(8,128)(2,1)}, u32[]{:S(2)}, u32[]{:S(2)}) collective-permute-start(bf16[384,1408]{1,0:T(8,128)(2,1)} %shard_map.131.mine), channel_id=1, source_target_pairs={{0,1},{1,0},{2,3},{3,2},{4,5},{5,4},{6,7},{7,6},{8,9},{9,8},{10,11... | collective-permute-start | bytes 3244040 | tf_op jit(solution)/shard_map/ppermute | solution.py:274
  58.9 1.1 copy-start.2
  60.0 16.7 %copy-start.22 = (bf16[512]{0:T(512)(128)(2,1)S(1)}, bf16[512]{0:T(512)(128)(2,1)}, u32[]{:S(2)}) copy-start(bf16[512]{0:T(512)(128)(2,1)} %param.18) | copy-start | bytes 3076
  66.0 0.7 copy-start.7
  66.7 0.7 copy-start.9
  67.4 0.7 copy-start.11
  68.1 0.7 copy-start.13
  68.8 0.7 copy-start.15
  69.4 8.3 %copy-start.17 = (bf16[96,768]{1,0:T(8,128)(2,1)}, bf16[96,768]{1,0:T(8,128)(2,1)S(1)}, u32[]{:S(2)}) copy-start(bf16[96,768]{1,0:T(8,128)(2,1)S(1)} %get-tuple-element.28.ctx) | copy-start | bytes 442372
  69.4 16.9 %copy-start.5 = (f32[512]{0:T(512)S(1)}, f32[512]{0:T(512)}, u32[]{:S(2)}) copy-start(f32[512]{0:T(512)} %param.19) | copy-start | bytes 6148
  69.4 16.9 %all-to-all-start = ((bf16[16,64,128]{2,1,0:T(8,128)(2,1)}), bf16[16,64,128]{2,1,0:T(8,128)(2,1)S(1)}, u32[]{:S(2)}, u32[]{:S(2)}) async-start(bf16[16,64,128]{2,1,0:T(8,128)(2,1)} %get-tuple-element.19), calls=%async_computation | async-start | bytes 524288 | tf_op jit(solution)/shard_map/all_to_all | solution.py:321
  86.3 2.6 %copy-start.1 = (bf16[5632,512]{1,0:T(8,128)(2,1)S(1)}, bf16[5632,512]{1,0:T(8,128)(2,1)}, u32[]{:S(2)}) copy-start(bf16[5632,512]{1,0:T(8,128)(2,1)} %all-gather.3.cloned.1.call-done) | copy-start | bytes 17301508
  89.0 0.9 copy-start.3
  89.9 23.8 %copy-start.8 = (f32[768,1]{1,0:T(8,128)S(1)}, f32[768,1]{1,0:T(8,128)}, u32[]{:S(2)}) copy-start(f32[768,1]{1,0:T(8,128)} %copy-done.7) | copy-start | bytes 9220
  89.9 23.8 %copy-start.10 = (bf16[768,96]{1,0:T(8,128)(2,1)S(1)}, bf16[768,96]{1,0:T(8,128)(2,1)}, u32[]{:S(2)}) copy-start(bf16[768,96]{1,0:T(8,128)(2,1)} %copy-done.9) | copy-start | bytes 442372
  89.9 23.8 %copy-start.12 = (bf16[768,96]{1,0:T(8,128)(2,1)S(1)}, bf16[768,96]{1,0:T(8,128)(2,1)}, u32[]{:S(2)}) copy-start(bf16[768,96]{1,0:T(8,128)(2,1)} %copy-done.11) | copy-start | bytes 442372
  89.9 23.8 %copy-start.14 = (bf16[96,768]{1,0:T(8,128)(2,1)S(1)}, bf16[96,768]{1,0:T(8,128)(2,1)}, u32[]{:S(2)}) copy-start(bf16[96,768]{1,0:T(8,128)(2,1)} %copy-done.13) | copy-start | bytes 442372
  89.9 23.8 %copy-start.16 = (bf16[96,768]{1,0:T(8,128)(2,1)S(1)}, bf16[96,768]{1,0:T(8,128)(2,1)}, u32[]{:S(2)}) copy-start(bf16[96,768]{1,0:T(8,128)(2,1)} %copy-done.15) | copy-start | bytes 442372
  89.9 23.8 %copy-start.18 = (bf16[96,768]{1,0:T(8,128)(2,1)S(1)}, bf16[96,768]{1,0:T(8,128)(2,1)}, u32[]{:S(2)}) copy-start(bf16[96,768]{1,0:T(8,128)(2,1)} %copy-done.17) | copy-start | bytes 442372
Sparse Core Ops, SparseCore 0:
  10.8 56.3 all-gather.2

commit v2 on v1

--- a/solution.py
+++ b/solution.py
@@ -7,6 +7,7 @@
 
 HD = 88
 HP = 96
+HL = 128
 DD = 512
 NZ = 8
 NX = 4
@@ -71,8 +72,9 @@
 
 
 def prep(keep, patches, gain):
+    width = patches.shape[1]
     return call(
-        prep_body, [((CAP, patches.shape[1]), BF16), ((CAP, patches.shape[1]), BF16), ((CAP, 128), BF16)],
+        prep_body, [((CAP, width), BF16), ((CAP, width), BF16), ((CAP, 128), BF16)],
         [], 1 << 20, 8, keep, patches, gain)
 
 
@@ -98,52 +100,82 @@
     )(*blocks)
 
 
-def attend_body(mine, other, w_t, swap, extra, sent, q_out, k_out, kt_out, v_out, stats, live_out, ctx_out):
-    def heads(x):
-        qkv = dot_nt(w_t[...], x[...])
-        pad = jnp.zeros((HP - HD, qkv.shape[1]), F32)
-        return [jnp.concatenate([qkv[i * HD:(i + 1) * HD], pad], axis=0) for i in range(3)]
-
-    q, k, v = [jnp.concatenate(pair, axis=1) for pair in zip(heads(mine), heads(other))]
-    q = (q * SCALE).astype(BF16)
-    vt = v.astype(BF16)
-    k_rows = k.T.astype(BF16)
-    live = jnp.concatenate([mine[:, 0:128], other[:, 0:128]], axis=0).astype(F32)[:, 0:1] < 0.5 * DEAD
-    q_out[...] = q
-    k_out[...] = k_rows
-    kt_out[...] = k.astype(BF16)
-    v_out[...] = v.T.astype(BF16)
-    live_out[...] = jnp.where(live, 0.0, -jnp.inf).astype(F32)
+def attend_body(mine, other, w, swap, extra, sent, saved, stats, xs, out, keep, keep_stats, sems):
+    half = ROWS // 2
+    loads = [
+        pltpu.make_async_copy(mine, xs.at[pl.ds(0, half)], sems.at[0]),
+        pltpu.make_async_copy(other, xs.at[pl.ds(half, half)], sems.at[1])]
+    for load in loads:
+        load.start()
+    parts = []
+    for i in range(2):
+        loads[i].wait()
+        parts.append(dot_nt(xs[half * i:half * (i + 1), :], w[...]))
+    qkv = jnp.concatenate(parts, axis=0)
+    k_rows = qkv[:, HL:2 * HL].astype(BF16)
+    q = (qkv[:, 0:HL] * SCALE).T.astype(BF16)
+    vt = qkv[:, 2 * HL:].T.astype(BF16)
+    keep[0:HL, :] = q
+    keep[HL:2 * HL, :] = qkv[:, HL:2 * HL].T.astype(BF16)
+    keep[2 * HL:3 * HL, :] = vt
+    heads = pltpu.make_async_copy(keep.at[pl.ds(0, 3 * HL)], saved.at[pl.ds(0, 3 * HL)], sems.at[2])
+    heads.start()
+    dead = jnp.where(xs[:, 0:128].astype(F32)[:, 0:1] < 0.5 * DEAD, 0.0, -jnp.inf)
     ctx = []
     for i in range(3):
         cols = slice(256 * i, 256 * (i + 1))
-        scores = jnp.where(live, dot(k_rows, q[:, cols]), -jnp.inf)
+        scores = dot(k_rows, q[:, cols]) + dead
         top = jnp.max(scores, axis=0, keepdims=True)
         expo = jnp.exp(scores - top)
         total = jnp.sum(expo, axis=0, keepdims=True)
-        stats[0:1, cols] = top
-        stats[1:2, cols] = total
+        keep_stats[0:1, cols] = top
+        keep_stats[1:2, cols] = total
         ctx.append(dot(vt, (expo / total).astype(BF16)))
-    ctx = jnp.concatenate(ctx, axis=1)
-    ctx = jnp.concatenate([ctx, jnp.zeros((128 - HP, ROWS), F32)], axis=0).astype(BF16)
-    sent[:, 0:CAP, :] = dot_nt(swap[...], ctx).astype(BF16).reshape(16, CAP, 128)
-    sent[:, CAP:, :] = extra[...]
-    ctx_out[...] = dot_nt(ctx, swap[...])[0:HP].astype(BF16)
-
-
-def attend(mine, other, w_t, swap, extra):
-    return call(
+    sums = pltpu.make_async_copy(keep_stats, stats, sems.at[3])
+    sums.start()
+    ctx = jnp.concatenate(ctx, axis=1).astype(BF16)
+    out[:, 0:CAP, :] = dot_nt(swap[...], ctx).astype(BF16).reshape(16, CAP, 128)
+    out[:, CAP:, :] = extra[...]
+    send = pltpu.make_async_copy(out, sent, sems.at[4])
+    send.start()
+    keep[3 * HL:, :] = dot_nt(ctx, swap[...]).astype(BF16)
+    last = pltpu.make_async_copy(keep.at[pl.ds(3 * HL, HL)], saved.at[pl.ds(3 * HL, HL)], sems.at[5])
+    last.start()
+    for copy in (heads, sums, send, last):
+        copy.wait()
+
+
+def attend(*args):
+    vmem = pl.BlockSpec(memory_space=pltpu.VMEM)
+    hbm = pl.BlockSpec(memory_space=pltpu.HBM)
+    return pl.pallas_call(
         attend_body,
-        [((16, 64, 128), BF16), ((HP, ROWS), BF16), ((ROWS, HP), BF16), ((HP, ROWS), BF16), ((ROWS, HP), BF16),
-         ((8, ROWS), F32), ((ROWS, 1), F32), ((HP, ROWS), BF16)],
-        [], 1700 << 20, 20, mine, other, w_t, swap, extra)
-
-
-def decode_body(came, weights, mask, gain, cot, table, recon, dvis, mixed, grad):
+        out_shape=[pltpu.HBM((16, 64, 128), BF16), pltpu.HBM((4 * HL, ROWS), BF16), pltpu.HBM((8, ROWS), F32)],
+        in_specs=[hbm, hbm, vmem, vmem, vmem],
+        out_specs=[hbm, hbm, hbm],
+        scratch_shapes=[pltpu.VMEM((ROWS, args[0].shape[1]), BF16), pltpu.VMEM((16, 64, 128), BF16),
+                        pltpu.VMEM((4 * HL, ROWS), BF16), pltpu.VMEM((8, ROWS), F32), pltpu.SemaphoreType.DMA((6,))],
+        compiler_params=pltpu.CompilerParams(vmem_limit_bytes=24 << 20),
+        cost_estimate=pl.CostEstimate(flops=1700 << 20, bytes_accessed=8 << 20, transcendentals=1 << 20),
+    )(*args)
+
+
+def decode_body(came, weights, cot, mask, gain, table, recon, dvis, mixed, grad, w_oe, w_fc, cots, sems):
+    loads = [
+        pltpu.make_async_copy(
+            weights.at[pl.ds(2 * i, 2), pl.ds(0, 2 * HID)], w_fc.at[pl.ds(2 * i, 2)], sems.at[i])
+        for i in range(8)]
+    oe = pltpu.make_async_copy(weights.at[:, pl.ds(2 * HID, HP)], w_oe, sems.at[8])
+    up = pltpu.make_async_copy(cot, cots, sems.at[9])
+    for load in (oe, up, loads[0]):
+        load.start()
     flat = came[...].reshape(16 * 64, 128)
     vis = jnp.zeros((CAP, DD), F32)
+    oe.wait()
+    for load in loads[1:]:
+        load.start()
     for g in range(16):
-        vis += dot(came[g, 0:CAP, 0:HP], weights[g, 2 * HID:2 * HID + HP, :])
+        vis += dot(came[g, 0:CAP, 0:HP], w_oe[g])
     row = lax.broadcasted_iota(jnp.int32, (CAP, 1024), 0)
     col = lax.broadcasted_iota(jnp.int32, (CAP, 1024), 1)
     source = jnp.zeros((CAP, 1024), jnp.int32)
@@ -171,11 +203,13 @@
     inv_std = lax.rsqrt(var + 1e-06)
     normed = centred * inv_std
     dn = (normed * gain[...]).astype(BF16)
-    cot_b = cot[...]
+    up.wait()
+    cot_b = cots[...]
     mixed[...] = dec_x
     for i in range(8):
-        fin = jnp.concatenate([weights[2 * i, 0:HID, :], weights[2 * i + 1, 0:HID, :]], axis=0)
-        fout = jnp.concatenate([weights[2 * i, HID:2 * HID, :], weights[2 * i + 1, HID:2 * HID, :]], axis=0)
+        loads[i].wait()
+        fin = jnp.concatenate([w_fc[2 * i, 0:HID, :], w_fc[2 * i + 1, 0:HID, :]], axis=0)
+        fout = jnp.concatenate([w_fc[2 * i, HID:2 * HID, :], w_fc[2 * i + 1, HID:2 * HID, :]], axis=0)
         hidden = dot_nt(dn, fin)
         dact = dot_nt(cot_b, fout)
         cdf = 0.5 * (1.0 + lax.erf(hidden * 0.7071067811865476))
@@ -195,32 +229,57 @@
     dvis[...] = dot(picker[0:CAP].astype(BF16), ddec).astype(BF16)
 
 
-def decode(came, weights, mask, gain, cot, table):
-    return call(
-        decode_body, [((FDEV, DD), BF16), ((CAP, DD), BF16)],
-        [pltpu.VMEM((FDEV, DD), F32), pltpu.VMEM((FDEV, DD), F32)], 2300 << 20, 20,
-        came, weights, mask, gain, cot, table)
-
-
-def back_body(dvis, w_oe, swap, q, k, kt, v, stats, dead, ctx, mine, other, parts, ds_all, pb_all):
-    dctx = dot(dot_nt(w_oe[...], dvis[...]).astype(BF16), swap[...]).astype(BF16)
-    grad_oe = dot(ctx[...], dvis[...])[0:HD]
+def decode(came, weights, cot, *args):
+    vmem = pl.BlockSpec(memory_space=pltpu.VMEM)
+    hbm = pl.BlockSpec(memory_space=pltpu.HBM)
+    return pl.pallas_call(
+        decode_body,
+        out_shape=[jax.ShapeDtypeStruct((FDEV, DD), BF16), jax.ShapeDtypeStruct((CAP, DD), BF16)],
+        in_specs=[vmem, hbm, hbm] + [vmem] * len(args),
+        out_specs=[vmem, vmem],
+        scratch_shapes=[pltpu.VMEM((FDEV, DD), F32), pltpu.VMEM((FDEV, DD), F32),
+                        pltpu.VMEM((16, HP, DD), BF16), pltpu.VMEM((16, 2 * HID, DD), BF16),
+                        pltpu.VMEM((FDEV, DD), BF16), pltpu.SemaphoreType.DMA((10,))],
+        compiler_params=pltpu.CompilerParams(vmem_limit_bytes=24 << 20),
+        cost_estimate=pl.CostEstimate(flops=2300 << 20, bytes_accessed=8 << 20, transcendentals=1 << 20),
+    )(came, pltpu.with_memory_space_constraint(weights, pltpu.HBM),
+      pltpu.with_memory_space_constraint(cot, pltpu.HBM), *args)
+
+
+def back_body(dvis, w_oe, swap, saved, stats, mine, other, parts, ds_all, pb_all, keep, keep_stats, xs, sems):
+    loads = [
+        pltpu.make_async_copy(saved, keep, sems.at[0]),
+        pltpu.make_async_copy(stats, keep_stats, sems.at[1]),
+        pltpu.make_async_copy(mine, xs.at[pl.ds(0, ROWS // 2)], sems.at[2]),
+        pltpu.make_async_copy(other, xs.at[pl.ds(ROWS // 2, ROWS // 2)], sems.at[3])]
+    for load in loads:
+        load.start()
+    dctx = dot(dot_nt(w_oe[...], dvis[...]).astype(BF16), swap[...])
+    dctx = jnp.concatenate([dctx, jnp.zeros((HL - HP, ROWS), F32)], axis=0).astype(BF16)
+    for load in loads:
+        load.wait()
+    x = xs[...]
+    grad_oe = dot(keep[3 * HL:, :], dvis[...])[0:HD]
+    q, kt = keep[0:HL, :], keep[HL:2 * HL, :]
+    k = kt.astype(F32).T.astype(BF16)
+    v = keep[2 * HL:3 * HL, :].astype(F32).T.astype(BF16)
+    dead = jnp.where(x[:, 0:128].astype(F32)[:, 0:1] < 0.5 * DEAD, 0.0, -jnp.inf)
     dq = []
     for i in range(3):
         cols = slice(256 * i, 256 * (i + 1))
-        scores = dot(k[...], q[:, cols]) + dead[...]
-        probs = jnp.exp(scores - stats[0:1, cols]) / stats[1:2, cols]
-        dprob = dot(v[...], dctx[:, cols])
+        scores = dot(k, q[:, cols]) + dead
+        probs = jnp.exp(scores - keep_stats[0:1, cols]) / keep_stats[1:2, cols]
+        dprob = dot(v, dctx[:, cols])
         inner = jnp.sum(probs * dprob, axis=0, keepdims=True)
         ds = (probs * (dprob - inner)).astype(BF16)
         ds_all[:, cols] = ds
         pb_all[:, cols] = probs.astype(BF16)
-        dq.append(dot(kt[...], ds) * SCALE)
+        dq.append(dot(kt, ds) * SCALE)
     dq = jnp.concatenate(dq, axis=1)[0:HD]
-    dk = dot_nt(q[...], ds_all[...])[0:HD]
+    dk = dot_nt(q, ds_all[...])[0:HD]
     dv = dot_nt(dctx, pb_all[...])[0:HD]
     dqkv = jnp.concatenate([dq, dk, dv], axis=0).astype(BF16)
-    grad = dot(dqkv[:, 0:ROWS // 2], mine[...]) + dot(dqkv[:, ROWS // 2:], other[...])
+    grad = dot(dqkv, x)
     wide = grad.shape[1] // 128
     pieces = [grad[:, 128 * j:128 * (j + 1)] for j in range(wide)]
     pieces += [grad_oe[:, 128 * j:128 * (j + 1)] for j in range(DD // 128)]
@@ -229,10 +288,37 @@
     parts[...] = jnp.concatenate(pieces, axis=0).astype(BF16)
 
 
-def back(*args):
+def back(dvis, w_oe, swap, saved, stats, mine, other):
+    vmem = pl.BlockSpec(memory_space=pltpu.VMEM)
+    hbm = pl.BlockSpec(memory_space=pltpu.HBM)
+    return pl.pallas_call(
+        back_body,
+        out_shape=jax.ShapeDtypeStruct((GRAD_ROWS, 128), BF16),
+        in_specs=[vmem, vmem, vmem, hbm, hbm, hbm, hbm],
+        out_specs=vmem,
+        scratch_shapes=[pltpu.VMEM((ROWS, ROWS), BF16), pltpu.VMEM((ROWS, ROWS), BF16),
+                        pltpu.VMEM((4 * HL, ROWS), BF16), pltpu.VMEM((8, ROWS), F32),
+                        pltpu.VMEM((ROWS, mine.shape[1]), BF16), pltpu.SemaphoreType.DMA((4,))],
+        compiler_params=pltpu.CompilerParams(vmem_limit_bytes=24 << 20),
+        cost_estimate=pl.CostEstimate(flops=2500 << 20, bytes_accessed=8 << 20, transcendentals=1 << 20),
+    )(dvis, w_oe, swap, saved, stats, mine, other)
+
+
+def finish_body(total, w_e2d, grad_q, grad_o):
+    rows = total[...].astype(F32)
+    wide = grad_q.shape[1] // 128
+    tall = 3 * HD
+    for j in range(wide):
+        grad_q[:, 128 * j:128 * (j + 1)] = rows[tall * j:tall * (j + 1)].astype(BF16)
+    at = tall * wide
+    grad_oe = jnp.concatenate([rows[at + HD * j:at + HD * (j + 1)] for j in range(DD // 128)], axis=1)
+    grad_o[...] = dot_nt(grad_oe.astype(BF16), w_e2d[...]).astype(BF16)
+
+
+def finish(total, w_e2d):
+    width = w_e2d.shape[0]
     return call(
-        back_body, [((GRAD_ROWS, 128), BF16)],
-        [pltpu.VMEM((ROWS, ROWS), BF16), pltpu.VMEM((ROWS, ROWS), BF16)], 2500 << 20, 20, *args)[0]
+        finish_body, [((3 * HD, width), BF16), ((HD, width), BF16)], [], 130 << 20, 12, total, w_e2d)
 
 
 def position_table(positions, width):
@@ -261,12 +347,13 @@
     return lax.ppermute(block, "seq", [(s, (s + 2 * step) % 16) for s in range(16)])
 
 
-def ring(block):
-    got = {0: block, 8: block}
-    for step in range(1, 5):
-        got[step] = z_shift(got[step - 1], 1)
-        if step < 4:
-            got[8 - step] = z_shift(got[9 - step], -1)
+def around(block):
+    got = {0: block}
+    for step in (1, -1, 2, -2):
+        got[step % NZ] = z_shift(block, step)
+    got[3] = z_shift(got[2], 1)
+    got[5] = z_shift(got[6], -1)
+    got[4] = z_shift(got[2], 2)
     return [got[k] for k in range(NZ)]
 
 
@@ -289,15 +376,14 @@
     cotangent,
 ):
     me = lax.axis_index("seq")
-    my_c = me % 2
+    my_z, my_c = me // 2, me % 2
     fdev = cotangent.shape[1]
-    my_z = me // 2
     cot = cotangent[0]
     cap = keep_pos.shape[1]
     rows = 16 * cap
 
     xn_own, x_slot, offsets = prep(keep_pos, patches[0], enc_gain[None])
-    mine = join(ring(xn_own))
+    mine = join(around(xn_own))
     other = swap_core(mine)
 
     x_vis = dot(x_slot, w_e2d).astype(BF16)
@@ -316,22 +402,19 @@
     swap = (dest[None, :] == tok[:, None]).astype(BF16)
     table = position_table((me * fdev + jnp.arange(fdev, dtype=jnp.int32)).astype(F32), DD)
 
-    w_t = w_qkv.transpose(0, 2, 1).reshape(3 * HD, -1)
-    sent, q, k, k_t, v, stats, dead, ctx = attend(mine, other, w_t, swap, extra)
+    w = jnp.pad(w_qkv.transpose(0, 2, 1), ((0, 0), (0, HL - HD), (0, 0))).reshape(3 * HL, -1)
+    sent, saved, stats = attend(mine, other, w, swap, extra)
     came = lax.all_to_all(sent, "seq", 0, 0, tiled=True)
-    recon, dvis_own = decode(came, weights, mask_token[None], dec_gain[None], cot, table)
+    recon, dvis_own = decode(came, weights, cot, mask_token[None], dec_gain[None], table)
     dvis = lax.all_gather(dvis_own, "seq", axis=0, tiled=True)
-    parts = back(dvis, w_oe_own, swap, q, k, k_t, v, stats, dead, ctx, mine, other)
+    parts = back(dvis, w_oe_own, swap, saved, stats, mine, other)
 
     parts = jnp.sum(exchange(parts.reshape(NX, 832, 128), "dp", X_GROUPS).astype(F32), axis=0).astype(BF16)
     parts = jnp.sum(exchange(parts.reshape(NY, 104, 128), "dp", Y_GROUPS).astype(F32), axis=0).astype(BF16)
     parts = spread(parts, "dp", Y_GROUPS).reshape(832, 128)
     total = spread(parts, "dp", X_GROUPS).reshape(GRAD_ROWS, 128)
-    wide = w_qkv.shape[1] // 128
-    cut = 3 * HD * wide
-    grad_q = total[:cut].reshape(wide, 3 * HD, 128).transpose(1, 0, 2).reshape(3, HD, wide * 128).transpose(0, 2, 1)
-    grad_oe = total[cut:cut + 4 * HD].reshape(4, HD, 128).transpose(1, 0, 2).reshape(HD, DD)
-    grad_o = dot_nt(grad_oe, w_e2d).astype(BF16)
+    grad_q, grad_o = finish(total, w_e2d)
+    grad_q = grad_q.reshape(3, HD, -1).transpose(0, 2, 1)
     return (recon[None], grad_q, grad_o)
 
 

time: 190 us -> 181 us (0.953)
  local copies, waits for them, and re-layouts: 11.6 us -> 3.82 us
  waiting for transfers between devices: 26.2 us -> 20.5 us
  Pallas kernels: 18 us -> 22.9 us
    pallas_call x0 -> x3, Pallas kernels: none -> 19.8 us  [the longest x1 8.25 us: decode(): pl.pallas_call(decode_body, out_shape=[jax.ShapeDtypeStruct((FDEV, DD), B...]
    pallas_call x4 -> x2, Pallas kernels: 17 us -> 2 us  [call(): pl.pallas_call(body, out_shape=[jax.ShapeDtypeStruct(shape, dtype) for sh...]
    unnamed x46 -> x26, local copies, waits for them, and re-layouts: 9.45 us -> 2.15 us
    ppermute x7, waiting for transfers between devices: 16 us -> 11.2 us  [z_shift(): lax.ppermute(block, 'seq', [(s, (s + 2 * step) % 16) for s in range(16)])]
    ppermute x7, starting transfers between devices: 25.6 us -> 28.6 us  [z_shift(): lax.ppermute(block, 'seq', [(s, (s + 2 * step) % 16) for s in range(16)])]
    all_to_all x1, starting transfers between devices: 7.24 us -> 5.34 us  [local(): came = lax.all_to_all(sent, 'seq', 0, 0, tiled=True)]
  transfers between devices with their start and end apart: 10 -> 10, of which waited for: 8 -> 4; matrix products, arithmetic and copies ran while one was open for 1% -> 2% of each run, Pallas kernels for 4% -> 4%
where the time goes in v2:
time: 181 us; the launch traced here: 180 us
  blocking collectives  77.8 us (43%)
  starting transfers between devices  36.1 us (20%)
  Pallas kernels  22.9 us (13%)
  waiting for transfers between devices  20.5 us (11%)
  between operations  14.4 us (8%)
  local copies, waits for them, and re-layouts  3.82 us (2%)
  other arithmetic  2.57 us (1%)
  matrix products  2.06 us (1%)
    all_to_all x4, blocking collectives, exchange(): lax.all_to_all(block, axis, 0, 0, axis_index_groups=groups, tiled=True)  59.2 us
    ppermute x7, starting transfers between devices, z_shift(): lax.ppermute(block, 'seq', [(s, (s + 2 * step) % 16) for s in range(16)])  28.6 us
    all_gather x1, blocking collectives, local(): dvis = lax.all_gather(dvis_own, 'seq', axis=0, tiled=True)  18.6 us
    ppermute x7, waiting for transfers between devices, z_shift(): lax.ppermute(block, 'seq', [(s, (s + 2 * step) % 16) for s in range(16)])  11.2 us
    all_to_all x1, waiting for transfers between devices, local(): came = lax.all_to_all(sent, 'seq', 0, 0, tiled=True)  8.66 us
    pallas_call x1, Pallas kernels, decode(): pl.pallas_call(decode_body, out_shape=[jax.ShapeDtypeStruct((FDEV, DD), B...  8.25 us
    pallas_call x1, Pallas kernels, attend(): pl.pallas_call(attend_body, out_shape=[pltpu.HBM((16, 64, 128), BF16), pl...  6.27 us
    all_to_all x1, starting transfers between devices, local(): came = lax.all_to_all(sent, 'seq', 0, 0, tiled=True)  5.34 us
  transfers between devices with their start and end apart: 10, of which 4 were waited for; matrix products, arithmetic and copies ran while one was open for 2% of the time, Pallas kernels for 4%

profile of v2, /device:TPU:64, one launch (start us, length us, event | category | flops | bytes accessed | tf_op | source)
XLA Modules:
  0.0 180.1 jit_solution(7287311246744800757)
XLA Ops:
  7.2 0.0 copy-start
  7.2 0.0 copy-start.10
  7.2 0.0 copy-start.9
  7.2 0.0 copy-start.11
  7.2 0.0 copy-start.3
  7.2 0.0 copy-start.5
  7.2 0.0 all-gather.3.cloned.1.call-start
  7.3 0.8 copy-done
  8.1 1.7 convolution_convert_fusion
  9.9 0.0 copy-done.10
  9.9 0.0 copy-done.9
  9.9 0.8 pad_maximum_fusion.1
  10.6 0.0 all-gather.3.cloned.1.call-update
  10.7 0.0 copy-done.11
  10.7 0.0 copy-done.3
  10.7 0.0 copy-done.5
  10.7 0.5 shard_map.130
  11.2 0.0 copy-start.1
  11.2 6.2 %collective-permute-start.1 = (bf16[48,1408]{1,0:T(8,128)(2,1)S(1)}, bf16[48,1408]{1,0:T(8,128)(2,1)S(1)}, u32[]{:S(2)}, u32[]{:S(2)}) collective-permute-start(bf16[48,1408]{1,0:T(8,128)(2,1)S(1)} %get-tuple-element.13.refs_0_), channel_id=1, source_target_pairs={{0,4},{1,5},{2,6},{3,7},{4,8},{5,9},{6,10},{7,11},{8,12},{9,13},{1... | collective-permute-start | bytes 405512 | tf_op jit(solution)/shard_map/ppermute | solution.py:347
  17.4 5.9 %collective-permute-start.4 = (bf16[48,1408]{1,0:T(8,128)(2,1)S(1)}, bf16[48,1408]{1,0:T(8,128)(2,1)S(1)}, u32[]{:S(2)}, u32[]{:S(2)}) collective-permute-start(bf16[48,1408]{1,0:T(8,128)(2,1)S(1)} %get-tuple-element.13.refs_0_), channel_id=1, source_target_pairs={{0,12},{1,13},{2,14},{3,15},{4,0},{5,1},{6,2},{7,3},{8,4},{9,5},{1... | collective-permute-start | bytes 405512 | tf_op jit(solution)/shard_map/ppermute | solution.py:347
  23.3 1.9 %collective-permute-start = (bf16[48,1408]{1,0:T(8,128)(2,1)S(1)}, bf16[48,1408]{1,0:T(8,128)(2,1)S(1)}, u32[]{:S(2)}, u32[]{:S(2)}) collective-permute-start(bf16[48,1408]{1,0:T(8,128)(2,1)S(1)} %get-tuple-element.13.refs_0_), channel_id=1, source_target_pairs={{0,2},{1,3},{2,4},{3,5},{4,6},{5,7},{6,8},{7,9},{8,10},{9,11},{10,... | collective-permute-start | bytes 405512 | tf_op jit(solution)/shard_map/ppermute | solution.py:347
  25.2 3.9 %collective-permute-start.6 = (bf16[48,1408]{1,0:T(8,128)(2,1)S(1)}, bf16[48,1408]{1,0:T(8,128)(2,1)S(1)}, u32[]{:S(2)}, u32[]{:S(2)}) collective-permute-start(bf16[48,1408]{1,0:T(8,128)(2,1)S(1)} %get-tuple-element.13.refs_0_), channel_id=1, source_target_pairs={{0,14},{1,15},{2,0},{3,1},{4,2},{5,3},{6,4},{7,5},{8,6},{9,7},{10,... | collective-permute-start | bytes 405512 | tf_op jit(solution)/shard_map/ppermute | solution.py:347
  29.2 0.0 collective-permute-done.1.refs_2_
  29.2 1.9 %collective-permute-start.2 = (bf16[48,1408]{1,0:T(8,128)(2,1)S(1)}, bf16[48,1408]{1,0:T(8,128)(2,1)S(1)}, u32[]{:S(2)}, u32[]{:S(2)}) collective-permute-start(bf16[48,1408]{1,0:T(8,128)(2,1)S(1)} %collective-permute-done.1.refs_2_), channel_id=1, source_target_pairs={{0,2},{1,3},{2,4},{3,5},{4,6},{5,7},{6,8},{7,9},{8,10},{9,11},{10,... | collective-permute-start | bytes 405512 | tf_op jit(solution)/shard_map/ppermute | solution.py:347
  31.1 6.9 %collective-permute-start.3 = (bf16[48,1408]{1,0:T(8,128)(2,1)S(1)}, bf16[48,1408]{1,0:T(8,128)(2,1)S(1)}, u32[]{:S(2)}, u32[]{:S(2)}) collective-permute-start(bf16[48,1408]{1,0:T(8,128)(2,1)S(1)} %collective-permute-done.1.refs_2_), channel_id=1, source_target_pairs={{0,4},{1,5},{2,6},{3,7},{4,8},{5,9},{6,10},{7,11},{8,12},{9,13},{1... | collective-permute-start | bytes 405512 | tf_op jit(solution)/shard_map/ppermute | solution.py:347
  38.0 0.0 collective-permute-done.4.refs_6_
  38.0 1.9 %collective-permute-start.5 = (bf16[48,1408]{1,0:T(8,128)(2,1)S(1)}, bf16[48,1408]{1,0:T(8,128)(2,1)S(1)}, u32[]{:S(2)}, u32[]{:S(2)}) collective-permute-start(bf16[48,1408]{1,0:T(8,128)(2,1)S(1)} %collective-permute-done.4.refs_6_), channel_id=1, source_target_pairs={{0,14},{1,15},{2,0},{3,1},{4,2},{5,3},{6,4},{7,5},{8,6},{9,7},{10,... | collective-permute-start | bytes 405512 | tf_op jit(solution)/shard_map/ppermute | solution.py:347
  39.9 0.0 collective-permute-done.refs_1_
  39.9 0.0 collective-permute-done.6.refs_7_
  39.9 0.5 collective-permute-done.2.refs_3_
  40.5 10.7 %collective-permute-done.3.refs_4_ = bf16[48,1408]{1,0:T(8,128)(2,1)S(1)} collective-permute-done((bf16[48,1408]{1,0:T(8,128)(2,1)S(1)}, bf16[48,1408]{1,0:T(8,128)(2,1)S(1)}, u32[]{:S(2)}, u32[]{:S(2)}) %collective-permute-start.3) | collective-permute-done | bytes 135200 | tf_op jit(solution)/shard_map/ppermute | solution.py:347
  51.1 0.0 collective-permute-done.5.refs_5_
  51.2 1.1 shard_map.131.mine
  52.2 0.0 copy-start.8
  52.2 2.1 %collective-permute-start.7 = (bf16[384,1408]{1,0:T(8,128)(2,1)}, bf16[384,1408]{1,0:T(8,128)(2,1)}, u32[]{:S(2)}, u32[]{:S(2)}) collective-permute-start(bf16[384,1408]{1,0:T(8,128)(2,1)} %shard_map.131.mine), channel_id=1, source_target_pairs={{0,1},{1,0},{2,3},{3,2},{4,5},{5,4},{6,7},{7,6},{8,9},{9,8},{10,11... | collective-permute-start | bytes 3244040 | tf_op jit(solution)/shard_map/ppermute | solution.py:361
  54.3 0.0 copy-done.1
  54.3 0.3 convolution_convert_fusion.1
  54.7 0.1 reshape.112
  54.8 0.1 slice_reduce_fusion
  54.9 0.1 reshape_squeeze.4
  55.0 0.0 copy-done.8
  55.0 1.1 pad.12
  56.1 0.1 pad.22.clone
  56.3 0.1 fusion.4.extra
  56.3 0.4 fusion.swap
  56.8 0.6 collective-permute-done.7.other
  57.3 1.3 copy-done.2
  58.6 6.3 %shard_map.132 = (bf16[16,64,128]{2,1,0:T(8,128)(2,1)}, bf16[512,768]{1,0:T(8,128)(2,1)}, f32[8,768]{1,0:T(8,128)}) custom-call(bf16[384,1408]{1,0:T(8,128)(2,1)} %shard_map.131.mine, bf16[384,1408]{1,0:T(8,128)(2,1)} %collective-permute-done.7.other, bf16[384,1408]{1,0:T(8,128)(2,1)S(1)} %bitcast.19, bf16[768,768]{1,0:T(8,128)(2,1)S(1)} %fusion.swap, ...), custom_call_target="tpu_custom_call" | custom-call | flops 1782579200 | bytes 8388608 | tf_op jit(solution)/shard_map/pallas_call | solution.py:151
  64.9 0.0 copy-start.4
  64.9 5.3 %all-to-all-start = ((bf16[16,64,128]{2,1,0:T(8,128)(2,1)}), bf16[16,64,128]{2,1,0:T(8,128)(2,1)}, u32[]{:S(2)}, u32[]{:S(2)}) async-start(bf16[16,64,128]{2,1,0:T(8,128)(2,1)} %get-tuple-element.16), calls=%async_computation | async-start | bytes 524288 | tf_op jit(solution)/shard_map/all_to_all | solution.py:407
  70.2 1.0 multiply_sine_fusion
  71.2 0.1 pad_maximum_fusion.table
  71.3 8.7 %all-to-all-done.came = bf16[16,64,128]{2,1,0:T(8,128)(2,1)} async-done(((bf16[16,64,128]{2,1,0:T(8,128)(2,1)}), bf16[16,64,128]{2,1,0:T(8,128)(2,1)}, u32[]{:S(2)}, u32[]{:S(2)}) %all-to-all-start) | async-done | bytes 262176 | tf_op jit(solution)/shard_map/all_to_all | solution.py:407
  80.0 8.2 %shard_map.133 = (bf16[256,512]{1,0:T(8,128)(2,1)}, bf16[48,512]{1,0:T(8,128)(2,1)S(1)}) custom-call(bf16[16,64,128]{2,1,0:T(8,128)(2,1)} %all-to-all-done.came, bf16[16,352,512]{2,1,0:T(8,128)(2,1)} %bitcast.26, bf16[256,512]{1,0:T(8,128)(2,1)} %bitcast.28, bf16[1,512]{1,0:T(2,128)(2,1)S(1)} %broadcast_in_dim.34.mask, f32[1,512]{1,0:T(1,128)S(1)} %bitcast.22, ...), custom_call_target="tpu_custom_call" | custom-call | flops 2411724800 | bytes 8388608 | tf_op jit(solution)/shard_map/pallas_call | solution.py:235
  88.2 18.6 %all_gather.11.dvis = bf16[768,512]{1,0:T(8,128)(2,1)S(1)} all-gather(bf16[48,512]{1,0:T(8,128)(2,1)S(1)} %get-tuple-element.18), channel_id=1, replica_groups=mesh['dp'=32,'seq'=16] {'seq'}, dimensions={0}, use_global_device_ids=true | all-gather | bytes 835584 | tf_op jit(solution)/shard_map/all_gather | solution.py:409
  106.8 0.0 copy-done.7
  106.8 5.3 %shard_map.134 = bf16[3328,128]{1,0:T(8,128)(2,1)S(1)} custom-call(bf16[768,512]{1,0:T(8,128)(2,1)S(1)} %all_gather.11.dvis, bf16[96,512]{1,0:T(8,128)(2,1)S(1)} %pad.14.w_oe, bf16[768,768]{1,0:T(8,128)(2,1)S(1)} %fusion.swap, bf16[512,768]{1,0:T(8,128)(2,1)S(1)} %copy-done.6, f32[8,768]{1,0:T(8,128)S(1)} %copy-done.7, bf16[384,1408]{1,0:T(8,128)(2,1)} %shard_map.131.mine, ...), custom_call_target="tpu_custom_call" | custom-call | flops 2621440000 | bytes 8388608 | tf_op jit(solution)/shard_map/pallas_call | solution.py:294
  112.1 17.6 %all_to_all.25 = bf16[4,832,128]{2,1,0:T(8,128)(2,1)S(1)} all-to-all(bf16[4,832,128]{2,1,0:T(8,128)(2,1)S(1)} %bitcast.20), channel_id=1, replica_groups={{0,16,32,48},{64,80,96,112},{128,144,160,176},{192,208,224,240},{256,27..., dimensions={0} | all-to-all | bytes 1703936 | tf_op jit(solution)/shard_map/all_to_all | solution.py:337
  129.7 0.2 reduce_sum.24
  129.9 17.0 %all_to_all.26 = bf16[8,104,128]{2,1,0:T(8,128)(2,1)S(1)} all-to-all(bf16[8,104,128]{2,1,0:T(8,128)(2,1)S(1)} %bitcast.23), channel_id=1, replica_groups={{0,64,128,192,256,320,384,448},{16,80,144,208,272,336,400,464},{32,96,1..., dimensions={0} | all-to-all | bytes 425984 | tf_op jit(solution)/shard_map/all_to_all | solution.py:337
  147.0 12.4 %all_to_all.27 = bf16[8,104,128]{2,1,0:T(8,128)(2,1)S(1)} all-to-all(bf16[8,104,128]{2,1,0:T(8,128)(2,1)S(1)} %broadcast_in_dim.37), channel_id=1, replica_groups={{0,64,128,192,256,320,384,448},{16,80,144,208,272,336,400,464},{32,96,1..., dimensions={0} | all-to-all | bytes 425984 | tf_op jit(solution)/shard_map/all_to_all | solution.py:337
  159.3 0.1 broadcast_in_dim.39
  159.4 12.2 %all_to_all.28 = bf16[4,832,128]{2,1,0:T(8,128)(2,1)S(1)} all-to-all(bf16[4,832,128]{2,1,0:T(8,128)(2,1)S(1)} %broadcast_in_dim.39), channel_id=1, replica_groups={{0,16,32,48},{64,80,96,112},{128,144,160,176},{192,208,224,240},{256,27..., dimensions={0} | all-to-all | bytes 1703936 | tf_op jit(solution)/shard_map/all_to_all | solution.py:337
  171.7 1.5 shard_map.135
  (17 shorter events, 0.1 us)
Async XLA Ops:
  7.2 1.0 copy-start
  7.2 2.7 %copy-start.10 = (bf16[128,512]{1,0:T(8,128)(2,1)S(1)}, bf16[128,512]{1,0:T(8,128)(2,1)}, u32[]{:S(2)}) copy-start(bf16[128,512]{1,0:T(8,128)(2,1)} %param.20) | copy-start | bytes 393220
  7.2 2.7 %copy-start.9 = (bf16[128,512]{1,0:T(8,128)(2,1)S(1)}, bf16[128,512]{1,0:T(8,128)(2,1)}, u32[]{:S(2)}) copy-start(bf16[128,512]{1,0:T(8,128)(2,1)} %param.21) | copy-start | bytes 393220
  7.2 3.5 %copy-start.11 = (f32[1408]{0:T(1024)S(1)}, f32[1408]{0:T(1024)}, u32[]{:S(2)}) copy-start(f32[1408]{0:T(1024)} %param.14) | copy-start | bytes 16900
  7.2 3.5 %copy-start.3 = (bf16[1,48,1408]{2,1,0:T(8,128)(2,1)S(1)}, bf16[1,48,1408]{2,1,0:T(8,128)(2,1)}, u32[]{:S(2)}) copy-start(bf16[1,48,1408]{2,1,0:T(8,128)(2,1)} %param.12) | copy-start | bytes 405508
  7.2 3.5 %copy-start.5 = (s32[1,48]{1,0:T(1,128)S(1)}, s32[1,48]{1,0:T(1,128)}, u32[]{:S(2)}) copy-start(s32[1,48]{1,0:T(1,128)} %keep.1) | copy-start | bytes 580
  7.2 72.7 %all-gather.3.cloned.1.call-start = ((), (), s32[]{:S(2)}) async-start(), calls=%async_computation.5 | async-start | bytes 6127616 | tf_op jit(solution)/shard_map/all_gather | solution.py:395
  11.2 43.1 %copy-start.1 = (bf16[1408,512]{1,0:T(8,128)(2,1)S(1)}, bf16[1408,512]{1,0:T(8,128)(2,1)}, u32[]{:S(2)}) copy-start(bf16[1408,512]{1,0:T(8,128)(2,1)} %w_e2d.1) | copy-start | bytes 4325380
  11.2 18.0 %collective-permute-start.1 = (bf16[48,1408]{1,0:T(8,128)(2,1)S(1)}, bf16[48,1408]{1,0:T(8,128)(2,1)S(1)}, u32[]{:S(2)}, u32[]{:S(2)}) collective-permute-start(bf16[48,1408]{1,0:T(8,128)(2,1)S(1)} %get-tuple-element.13.refs_0_), channel_id=1, source_target_pairs={{0,4},{1,5},{2,6},{3,7},{4,8},{5,9},{6,10},{7,11},{8,12},{9,13},{1... | collective-permute-start | bytes 405512 | tf_op jit(solution)/shard_map/ppermute | solution.py:347
  17.4 20.5 %collective-permute-start.4 = (bf16[48,1408]{1,0:T(8,128)(2,1)S(1)}, bf16[48,1408]{1,0:T(8,128)(2,1)S(1)}, u32[]{:S(2)}, u32[]{:S(2)}) collective-permute-start(bf16[48,1408]{1,0:T(8,128)(2,1)S(1)} %get-tuple-element.13.refs_0_), channel_id=1, source_target_pairs={{0,12},{1,13},{2,14},{3,15},{4,0},{5,1},{6,2},{7,3},{8,4},{9,5},{1... | collective-permute-start | bytes 405512 | tf_op jit(solution)/shard_map/ppermute | solution.py:347
  23.3 16.6 %collective-permute-start = (bf16[48,1408]{1,0:T(8,128)(2,1)S(1)}, bf16[48,1408]{1,0:T(8,128)(2,1)S(1)}, u32[]{:S(2)}, u32[]{:S(2)}) collective-permute-start(bf16[48,1408]{1,0:T(8,128)(2,1)S(1)} %get-tuple-element.13.refs_0_), channel_id=1, source_target_pairs={{0,2},{1,3},{2,4},{3,5},{4,6},{5,7},{6,8},{7,9},{8,10},{9,11},{10,... | collective-permute-start | bytes 405512 | tf_op jit(solution)/shard_map/ppermute | solution.py:347
  25.2 14.7 %collective-permute-start.6 = (bf16[48,1408]{1,0:T(8,128)(2,1)S(1)}, bf16[48,1408]{1,0:T(8,128)(2,1)S(1)}, u32[]{:S(2)}, u32[]{:S(2)}) collective-permute-start(bf16[48,1408]{1,0:T(8,128)(2,1)S(1)} %get-tuple-element.13.refs_0_), channel_id=1, source_target_pairs={{0,14},{1,15},{2,0},{3,1},{4,2},{5,3},{6,4},{7,5},{8,6},{9,7},{10,... | collective-permute-start | bytes 405512 | tf_op jit(solution)/shard_map/ppermute | solution.py:347
  29.2 11.3 %collective-permute-start.2 = (bf16[48,1408]{1,0:T(8,128)(2,1)S(1)}, bf16[48,1408]{1,0:T(8,128)(2,1)S(1)}, u32[]{:S(2)}, u32[]{:S(2)}) collective-permute-start(bf16[48,1408]{1,0:T(8,128)(2,1)S(1)} %collective-permute-done.1.refs_2_), channel_id=1, source_target_pairs={{0,2},{1,3},{2,4},{3,5},{4,6},{5,7},{6,8},{7,9},{8,10},{9,11},{10,... | collective-permute-start | bytes 405512 | tf_op jit(solution)/shard_map/ppermute | solution.py:347
  31.1 20.0 %collective-permute-start.3 = (bf16[48,1408]{1,0:T(8,128)(2,1)S(1)}, bf16[48,1408]{1,0:T(8,128)(2,1)S(1)}, u32[]{:S(2)}, u32[]{:S(2)}) collective-permute-start(bf16[48,1408]{1,0:T(8,128)(2,1)S(1)} %collective-permute-done.1.refs_2_), channel_id=1, source_target_pairs={{0,4},{1,5},{2,6},{3,7},{4,8},{5,9},{6,10},{7,11},{8,12},{9,13},{1... | collective-permute-start | bytes 405512 | tf_op jit(solution)/shard_map/ppermute | solution.py:347
  38.0 13.2 %collective-permute-start.5 = (bf16[48,1408]{1,0:T(8,128)(2,1)S(1)}, bf16[48,1408]{1,0:T(8,128)(2,1)S(1)}, u32[]{:S(2)}, u32[]{:S(2)}) collective-permute-start(bf16[48,1408]{1,0:T(8,128)(2,1)S(1)} %collective-permute-done.4.refs_6_), channel_id=1, source_target_pairs={{0,14},{1,15},{2,0},{3,1},{4,2},{5,3},{6,4},{7,5},{8,6},{9,7},{10,... | collective-permute-start | bytes 405512 | tf_op jit(solution)/shard_map/ppermute | solution.py:347
  52.2 2.8 %copy-start.8 = (bf16[3,1408,88]{1,2,0:T(8,128)(2,1)S(1)}, bf16[3,1408,88]{1,2,0:T(8,128)(2,1)}, u32[]{:S(2)}) copy-start(bf16[3,1408,88]{1,2,0:T(8,128)(2,1)} %param.15) | copy-start | bytes 2230276
  52.2 5.1 %collective-permute-start.7 = (bf16[384,1408]{1,0:T(8,128)(2,1)}, bf16[384,1408]{1,0:T(8,128)(2,1)}, u32[]{:S(2)}, u32[]{:S(2)}) collective-permute-start(bf16[384,1408]{1,0:T(8,128)(2,1)} %shard_map.131.mine), channel_id=1, source_target_pairs={{0,1},{1,0},{2,3},{3,2},{4,5},{5,4},{6,7},{7,6},{8,9},{9,8},{10,11... | collective-permute-start | bytes 3244040 | tf_op jit(solution)/shard_map/ppermute | solution.py:361
  57.3 1.3 copy-start.2
  58.6 11.6 %copy-start.12 = (bf16[512]{0:T(512)(128)(2,1)S(1)}, bf16[512]{0:T(512)(128)(2,1)}, u32[]{:S(2)}) copy-start(bf16[512]{0:T(512)(128)(2,1)} %param.18) | copy-start | bytes 3076
  64.9 15.1 %copy-start.4 = (f32[512]{0:T(512)S(1)}, f32[512]{0:T(512)}, u32[]{:S(2)}) copy-start(f32[512]{0:T(512)} %param.19) | copy-start | bytes 6148
  64.9 15.1 %all-to-all-start = ((bf16[16,64,128]{2,1,0:T(8,128)(2,1)}), bf16[16,64,128]{2,1,0:T(8,128)(2,1)}, u32[]{:S(2)}, u32[]{:S(2)}) async-start(bf16[16,64,128]{2,1,0:T(8,128)(2,1)} %get-tuple-element.16), calls=%async_computation | async-start | bytes 524288 | tf_op jit(solution)/shard_map/all_to_all | solution.py:407
  80.0 26.9 %copy-start.6 = (bf16[512,768]{1,0:T(8,128)(2,1)S(1)}, bf16[512,768]{1,0:T(8,128)(2,1)}, u32[]{:S(2)}) copy-start(bf16[512,768]{1,0:T(8,128)(2,1)} %get-tuple-element.19.saved) | copy-start | bytes 2359300
  80.0 26.9 %copy-start.7 = (f32[8,768]{1,0:T(8,128)S(1)}, f32[8,768]{1,0:T(8,128)}, u32[]{:S(2)}) copy-start(f32[8,768]{1,0:T(8,128)} %get-tuple-element.20.stats) | copy-start | bytes 73732
Sparse Core Ops, SparseCore 0:
  10.8 59.4 all-gather.2

commit v3 on v2

--- a/solution.py
+++ b/solution.py
@@ -51,7 +51,16 @@
     )(*args)
 
 
-def prep_body(keep, patches, gain, xn, x_slot, offsets):
+def prep_body(keep, gain, patches, w_out, w_e2d, fc_in, fc_out, xn, x_vis, offsets, w_oe, pack,
+              x_in, out_in, e2d_in, packed, sems):
+    loads = [
+        pltpu.make_async_copy(patches, x_in, sems.at[0]),
+        pltpu.make_async_copy(w_out, out_in, sems.at[1]),
+        pltpu.make_async_copy(w_e2d, e2d_in, sems.at[2]),
+        pltpu.make_async_copy(fc_in, packed.at[pl.ds(0, HID)], sems.at[3]),
+        pltpu.make_async_copy(fc_out, packed.at[pl.ds(HID, HID)], sems.at[4])]
+    for copy in loads:
+        copy.start()
     at_row = lax.broadcasted_iota(jnp.int32, (CAP, CAP), 0)
     at_col = lax.broadcasted_iota(jnp.int32, (CAP, CAP), 1)
     own = jnp.broadcast_to(keep[...], (CAP, CAP))
@@ -63,19 +72,50 @@
     pick = at_row == slot
     live = jnp.sum(pick.astype(F32), axis=1, keepdims=True) > 0.5
     spot = jnp.sum(jnp.where(pick, own - owner * FDEV, 0).astype(F32), axis=1, keepdims=True)
-    rows = dot(pick.astype(F32).astype(BF16), patches[...])
-    x_slot[...] = rows.astype(BF16)
+    loads[0].wait()
+    rows = dot(pick.astype(F32).astype(BF16), x_in[...])
     lane = lax.broadcasted_iota(jnp.int32, rows.shape, 1)
     dead_row = jnp.where(lane == 0, DEAD, 0.0)
     xn[...] = jnp.where(live, layer_norm(rows, gain[...]), dead_row).astype(BF16)
     offsets[...] = jnp.broadcast_to(jnp.where(live, spot, -1.0), (CAP, 128)).astype(BF16)
-
-
-def prep(keep, patches, gain):
-    width = patches.shape[1]
-    return call(
-        prep_body, [((CAP, width), BF16), ((CAP, width), BF16), ((CAP, 128), BF16)],
-        [], 1 << 20, 8, keep, patches, gain)
+    for copy in loads[1:]:
+        copy.wait()
+    both = jnp.concatenate([dot(out_in[...], e2d_in[...]), jnp.zeros((HP - HD, DD), F32)], axis=0).astype(BF16)
+    w_oe[...] = both
+    packed[2 * HID:, :] = both
+    done = pltpu.make_async_copy(packed, pack, sems.at[5])
+    done.start()
+    x_vis[...] = dot(rows.astype(BF16), e2d_in[...]).astype(BF16)
+    done.wait()
+
+
+def prep(keep, gain, *args):
+    width = gain.shape[1]
+    vmem = pl.BlockSpec(memory_space=pltpu.VMEM)
+    hbm = pl.BlockSpec(memory_space=pltpu.HBM)
+    return pl.pallas_call(
+        prep_body,
+        out_shape=[jax.ShapeDtypeStruct((CAP, width), BF16), jax.ShapeDtypeStruct((CAP, DD), BF16),
+                   jax.ShapeDtypeStruct((CAP, 128), BF16), jax.ShapeDtypeStruct((HP, DD), BF16),
+                   pltpu.HBM((2 * HID + HP, DD), BF16)],
+        in_specs=[vmem, vmem] + [hbm] * len(args),
+        out_specs=[vmem, vmem, vmem, vmem, hbm],
+        scratch_shapes=[pltpu.VMEM((CAP, width), BF16), pltpu.VMEM((HD, width), BF16), pltpu.VMEM((width, DD), BF16),
+                        pltpu.VMEM((2 * HID + HP, DD), BF16), pltpu.SemaphoreType.DMA((6,))],
+        compiler_params=pltpu.CompilerParams(vmem_limit_bytes=12 << 20),
+        cost_estimate=pl.CostEstimate(flops=200 << 20, bytes_accessed=3 << 20, transcendentals=0),
+    )(keep, gain, *[pltpu.with_memory_space_constraint(arg, pltpu.HBM) for arg in args])
+
+
+def turn_body(w_t, w):
+    rows = w_t[...].astype(F32)
+    gap = jnp.zeros((HL - HD, rows.shape[1]), F32)
+    heads = [part for i in range(3) for part in (rows[HD * i:HD * (i + 1)], gap)]
+    w[...] = jnp.concatenate(heads, axis=0).T.astype(BF16)
+
+
+def turn(w_t):
+    return call(turn_body, [((w_t.shape[1], 3 * HL), BF16)], [], 1 << 20, 16, w_t)[0]
 
 
 def join_body(*refs):
@@ -110,7 +150,7 @@
     parts = []
     for i in range(2):
         loads[i].wait()
-        parts.append(dot_nt(xs[half * i:half * (i + 1), :], w[...]))
+        parts.append(dot(xs[half * i:half * (i + 1), :], w[...]))
     qkv = jnp.concatenate(parts, axis=0)
     k_rows = qkv[:, HL:2 * HL].astype(BF16)
     q = (qkv[:, 0:HL] * SCALE).T.astype(BF16)
@@ -160,20 +200,37 @@
     )(*args)
 
 
-def decode_body(came, weights, cot, mask, gain, table, recon, dvis, mixed, grad, w_oe, w_fc, cots, sems):
+def load_body(weights, cot, w_oe, w_fc, dact, sems):
     loads = [
         pltpu.make_async_copy(
             weights.at[pl.ds(2 * i, 2), pl.ds(0, 2 * HID)], w_fc.at[pl.ds(2 * i, 2)], sems.at[i])
         for i in range(8)]
     oe = pltpu.make_async_copy(weights.at[:, pl.ds(2 * HID, HP)], w_oe, sems.at[8])
-    up = pltpu.make_async_copy(cot, cots, sems.at[9])
-    for load in (oe, up, loads[0]):
-        load.start()
+    for copy in (*loads, oe):
+        copy.start()
+    for i in range(8):
+        loads[i].wait()
+        fout = jnp.concatenate([w_fc[2 * i, HID:2 * HID, :], w_fc[2 * i + 1, HID:2 * HID, :]], axis=0)
+        dact[:, 2 * HID * i:2 * HID * (i + 1)] = dot_nt(cot[...], fout)
+    oe.wait()
+
+
+def load(weights, cot):
+    vmem = pl.BlockSpec(memory_space=pltpu.VMEM)
+    return pl.pallas_call(
+        load_body,
+        out_shape=[pltpu.VMEM((16, HP, DD), BF16), pltpu.VMEM((16, 2 * HID, DD), BF16), pltpu.VMEM((FDEV, 16 * HID), F32)],
+        in_specs=[pl.BlockSpec(memory_space=pltpu.HBM), vmem],
+        out_specs=[vmem] * 3,
+        scratch_shapes=[pltpu.SemaphoreType.DMA((9,))],
+        compiler_params=pltpu.CompilerParams(vmem_limit_bytes=24 << 20),
+        cost_estimate=pl.CostEstimate(flops=540 << 20, bytes_accessed=8 << 20, transcendentals=0),
+    )(pltpu.with_memory_space_constraint(weights, pltpu.HBM), cot)
+
+
+def decode_body(came, w_oe, w_fc, dact_in, cot, mask, gain, table, recon, dvis, mixed, grad):
     flat = came[...].reshape(16 * 64, 128)
     vis = jnp.zeros((CAP, DD), F32)
-    oe.wait()
-    for load in loads[1:]:
-        load.start()
     for g in range(16):
         vis += dot(came[g, 0:CAP, 0:HP], w_oe[g])
     row = lax.broadcasted_iota(jnp.int32, (CAP, 1024), 0)
@@ -203,15 +260,13 @@
     inv_std = lax.rsqrt(var + 1e-06)
     normed = centred * inv_std
     dn = (normed * gain[...]).astype(BF16)
-    up.wait()
-    cot_b = cots[...]
+    cot_b = cot[...]
     mixed[...] = dec_x
     for i in range(8):
-        loads[i].wait()
         fin = jnp.concatenate([w_fc[2 * i, 0:HID, :], w_fc[2 * i + 1, 0:HID, :]], axis=0)
         fout = jnp.concatenate([w_fc[2 * i, HID:2 * HID, :], w_fc[2 * i + 1, HID:2 * HID, :]], axis=0)
         hidden = dot_nt(dn, fin)
-        dact = dot_nt(cot_b, fout)
+        dact = dact_in[:, 2 * HID * i:2 * HID * (i + 1)]
         cdf = 0.5 * (1.0 + lax.erf(hidden * 0.7071067811865476))
         pdf = jnp.exp(-0.5 * hidden * hidden) * 0.3989422804014327
         act = (hidden * cdf).astype(BF16)
@@ -229,21 +284,10 @@
     dvis[...] = dot(picker[0:CAP].astype(BF16), ddec).astype(BF16)
 
 
-def decode(came, weights, cot, *args):
-    vmem = pl.BlockSpec(memory_space=pltpu.VMEM)
-    hbm = pl.BlockSpec(memory_space=pltpu.HBM)
-    return pl.pallas_call(
-        decode_body,
-        out_shape=[jax.ShapeDtypeStruct((FDEV, DD), BF16), jax.ShapeDtypeStruct((CAP, DD), BF16)],
-        in_specs=[vmem, hbm, hbm] + [vmem] * len(args),
-        out_specs=[vmem, vmem],
-        scratch_shapes=[pltpu.VMEM((FDEV, DD), F32), pltpu.VMEM((FDEV, DD), F32),
-                        pltpu.VMEM((16, HP, DD), BF16), pltpu.VMEM((16, 2 * HID, DD), BF16),
-                        pltpu.VMEM((FDEV, DD), BF16), pltpu.SemaphoreType.DMA((10,))],
-        compiler_params=pltpu.CompilerParams(vmem_limit_bytes=24 << 20),
-        cost_estimate=pl.CostEstimate(flops=2300 << 20, bytes_accessed=8 << 20, transcendentals=1 << 20),
-    )(came, pltpu.with_memory_space_constraint(weights, pltpu.HBM),
-      pltpu.with_memory_space_constraint(cot, pltpu.HBM), *args)
+def decode(*args):
+    return call(
+        decode_body, [((FDEV, DD), BF16), ((CAP, DD), BF16)],
+        [pltpu.VMEM((FDEV, DD), F32), pltpu.VMEM((FDEV, DD), F32)], 1800 << 20, 24, *args)
 
 
 def back_body(dvis, w_oe, swap, saved, stats, mine, other, parts, ds_all, pb_all, keep, keep_stats, xs, sems):
@@ -353,7 +397,7 @@
         got[step % NZ] = z_shift(block, step)
     got[3] = z_shift(got[2], 1)
     got[5] = z_shift(got[6], -1)
-    got[4] = z_shift(got[2], 2)
+    got[4] = z_shift(got[6], -2)
     return [got[k] for k in range(NZ)]
 
 
@@ -382,17 +426,13 @@
     cap = keep_pos.shape[1]
     rows = 16 * cap
 
-    xn_own, x_slot, offsets = prep(keep_pos, patches[0], enc_gain[None])
-    mine = join(around(xn_own))
-    other = swap_core(mine)
-
-    x_vis = dot(x_slot, w_e2d).astype(BF16)
+    xn_own, x_vis, offsets, w_oe_own, pack = prep(
+        keep_pos, enc_gain[None], patches[0], w_out, w_e2d, fc_in, fc_out)
+    weights = lax.all_gather(pack, "seq", axis=0)
+
     places = jnp.pad(offsets[:, 0].reshape(16, 1, SLOTS), ((0, 0), (0, 0), (0, 128 - SLOTS)))
     extra = jnp.concatenate(
         [x_vis.reshape(16, 12, 128), places, jnp.zeros((16, 3, 128), BF16)], axis=1)
-
-    w_oe_own = jnp.pad(dot(w_out, w_e2d).astype(BF16), ((0, HP - HD), (0, 0)))
-    weights = lax.all_gather(jnp.concatenate([fc_in, fc_out, w_oe_own], axis=0), "seq", axis=0)
 
     tok = jnp.arange(rows, dtype=jnp.int32)
     block = tok // cap
@@ -402,10 +442,16 @@
     swap = (dest[None, :] == tok[:, None]).astype(BF16)
     table = position_table((me * fdev + jnp.arange(fdev, dtype=jnp.int32)).astype(F32), DD)
 
-    w = jnp.pad(w_qkv.transpose(0, 2, 1), ((0, 0), (0, HL - HD), (0, 0))).reshape(3 * HL, -1)
+    w = turn(w_qkv.transpose(0, 2, 1).reshape(3 * HD, -1))
+    blocks = around(xn_own)
+    blocks[4], w, swap, extra, table = lax.optimization_barrier((blocks[4], w, swap, extra, table))
+    mine = join(blocks)
+    other = swap_core(mine)
     sent, saved, stats = attend(mine, other, w, swap, extra)
     came = lax.all_to_all(sent, "seq", 0, 0, tiled=True)
-    recon, dvis_own = decode(came, weights, cot, mask_token[None], dec_gain[None], table)
+    weights, stats = lax.optimization_barrier((weights, stats))
+    w_oe, w_fc, dact = load(weights, cot)
+    recon, dvis_own = decode(came, w_oe, w_fc, dact, cot, mask_token[None], dec_gain[None], table)
     dvis = lax.all_gather(dvis_own, "seq", axis=0, tiled=True)
     parts = back(dvis, w_oe_own, swap, saved, stats, mine, other)
 

time: 181 us -> 179 us (0.989)
  waiting for transfers between devices: 20.5 us -> 13.6 us
  local copies, waits for them, and re-layouts: 3.82 us -> 8.63 us
  matrix products: 2.06 us -> 0 us
    all_to_all x1, waiting for transfers between devices: 8.66 us -> 0.01 us  [local(): came = lax.all_to_all(sent, 'seq', 0, 0, tiled=True)]
    unnamed x26 -> x36, local copies, waits for them, and re-layouts: 2.15 us -> 7.43 us
    pallas_call x2 -> x3, Pallas kernels: 2 us -> 6.8 us  [call(): pl.pallas_call(body, out_shape=[jax.ShapeDtypeStruct(shape, dtype) for sh...]
    ppermute x7, waiting for transfers between devices: 11.2 us -> 7.95 us  [z_shift(): lax.ppermute(block, 'seq', [(s, (s + 2 * step) % 16) for s in range(16)])]
    all_gather x1, waiting for transfers between devices: 0.01 us -> 2.94 us  [local(): weights = lax.all_gather(pack, 'seq', axis=0)]
    ppermute x1, waiting for transfers between devices: 0.56 us -> 2.67 us  [swap_core(): return lax.ppermute(block, 'seq', [(s, s ^ 1) for s in range(16)])]
    dot_general x2 -> x0, matrix products: 2.06 us -> none  [dot(): return jnp.dot(a, b, preferred_element_type=F32)]
    pallas_call x1 -> x2, Pallas kernels: 8.25 us -> 6.47 us  [the longest x1 3.67 us: load(): pl.pallas_call(load_body, out_shape=[pltpu.VMEM((16, HP, DD), BF16), pltp...]
  transfers between devices with their start and end apart: 10 -> 10, of which waited for: 4 -> 4; matrix products, arithmetic and copies ran while one was open for 2% -> 1% of each run, Pallas kernels for 4% -> 6%
where the time goes in v3:
time: 179 us; the launch traced here: 178 us
  blocking collectives  77.8 us (43%)
  starting transfers between devices  37.7 us (21%)
  Pallas kernels  23.9 us (13%)
  between operations  14.4 us (8%)
  waiting for transfers between devices  13.6 us (8%)
  local copies, waits for them, and re-layouts  8.63 us (5%)
  other arithmetic  1.81 us (1%)
    all_to_all x4, blocking collectives, exchange(): lax.all_to_all(block, axis, 0, 0, axis_index_groups=groups, tiled=True)  59.6 us
    ppermute x7, starting transfers between devices, z_shift(): lax.ppermute(block, 'seq', [(s, (s + 2 * step) % 16) for s in range(16)])  29.8 us
    all_gather x1, blocking collectives, local(): dvis = lax.all_gather(dvis_own, 'seq', axis=0, tiled=True)  18.2 us
    ppermute x7, waiting for transfers between devices, z_shift(): lax.ppermute(block, 'seq', [(s, (s + 2 * step) % 16) for s in range(16)])  7.95 us
    unnamed x36, local copies, waits for them, and re-layouts  7.43 us
    pallas_call x3, Pallas kernels, call(): pl.pallas_call(body, out_shape=[jax.ShapeDtypeStruct(shape, dtype) for sh...  6.8 us
    all_to_all x1, starting transfers between devices, local(): came = lax.all_to_all(sent, 'seq', 0, 0, tiled=True)  5.83 us
    pallas_call x1, Pallas kernels, attend(): pl.pallas_call(attend_body, out_shape=[pltpu.HBM((16, 64, 128), BF16), pl...  5.06 us
  transfers between devices with their start and end apart: 10, of which 4 were waited for; matrix products, arithmetic and copies ran while one was open for 1% of the time, Pallas kernels for 6%

profile of v3, /device:TPU:64, one launch (start us, length us, event | category | flops | bytes accessed | tf_op | source)
XLA Modules:
  0.0 177.9 jit_solution(8771869185860553530)
XLA Ops:
  7.2 0.0 all-gather.3.cloned.1.call-start
  7.2 0.7 broadcast_in_dim.32.gain
  7.9 0.7 copy-done.11
  8.6 2.8 %shard_map.130 = (bf16[48,1408]{1,0:T(8,128)(2,1)S(1)}, bf16[48,512]{1,0:T(8,128)(2,1)S(1)}, bf16[48,128]{1,0:T(8,128)(2,1)S(1)}, bf16[96,512]{1,0:T(8,128)(2,1)S(1)}, bf16[352,512]{1,0:T(8,128)(2,1)}) custom-call(s32[1,48]{1,0:T(1,128)S(1)} %copy-done.11, f32[1,1408]{1,0:T(1,128)S(1)} %broadcast_in_dim.32.gain, bf16[48,1408]{1,0:T(8,128)(2,1)} %bitcast.24, ...), custom_call_target="tpu_custom_call" | custom-call | flops 209715200 | bytes 3145728 | tf_op jit(solution)/shard_map/pallas_call | solution.py:96
  11.4 0.0 copy-start.14
  11.4 0.0 all-gather.3.cloned.1.call-update
  11.4 10.2 %collective-permute-start.3 = (bf16[48,1408]{1,0:T(8,128)(2,1)S(1)}, bf16[48,1408]{1,0:T(8,128)(2,1)S(1)}, u32[]{:S(2)}, u32[]{:S(2)}) collective-permute-start(bf16[48,1408]{1,0:T(8,128)(2,1)S(1)} %get-tuple-element.25.refs_0_), channel_id=1, source_target_pairs={{0,12},{1,13},{2,14},{3,15},{4,0},{5,1},{6,2},{7,3},{8,4},{9,5},{1... | collective-permute-start | bytes 405512 | tf_op jit(solution)/shard_map/ppermute | solution.py:391
  21.6 1.9 %collective-permute-start.1 = (bf16[48,1408]{1,0:T(8,128)(2,1)S(1)}, bf16[48,1408]{1,0:T(8,128)(2,1)S(1)}, u32[]{:S(2)}, u32[]{:S(2)}) collective-permute-start(bf16[48,1408]{1,0:T(8,128)(2,1)S(1)} %get-tuple-element.25.refs_0_), channel_id=1, source_target_pairs={{0,4},{1,5},{2,6},{3,7},{4,8},{5,9},{6,10},{7,11},{8,12},{9,13},{1... | collective-permute-start | bytes 405512 | tf_op jit(solution)/shard_map/ppermute | solution.py:391
  23.5 1.9 %collective-permute-start = (bf16[48,1408]{1,0:T(8,128)(2,1)S(1)}, bf16[48,1408]{1,0:T(8,128)(2,1)S(1)}, u32[]{:S(2)}, u32[]{:S(2)}) collective-permute-start(bf16[48,1408]{1,0:T(8,128)(2,1)S(1)} %get-tuple-element.25.refs_0_), channel_id=1, source_target_pairs={{0,2},{1,3},{2,4},{3,5},{4,6},{5,7},{6,8},{7,9},{8,10},{9,11},{10,... | collective-permute-start | bytes 405512 | tf_op jit(solution)/shard_map/ppermute | solution.py:391
  25.4 3.9 %collective-permute-start.6 = (bf16[48,1408]{1,0:T(8,128)(2,1)S(1)}, bf16[48,1408]{1,0:T(8,128)(2,1)S(1)}, u32[]{:S(2)}, u32[]{:S(2)}) collective-permute-start(bf16[48,1408]{1,0:T(8,128)(2,1)S(1)} %get-tuple-element.25.refs_0_), channel_id=1, source_target_pairs={{0,14},{1,15},{2,0},{3,1},{4,2},{5,3},{6,4},{7,5},{8,6},{9,7},{10,... | collective-permute-start | bytes 405512 | tf_op jit(solution)/shard_map/ppermute | solution.py:391
  29.4 0.1 reshape.112
  29.5 0.1 slice_reduce_fusion
  29.6 0.1 reshape_squeeze.4
  29.7 0.1 pad.9.clone
  29.8 0.4 fusion.swap
  30.3 0.0 copy-start.5
  30.3 1.0 multiply_sine_fusion
  31.3 0.0 collective-permute-done.3.refs_6_
  31.3 6.0 %collective-permute-start.4 = (bf16[48,1408]{1,0:T(8,128)(2,1)S(1)}, bf16[48,1408]{1,0:T(8,128)(2,1)S(1)}, u32[]{:S(2)}, u32[]{:S(2)}) collective-permute-start(bf16[48,1408]{1,0:T(8,128)(2,1)S(1)} %collective-permute-done.3.refs_6_), channel_id=1, source_target_pairs={{0,12},{1,13},{2,14},{3,15},{4,0},{5,1},{6,2},{7,3},{8,4},{9,5},{1... | collective-permute-start | bytes 405512 | tf_op jit(solution)/shard_map/ppermute | solution.py:391
  37.3 2.5 %collective-permute-start.5 = (bf16[48,1408]{1,0:T(8,128)(2,1)S(1)}, bf16[48,1408]{1,0:T(8,128)(2,1)S(1)}, u32[]{:S(2)}, u32[]{:S(2)}) collective-permute-start(bf16[48,1408]{1,0:T(8,128)(2,1)S(1)} %collective-permute-done.3.refs_6_), channel_id=1, source_target_pairs={{0,14},{1,15},{2,0},{3,1},{4,2},{5,3},{6,4},{7,5},{8,6},{9,7},{10,... | collective-permute-start | bytes 405512 | tf_op jit(solution)/shard_map/ppermute | solution.py:391
  39.8 0.0 collective-permute-done.1.refs_2_
  39.8 3.4 %collective-permute-start.2 = (bf16[48,1408]{1,0:T(8,128)(2,1)S(1)}, bf16[48,1408]{1,0:T(8,128)(2,1)S(1)}, u32[]{:S(2)}, u32[]{:S(2)}) collective-permute-start(bf16[48,1408]{1,0:T(8,128)(2,1)S(1)} %collective-permute-done.1.refs_2_), channel_id=1, source_target_pairs={{0,2},{1,3},{2,4},{3,5},{4,6},{5,7},{6,8},{7,9},{8,10},{9,11},{10,... | collective-permute-start | bytes 405512 | tf_op jit(solution)/shard_map/ppermute | solution.py:391
  43.2 0.1 fusion.4.extra
  43.3 0.0 copy-done.14
  43.3 0.4 shard_map.131.w
  43.7 0.1 pad_maximum_fusion.table
  43.7 2.7 %collective-permute-done.4.refs_4_ = bf16[48,1408]{1,0:T(8,128)(2,1)S(1)} collective-permute-done((bf16[48,1408]{1,0:T(8,128)(2,1)S(1)}, bf16[48,1408]{1,0:T(8,128)(2,1)S(1)}, u32[]{:S(2)}, u32[]{:S(2)}) %collective-permute-start.4) | collective-permute-done | bytes 135200 | tf_op jit(solution)/shard_map/ppermute | solution.py:391
  46.5 0.0 collective-permute-done.refs_1_
  46.5 0.0 collective-permute-done.6.refs_7_
  46.5 5.2 %collective-permute-done.5.refs_5_ = bf16[48,1408]{1,0:T(8,128)(2,1)S(1)} collective-permute-done((bf16[48,1408]{1,0:T(8,128)(2,1)S(1)}, bf16[48,1408]{1,0:T(8,128)(2,1)S(1)}, u32[]{:S(2)}, u32[]{:S(2)}) %collective-permute-start.5) | collective-permute-done | bytes 135200 | tf_op jit(solution)/shard_map/ppermute | solution.py:391
  51.7 0.0 collective-permute-done.2.refs_3_
  51.7 1.5 shard_map.132.mine
  53.1 0.0 copy-start.7
  53.1 0.0 copy-start.17
  53.2 0.0 copy-start.9
  53.2 2.1 %collective-permute-start.7 = (bf16[384,1408]{1,0:T(8,128)(2,1)S(1)}, bf16[384,1408]{1,0:T(8,128)(2,1)S(1)}, u32[]{:S(2)}, u32[]{:S(2)}) collective-permute-start(bf16[384,1408]{1,0:T(8,128)(2,1)S(1)} %shard_map.132.mine), channel_id=1, source_target_pairs={{0,1},{1,0},{2,3},{3,2},{4,5},{5,4},{6,7},{7,6},{8,9},{9,8},{10,11... | collective-permute-start | bytes 3244040 | tf_op jit(solution)/shard_map/ppermute | solution.py:405
  55.2 2.7 %collective-permute-done.7.other = bf16[384,1408]{1,0:T(8,128)(2,1)S(1)} collective-permute-done((bf16[384,1408]{1,0:T(8,128)(2,1)S(1)}, bf16[384,1408]{1,0:T(8,128)(2,1)S(1)}, u32[]{:S(2)}, u32[]{:S(2)}) %collective-permute-start.7) | collective-permute-done | bytes 1081376 | tf_op jit(solution)/shard_map/ppermute | solution.py:405
  57.9 0.0 copy-done.5
  57.9 5.1 %shard_map.133 = (bf16[16,64,128]{2,1,0:T(8,128)(2,1)}, bf16[512,768]{1,0:T(8,128)(2,1)}, f32[8,768]{1,0:T(8,128)}) custom-call(bf16[384,1408]{1,0:T(8,128)(2,1)S(1)} %shard_map.132.mine, bf16[384,1408]{1,0:T(8,128)(2,1)S(1)} %collective-permute-done.7.other, bf16[1408,384]{1,0:T(8,128)(2,1)S(1)} %shard_map.131.w, bf16[768,768]{1,0:T(8,128)(2,1)S(1)} %fusion.swap, ...), custom_call_target="tpu_custom_call" | custom-call | flops 1782579200 | bytes 8388608 | tf_op jit(solution)/shard_map/pallas_call | solution.py:191
  63.0 0.0 copy-done.7
  63.0 0.0 copy-done.12
  63.0 5.8 %all-to-all-start = ((bf16[16,64,128]{2,1,0:T(8,128)(2,1)}), bf16[16,64,128]{2,1,0:T(8,128)(2,1)S(1)}, u32[]{:S(2)}, u32[]{:S(2)}) async-start(bf16[16,64,128]{2,1,0:T(8,128)(2,1)} %get-tuple-element.32), calls=%async_computation | async-start | bytes 524288 | tf_op jit(solution)/shard_map/all_to_all | solution.py:451
  68.8 2.9 %all-gather.3.cloned.1.call-done = bf16[5632,512]{1,0:T(8,128)(2,1)} async-done(((bf16[352,512]{1,0:T(8,128)(2,1)}), bf16[5632,512]{1,0:T(8,128)(2,1)}) %all-gather.3.cloned.1.call-update) | async-done | bytes 5767184 | tf_op jit(solution)/shard_map/all_gather | solution.py:431
  71.8 3.7 %shard_map.134 = (bf16[16,96,512]{2,1,0:T(8,128)(2,1)S(1)}, bf16[16,256,512]{2,1,0:T(8,128)(2,1)S(1)}, f32[256,2048]{1,0:T(8,128)S(1)}) custom-call(bf16[16,352,512]{2,1,0:T(8,128)(2,1)} %bitcast.21, bf16[256,512]{1,0:T(8,128)(2,1)S(1)} %bitcast.16), custom_call_target="tpu_custom_call" | custom-call | flops 566231040 | bytes 8388608 | tf_op jit(solution)/shard_map/pallas_call | solution.py:220
  75.5 1.9 %copy-done.1 = bf16[16,256,512]{2,1,0:T(8,128)(2,1)} copy-done((bf16[16,256,512]{2,1,0:T(8,128)(2,1)}, bf16[16,256,512]{2,1,0:T(8,128)(2,1)S(1)}, u32[]{:S(2)}) %copy-start.1) | copy-done | bytes 4194328
  77.4 1.2 copy-done.3
  78.6 0.0 all-to-all-done.came
  78.6 2.2 %copy-done.2 = bf16[16,256,512]{2,1,0:T(8,128)(2,1)S(1)} copy-done((bf16[16,256,512]{2,1,0:T(8,128)(2,1)S(1)}, bf16[16,256,512]{2,1,0:T(8,128)(2,1)}, u32[]{:S(2)}) %copy-start.2) | copy-done | bytes 4194328
  80.8 1.4 copy-done.4
  82.2 0.0 copy-start.16
  82.2 4.9 %shard_map.135 = (bf16[256,512]{1,0:T(8,128)(2,1)}, bf16[48,512]{1,0:T(8,128)(2,1)S(1)}) custom-call(bf16[16,64,128]{2,1,0:T(8,128)(2,1)S(1)} %all-to-all-done.came, bf16[16,96,512]{2,1,0:T(8,128)(2,1)S(1)} %copy-done.4, bf16[16,256,512]{2,1,0:T(8,128)(2,1)S(1)} %copy-done.2, f32[256,2048]{1,0:T(8,128)S(1)} %get-tuple-element.38.dact_in, ...), custom_call_target="tpu_custom_call" | custom-call | flops 1887436800 | bytes 8388608 | tf_op jit(solution)/shard_map/pallas_call | solution.py:43
  87.1 18.2 %all_gather.11.dvis = bf16[768,512]{1,0:T(8,128)(2,1)S(1)} all-gather(bf16[48,512]{1,0:T(8,128)(2,1)S(1)} %get-tuple-element.41), channel_id=1, replica_groups=mesh['dp'=32,'seq'=16] {'seq'}, dimensions={0}, use_global_device_ids=true | all-gather | bytes 835584 | tf_op jit(solution)/shard_map/all_gather | solution.py:455
  105.3 0.0 copy-done.8
  105.3 0.0 copy-done.15
  105.3 4.1 %shard_map.136 = bf16[3328,128]{1,0:T(8,128)(2,1)S(1)} custom-call(bf16[768,512]{1,0:T(8,128)(2,1)S(1)} %all_gather.11.dvis, bf16[96,512]{1,0:T(8,128)(2,1)S(1)} %get-tuple-element.42.w_oe, bf16[768,768]{1,0:T(8,128)(2,1)S(1)} %copy-done.6, bf16[512,768]{1,0:T(8,128)(2,1)S(1)} %copy-done.15, f32[8,768]{1,0:T(8,128)S(1)} %copy-done.16, ...), custom_call_target="tpu_custom_call" | custom-call | flops 2621440000 | bytes 8388608 | tf_op jit(solution)/shard_map/pallas_call | solution.py:338
  109.5 17.6 %all_to_all.25 = bf16[4,832,128]{2,1,0:T(8,128)(2,1)S(1)} all-to-all(bf16[4,832,128]{2,1,0:T(8,128)(2,1)S(1)} %bitcast.18), channel_id=1, replica_groups={{0,16,32,48},{64,80,96,112},{128,144,160,176},{192,208,224,240},{256,27..., dimensions={0} | all-to-all | bytes 1703936 | tf_op jit(solution)/shard_map/all_to_all | solution.py:381
  127.1 0.2 reduce_sum.24
  127.3 17.3 %all_to_all.26 = bf16[8,104,128]{2,1,0:T(8,128)(2,1)S(1)} all-to-all(bf16[8,104,128]{2,1,0:T(8,128)(2,1)S(1)} %bitcast.22), channel_id=1, replica_groups={{0,64,128,192,256,320,384,448},{16,80,144,208,272,336,400,464},{32,96,1..., dimensions={0} | all-to-all | bytes 425984 | tf_op jit(solution)/shard_map/all_to_all | solution.py:381
  144.7 0.0 copy-start
  144.7 12.5 %all_to_all.27 = bf16[8,104,128]{2,1,0:T(8,128)(2,1)S(1)} all-to-all(bf16[8,104,128]{2,1,0:T(8,128)(2,1)S(1)} %broadcast_in_dim.37), channel_id=1, replica_groups={{0,64,128,192,256,320,384,448},{16,80,144,208,272,336,400,464},{32,96,1..., dimensions={0} | all-to-all | bytes 425984 | tf_op jit(solution)/shard_map/all_to_all | solution.py:381
  157.2 0.1 broadcast_in_dim.39
  157.3 12.2 %all_to_all.28 = bf16[4,832,128]{2,1,0:T(8,128)(2,1)S(1)} all-to-all(bf16[4,832,128]{2,1,0:T(8,128)(2,1)S(1)} %broadcast_in_dim.39), channel_id=1, replica_groups={{0,16,32,48},{64,80,96,112},{128,144,160,176},{192,208,224,240},{256,27..., dimensions={0} | all-to-all | bytes 1703936 | tf_op jit(solution)/shard_map/all_to_all | solution.py:381
  169.5 0.0 copy-done
  169.5 1.5 shard_map.137
  (24 shorter events, 0.1 us)
Async XLA Ops:
  7.2 64.6 %all-gather.3.cloned.1.call-start = ((), (), s32[]{:S(2)}) async-start(), calls=%async_computation.5 | async-start | bytes 6127616 | tf_op jit(solution)/shard_map/all_gather | solution.py:431
  7.9 0.7 copy-start.11
  11.4 31.9 %copy-start.14 = (bf16[3,1408,88]{1,2,0:T(8,128)(2,1)S(1)}, bf16[3,1408,88]{1,2,0:T(8,128)(2,1)}, u32[]{:S(2)}) copy-start(bf16[3,1408,88]{1,2,0:T(8,128)(2,1)} %param.15) | copy-start | bytes 2230276
  11.4 19.9 %collective-permute-start.3 = (bf16[48,1408]{1,0:T(8,128)(2,1)S(1)}, bf16[48,1408]{1,0:T(8,128)(2,1)S(1)}, u32[]{:S(2)}, u32[]{:S(2)}) collective-permute-start(bf16[48,1408]{1,0:T(8,128)(2,1)S(1)} %get-tuple-element.25.refs_0_), channel_id=1, source_target_pairs={{0,12},{1,13},{2,14},{3,15},{4,0},{5,1},{6,2},{7,3},{8,4},{9,5},{1... | collective-permute-start | bytes 405512 | tf_op jit(solution)/shard_map/ppermute | solution.py:391
  21.6 18.2 %collective-permute-start.1 = (bf16[48,1408]{1,0:T(8,128)(2,1)S(1)}, bf16[48,1408]{1,0:T(8,128)(2,1)S(1)}, u32[]{:S(2)}, u32[]{:S(2)}) collective-permute-start(bf16[48,1408]{1,0:T(8,128)(2,1)S(1)} %get-tuple-element.25.refs_0_), channel_id=1, source_target_pairs={{0,4},{1,5},{2,6},{3,7},{4,8},{5,9},{6,10},{7,11},{8,12},{9,13},{1... | collective-permute-start | bytes 405512 | tf_op jit(solution)/shard_map/ppermute | solution.py:391
  23.5 22.9 %collective-permute-start = (bf16[48,1408]{1,0:T(8,128)(2,1)S(1)}, bf16[48,1408]{1,0:T(8,128)(2,1)S(1)}, u32[]{:S(2)}, u32[]{:S(2)}) collective-permute-start(bf16[48,1408]{1,0:T(8,128)(2,1)S(1)} %get-tuple-element.25.refs_0_), channel_id=1, source_target_pairs={{0,2},{1,3},{2,4},{3,5},{4,6},{5,7},{6,8},{7,9},{8,10},{9,11},{10,... | collective-permute-start | bytes 405512 | tf_op jit(solution)/shard_map/ppermute | solution.py:391
  25.4 21.0 %collective-permute-start.6 = (bf16[48,1408]{1,0:T(8,128)(2,1)S(1)}, bf16[48,1408]{1,0:T(8,128)(2,1)S(1)}, u32[]{:S(2)}, u32[]{:S(2)}) collective-permute-start(bf16[48,1408]{1,0:T(8,128)(2,1)S(1)} %get-tuple-element.25.refs_0_), channel_id=1, source_target_pairs={{0,14},{1,15},{2,0},{3,1},{4,2},{5,3},{6,4},{7,5},{8,6},{9,7},{10,... | collective-permute-start | bytes 405512 | tf_op jit(solution)/shard_map/ppermute | solution.py:391
  30.3 27.6 %copy-start.5 = (bf16[768,768]{1,0:T(8,128)(2,1)}, bf16[768,768]{1,0:T(8,128)(2,1)S(1)}, u32[]{:S(2)}) copy-start(bf16[768,768]{1,0:T(8,128)(2,1)S(1)} %fusion.swap) | copy-start | bytes 3538948
  31.3 15.2 %collective-permute-start.4 = (bf16[48,1408]{1,0:T(8,128)(2,1)S(1)}, bf16[48,1408]{1,0:T(8,128)(2,1)S(1)}, u32[]{:S(2)}, u32[]{:S(2)}) collective-permute-start(bf16[48,1408]{1,0:T(8,128)(2,1)S(1)} %collective-permute-done.3.refs_6_), channel_id=1, source_target_pairs={{0,12},{1,13},{2,14},{3,15},{4,0},{5,1},{6,2},{7,3},{8,4},{9,5},{1... | collective-permute-start | bytes 405512 | tf_op jit(solution)/shard_map/ppermute | solution.py:391
  37.3 14.4 %collective-permute-start.5 = (bf16[48,1408]{1,0:T(8,128)(2,1)S(1)}, bf16[48,1408]{1,0:T(8,128)(2,1)S(1)}, u32[]{:S(2)}, u32[]{:S(2)}) collective-permute-start(bf16[48,1408]{1,0:T(8,128)(2,1)S(1)} %collective-permute-done.3.refs_6_), channel_id=1, source_target_pairs={{0,14},{1,15},{2,0},{3,1},{4,2},{5,3},{6,4},{7,5},{8,6},{9,7},{10,... | collective-permute-start | bytes 405512 | tf_op jit(solution)/shard_map/ppermute | solution.py:391
  39.8 11.9 %collective-permute-start.2 = (bf16[48,1408]{1,0:T(8,128)(2,1)S(1)}, bf16[48,1408]{1,0:T(8,128)(2,1)S(1)}, u32[]{:S(2)}, u32[]{:S(2)}) collective-permute-start(bf16[48,1408]{1,0:T(8,128)(2,1)S(1)} %collective-permute-done.1.refs_2_), channel_id=1, source_target_pairs={{0,2},{1,3},{2,4},{3,5},{4,6},{5,7},{6,8},{7,9},{8,10},{9,11},{10,... | collective-permute-start | bytes 405512 | tf_op jit(solution)/shard_map/ppermute | solution.py:391
  53.1 9.8 %copy-start.7 = (bf16[384,1408]{1,0:T(8,128)(2,1)}, bf16[384,1408]{1,0:T(8,128)(2,1)S(1)}, u32[]{:S(2)}) copy-start(bf16[384,1408]{1,0:T(8,128)(2,1)S(1)} %shard_map.132.mine) | copy-start | bytes 3244036
  53.1 15.7 %copy-start.17 = (bf16[512]{0:T(512)(128)(2,1)S(1)}, bf16[512]{0:T(512)(128)(2,1)}, u32[]{:S(2)}) copy-start(bf16[512]{0:T(512)(128)(2,1)} %param.18) | copy-start | bytes 3076
  53.2 18.6 %copy-start.9 = (bf16[1,256,512]{2,1,0:T(8,128)(2,1)S(1)}, bf16[1,256,512]{2,1,0:T(8,128)(2,1)}, u32[]{:S(2)}) copy-start(bf16[1,256,512]{2,1,0:T(8,128)(2,1)} %param.22) | copy-start | bytes 786436
  53.2 4.7 %collective-permute-start.7 = (bf16[384,1408]{1,0:T(8,128)(2,1)S(1)}, bf16[384,1408]{1,0:T(8,128)(2,1)S(1)}, u32[]{:S(2)}, u32[]{:S(2)}) collective-permute-start(bf16[384,1408]{1,0:T(8,128)(2,1)S(1)} %shard_map.132.mine), channel_id=1, source_target_pairs={{0,1},{1,0},{2,3},{3,2},{4,5},{5,4},{6,7},{7,6},{8,9},{9,8},{10,11... | collective-permute-start | bytes 3244040 | tf_op jit(solution)/shard_map/ppermute | solution.py:405
  57.9 5.1 %copy-start.12 = (bf16[384,1408]{1,0:T(8,128)(2,1)}, bf16[384,1408]{1,0:T(8,128)(2,1)S(1)}, u32[]{:S(2)}) copy-start(bf16[384,1408]{1,0:T(8,128)(2,1)S(1)} %collective-permute-done.7.other) | copy-start | bytes 3244036
  63.0 15.6 %all-to-all-start = ((bf16[16,64,128]{2,1,0:T(8,128)(2,1)}), bf16[16,64,128]{2,1,0:T(8,128)(2,1)S(1)}, u32[]{:S(2)}, u32[]{:S(2)}) async-start(bf16[16,64,128]{2,1,0:T(8,128)(2,1)} %get-tuple-element.32), calls=%async_computation | async-start | bytes 524288 | tf_op jit(solution)/shard_map/all_to_all | solution.py:451
  71.8 6.8 %copy-start.10 = (f32[512]{0:T(512)S(1)}, f32[512]{0:T(512)}, u32[]{:S(2)}) copy-start(f32[512]{0:T(512)} %param.19) | copy-start | bytes 6148
  75.5 1.9 %copy-start.1 = (bf16[16,256,512]{2,1,0:T(8,128)(2,1)}, bf16[16,256,512]{2,1,0:T(8,128)(2,1)S(1)}, u32[]{:S(2)}) copy-start(bf16[16,256,512]{2,1,0:T(8,128)(2,1)S(1)} %get-tuple-element.37.w_fc) | copy-start | bytes 12582916
  77.4 1.2 copy-start.3
  78.6 2.2 %copy-start.2 = (bf16[16,256,512]{2,1,0:T(8,128)(2,1)S(1)}, bf16[16,256,512]{2,1,0:T(8,128)(2,1)}, u32[]{:S(2)}) copy-start(bf16[16,256,512]{2,1,0:T(8,128)(2,1)} %copy-done.1) | copy-start | bytes 12582916
  80.8 1.4 copy-start.4
  82.2 23.1 %copy-start.6 = (bf16[768,768]{1,0:T(8,128)(2,1)S(1)}, bf16[768,768]{1,0:T(8,128)(2,1)}, u32[]{:S(2)}) copy-start(bf16[768,768]{1,0:T(8,128)(2,1)} %copy-done.5) | copy-start | bytes 3538948
  82.2 23.1 %copy-start.8 = (bf16[384,1408]{1,0:T(8,128)(2,1)S(1)}, bf16[384,1408]{1,0:T(8,128)(2,1)}, u32[]{:S(2)}) copy-start(bf16[384,1408]{1,0:T(8,128)(2,1)} %copy-done.7) | copy-start | bytes 3244036
  82.2 23.1 %copy-start.13 = (bf16[384,1408]{1,0:T(8,128)(2,1)S(1)}, bf16[384,1408]{1,0:T(8,128)(2,1)}, u32[]{:S(2)}) copy-start(bf16[384,1408]{1,0:T(8,128)(2,1)} %copy-done.12) | copy-start | bytes 3244036
  82.2 23.1 %copy-start.15 = (bf16[512,768]{1,0:T(8,128)(2,1)S(1)}, bf16[512,768]{1,0:T(8,128)(2,1)}, u32[]{:S(2)}) copy-start(bf16[512,768]{1,0:T(8,128)(2,1)} %get-tuple-element.43.saved) | copy-start | bytes 2359300
  82.2 23.1 %copy-start.16 = (f32[8,768]{1,0:T(8,128)S(1)}, f32[8,768]{1,0:T(8,128)}, u32[]{:S(2)}) copy-start(f32[8,768]{1,0:T(8,128)} %get-tuple-element.44.stats) | copy-start | bytes 73732
  144.7 24.8 %copy-start = (bf16[1408,512]{1,0:T(8,128)(2,1)S(1)}, bf16[1408,512]{1,0:T(8,128)(2,1)}, u32[]{:S(2)}) copy-start(bf16[1408,512]{1,0:T(8,128)(2,1)} %w_e2d.3) | copy-start | bytes 4325380
Sparse Core Ops, SparseCore 0:
  11.5 60.1 all-gather.2

commit v4 on v2

--- a/solution.py
+++ b/solution.py
@@ -1,3 +1,5 @@
+import functools
+
 import jax
 import jax.numpy as jnp
 from jax import lax
@@ -51,7 +53,9 @@
     )(*args)
 
 
-def prep_body(keep, patches, gain, xn, x_slot, offsets):
+def prep_body(keep, gain, patches, xn, x_slot, offsets, x_in, sem):
+    fetch = pltpu.make_async_copy(patches, x_in, sem.at[0])
+    fetch.start()
     at_row = lax.broadcasted_iota(jnp.int32, (CAP, CAP), 0)
     at_col = lax.broadcasted_iota(jnp.int32, (CAP, CAP), 1)
     own = jnp.broadcast_to(keep[...], (CAP, CAP))
@@ -63,24 +67,84 @@
     pick = at_row == slot
     live = jnp.sum(pick.astype(F32), axis=1, keepdims=True) > 0.5
     spot = jnp.sum(jnp.where(pick, own - owner * FDEV, 0).astype(F32), axis=1, keepdims=True)
-    rows = dot(pick.astype(F32).astype(BF16), patches[...])
+    offsets[...] = jnp.broadcast_to(jnp.where(live, spot, -1.0), (CAP, 128)).astype(BF16)
+    fetch.wait()
+    rows = dot(pick.astype(F32).astype(BF16), x_in[...])
     x_slot[...] = rows.astype(BF16)
     lane = lax.broadcasted_iota(jnp.int32, rows.shape, 1)
     dead_row = jnp.where(lane == 0, DEAD, 0.0)
     xn[...] = jnp.where(live, layer_norm(rows, gain[...]), dead_row).astype(BF16)
-    offsets[...] = jnp.broadcast_to(jnp.where(live, spot, -1.0), (CAP, 128)).astype(BF16)
-
-
-def prep(keep, patches, gain):
-    width = patches.shape[1]
-    return call(
-        prep_body, [((CAP, width), BF16), ((CAP, width), BF16), ((CAP, 128), BF16)],
-        [], 1 << 20, 8, keep, patches, gain)
-
-
-def join_body(*refs):
-    blocks, out, sems = refs[:NZ], refs[NZ], refs[NZ + 1]
-    copies = [pltpu.make_async_copy(blocks[k], out.at[pl.ds(CAP * k, CAP)], sems.at[k]) for k in range(NZ)]
+
+
+def prep(keep, gain, patches):
+    cap, width = patches.shape
+    vmem = pl.BlockSpec(memory_space=pltpu.VMEM)
+    return pl.pallas_call(
+        prep_body,
+        out_shape=[jax.ShapeDtypeStruct((cap, width), BF16), jax.ShapeDtypeStruct((cap, width), BF16),
+                   jax.ShapeDtypeStruct((cap, 128), BF16)],
+        in_specs=[vmem, vmem, pl.BlockSpec(memory_space=pltpu.HBM)],
+        out_specs=[vmem] * 3,
+        scratch_shapes=[pltpu.VMEM((cap, width), BF16), pltpu.SemaphoreType.DMA((1,))],
+        compiler_params=pltpu.CompilerParams(vmem_limit_bytes=8 << 20),
+        cost_estimate=pl.CostEstimate(flops=10 << 20, bytes_accessed=1 << 19, transcendentals=0),
+    )(keep, gain, pltpu.with_memory_space_constraint(patches, pltpu.HBM))
+
+
+def pack_body(x_slot, w_out, w_e2d, fc_in, fc_out, x_vis, w_oe, pack, out_in, e2d_in, packed, sems):
+    loads = [
+        pltpu.make_async_copy(w_out, out_in, sems.at[0]),
+        pltpu.make_async_copy(w_e2d, e2d_in, sems.at[1]),
+        pltpu.make_async_copy(fc_in, packed.at[pl.ds(0, HID)], sems.at[2]),
+        pltpu.make_async_copy(fc_out, packed.at[pl.ds(HID, HID)], sems.at[3])]
+    for copy in loads:
+        copy.start()
+    for copy in loads:
+        copy.wait()
+    both = jnp.concatenate([dot(out_in[...], e2d_in[...]), jnp.zeros((HP - HD, DD), F32)], axis=0).astype(BF16)
+    w_oe[...] = both
+    packed[2 * HID:, :] = both
+    done = pltpu.make_async_copy(packed, pack, sems.at[4])
+    done.start()
+    x_vis[...] = dot(x_slot[...], e2d_in[...]).astype(BF16)
+    done.wait()
+
+
+def pack_up(x_slot, *args):
+    width = x_slot.shape[1]
+    vmem = pl.BlockSpec(memory_space=pltpu.VMEM)
+    hbm = pl.BlockSpec(memory_space=pltpu.HBM)
+    return pl.pallas_call(
+        pack_body,
+        out_shape=[jax.ShapeDtypeStruct((CAP, DD), BF16), jax.ShapeDtypeStruct((HP, DD), BF16),
+                   pltpu.HBM((2 * HID + HP, DD), BF16)],
+        in_specs=[vmem] + [hbm] * len(args),
+        out_specs=[vmem, vmem, hbm],
+        scratch_shapes=[pltpu.VMEM((HD, width), BF16), pltpu.VMEM((width, DD), BF16),
+                        pltpu.VMEM((2 * HID + HP, DD), BF16), pltpu.SemaphoreType.DMA((5,))],
+        compiler_params=pltpu.CompilerParams(vmem_limit_bytes=12 << 20),
+        cost_estimate=pl.CostEstimate(flops=200 << 20, bytes_accessed=3 << 20, transcendentals=0),
+    )(x_slot, *[pltpu.with_memory_space_constraint(arg, pltpu.HBM) for arg in args])
+
+
+def turn_body(w_t, w):
+    rows = w_t[...].astype(F32)
+    gap = jnp.zeros((HL - HD, rows.shape[1]), F32)
+    heads = [part for i in range(3) for part in (rows[HD * i:HD * (i + 1)], gap)]
+    w[...] = jnp.concatenate(heads, axis=0).T.astype(BF16)
+
+
+def turn(w_t):
+    return call(turn_body, [((w_t.shape[1], 3 * HL), BF16)], [], 1 << 20, 16, w_t)[0]
+
+
+def join_body(places, *refs):
+    blocks, out, sems = refs[:len(places)], refs[len(places)], refs[len(places) + 1]
+    copies = []
+    for i, (k, column) in enumerate(places):
+        rows, width = blocks[i].shape
+        part = out.at[pl.ds(rows * k, rows), pl.ds(column, width)]
+        copies.append(pltpu.make_async_copy(blocks[i], part, sems.at[i]))
     for copy in copies:
         copy.start()
     for copy in copies:
@@ -88,16 +152,22 @@
 
 
 def join(blocks):
-    rows, width = blocks[0].shape
-    return pl.pallas_call(
-        join_body,
-        out_shape=jax.ShapeDtypeStruct((NZ * rows, width), blocks[0].dtype),
-        in_specs=[pl.BlockSpec(memory_space=pl.ANY)] * NZ,
+    places = []
+    for k, parts in enumerate(blocks):
+        column = 0
+        for part in parts:
+            places.append((k, column))
+            column += part.shape[1]
+    flat = [part for parts in blocks for part in parts]
+    return pl.pallas_call(
+        functools.partial(join_body, places),
+        out_shape=jax.ShapeDtypeStruct((NZ * flat[0].shape[0], flat[0].shape[1]), flat[0].dtype),
+        in_specs=[pl.BlockSpec(memory_space=pl.ANY)] * len(flat),
         out_specs=pl.BlockSpec(memory_space=pl.ANY),
-        scratch_shapes=[pltpu.SemaphoreType.DMA((NZ,))],
+        scratch_shapes=[pltpu.SemaphoreType.DMA((len(flat),))],
         compiler_params=pltpu.CompilerParams(vmem_limit_bytes=4 << 20),
         cost_estimate=pl.CostEstimate(flops=0, bytes_accessed=4 << 20, transcendentals=0),
-    )(*blocks)
+    )(*flat)
 
 
 def attend_body(mine, other, w, swap, extra, sent, saved, stats, xs, out, keep, keep_stats, sems):
@@ -110,7 +180,7 @@
     parts = []
     for i in range(2):
         loads[i].wait()
-        parts.append(dot_nt(xs[half * i:half * (i + 1), :], w[...]))
+        parts.append(dot(xs[half * i:half * (i + 1), :], w[...]))
     qkv = jnp.concatenate(parts, axis=0)
     k_rows = qkv[:, HL:2 * HL].astype(BF16)
     q = (qkv[:, 0:HL] * SCALE).T.astype(BF16)
@@ -161,19 +231,17 @@
 
 
 def decode_body(came, weights, cot, mask, gain, table, recon, dvis, mixed, grad, w_oe, w_fc, cots, sems):
-    loads = [
+    loads = [pltpu.make_async_copy(weights.at[:, pl.ds(2 * HID, HP)], w_oe, sems.at[0])]
+    loads += [
         pltpu.make_async_copy(
-            weights.at[pl.ds(2 * i, 2), pl.ds(0, 2 * HID)], w_fc.at[pl.ds(2 * i, 2)], sems.at[i])
-        for i in range(8)]
-    oe = pltpu.make_async_copy(weights.at[:, pl.ds(2 * HID, HP)], w_oe, sems.at[8])
-    up = pltpu.make_async_copy(cot, cots, sems.at[9])
-    for load in (oe, up, loads[0]):
-        load.start()
+            weights.at[pl.ds(8 * i, 8), pl.ds(0, 2 * HID)], w_fc.at[pl.ds(8 * i, 8)], sems.at[1 + i])
+        for i in range(2)]
+    up = pltpu.make_async_copy(cot, cots, sems.at[3])
+    for copy in (loads[0], up, *loads[1:]):
+        copy.start()
     flat = came[...].reshape(16 * 64, 128)
     vis = jnp.zeros((CAP, DD), F32)
-    oe.wait()
-    for load in loads[1:]:
-        load.start()
+    loads[0].wait()
     for g in range(16):
         vis += dot(came[g, 0:CAP, 0:HP], w_oe[g])
     row = lax.broadcasted_iota(jnp.int32, (CAP, 1024), 0)
@@ -207,7 +275,8 @@
     cot_b = cots[...]
     mixed[...] = dec_x
     for i in range(8):
-        loads[i].wait()
+        if i % 4 == 0:
+            loads[1 + i // 4].wait()
         fin = jnp.concatenate([w_fc[2 * i, 0:HID, :], w_fc[2 * i + 1, 0:HID, :]], axis=0)
         fout = jnp.concatenate([w_fc[2 * i, HID:2 * HID, :], w_fc[2 * i + 1, HID:2 * HID, :]], axis=0)
         hidden = dot_nt(dn, fin)
@@ -239,7 +308,7 @@
         out_specs=[vmem, vmem],
         scratch_shapes=[pltpu.VMEM((FDEV, DD), F32), pltpu.VMEM((FDEV, DD), F32),
                         pltpu.VMEM((16, HP, DD), BF16), pltpu.VMEM((16, 2 * HID, DD), BF16),
-                        pltpu.VMEM((FDEV, DD), BF16), pltpu.SemaphoreType.DMA((10,))],
+                        pltpu.VMEM((FDEV, DD), BF16), pltpu.SemaphoreType.DMA((4,))],
         compiler_params=pltpu.CompilerParams(vmem_limit_bytes=24 << 20),
         cost_estimate=pl.CostEstimate(flops=2300 << 20, bytes_accessed=8 << 20, transcendentals=1 << 20),
     )(came, pltpu.with_memory_space_constraint(weights, pltpu.HBM),
@@ -354,7 +423,7 @@
     got[3] = z_shift(got[2], 1)
     got[5] = z_shift(got[6], -1)
     got[4] = z_shift(got[2], 2)
-    return [got[k] for k in range(NZ)]
+    return [[got[k]] for k in range(NZ)]
 
 
 def swap_core(block):
@@ -382,17 +451,13 @@
     cap = keep_pos.shape[1]
     rows = 16 * cap
 
-    xn_own, x_slot, offsets = prep(keep_pos, patches[0], enc_gain[None])
-    mine = join(around(xn_own))
-    other = swap_core(mine)
-
-    x_vis = dot(x_slot, w_e2d).astype(BF16)
+    xn_own, x_slot, offsets = prep(keep_pos, enc_gain[None], patches[0])
+    x_vis, w_oe_own, pack = pack_up(x_slot, w_out, w_e2d, fc_in, fc_out)
+    weights = lax.all_gather(pack, "seq", axis=0)
+
     places = jnp.pad(offsets[:, 0].reshape(16, 1, SLOTS), ((0, 0), (0, 0), (0, 128 - SLOTS)))
     extra = jnp.concatenate(
         [x_vis.reshape(16, 12, 128), places, jnp.zeros((16, 3, 128), BF16)], axis=1)
-
-    w_oe_own = jnp.pad(dot(w_out, w_e2d).astype(BF16), ((0, HP - HD), (0, 0)))
-    weights = lax.all_gather(jnp.concatenate([fc_in, fc_out, w_oe_own], axis=0), "seq", axis=0)
 
     tok = jnp.arange(rows, dtype=jnp.int32)
     block = tok // cap
@@ -402,7 +467,11 @@
     swap = (dest[None, :] == tok[:, None]).astype(BF16)
     table = position_table((me * fdev + jnp.arange(fdev, dtype=jnp.int32)).astype(F32), DD)
 
-    w = jnp.pad(w_qkv.transpose(0, 2, 1), ((0, 0), (0, HL - HD), (0, 0))).reshape(3 * HL, -1)
+    w = turn(w_qkv.transpose(0, 2, 1).reshape(3 * HD, -1))
+    blocks = around(xn_own)
+    blocks[4][0], w, swap, extra, table = lax.optimization_barrier((blocks[4][0], w, swap, extra, table))
+    mine = join(blocks)
+    other = swap_core(mine)
     sent, saved, stats = attend(mine, other, w, swap, extra)
     came = lax.all_to_all(sent, "seq", 0, 0, tiled=True)
     recon, dvis_own = decode(came, weights, cot, mask_token[None], dec_gain[None], table)

time: 181 us -> 178 us (0.983)
  starting transfers between devices: 36.1 us -> 39 us
  matrix products: 2.06 us -> 0 us
  local copies, waits for them, and re-layouts: 3.82 us -> 1.91 us
    pallas_call x1 -> x3, Pallas kernels: 1.07 us -> 5.47 us  [the longest x1 2.73 us: pack_up(): pl.pallas_call(pack_body, out_shape=[jax.ShapeDtypeStruct((CAP, DD), BF16...]
    ppermute x7, waiting for transfers between devices: 11.2 us -> 7.02 us  [z_shift(): lax.ppermute(block, 'seq', [(s, (s + 2 * step) % 16) for s in range(16)])]
    all_to_all x1, starting transfers between devices: 5.34 us -> 8.38 us  [local(): came = lax.all_to_all(sent, 'seq', 0, 0, tiled=True)]
    ppermute x1, waiting for transfers between devices: 0.56 us -> 2.67 us  [swap_core(): return lax.ppermute(block, 'seq', [(s, s ^ 1) for s in range(16)])]
    dot_general x2 -> x0, matrix products: 2.06 us -> none  [dot(): return jnp.dot(a, b, preferred_element_type=F32)]
  transfers between devices with their start and end apart: 10 -> 10, of which waited for: 4 -> 4; matrix products, arithmetic and copies ran while one was open for 2% -> 1% of each run, Pallas kernels for 4% -> 4%
where the time goes in v4:
time: 178 us; the launch traced here: 177 us
  blocking collectives  77.4 us (43%)
  starting transfers between devices  39 us (22%)
  Pallas kernels  23.4 us (13%)
  waiting for transfers between devices  19.3 us (11%)
  between operations  14.4 us (8%)
  local copies, waits for them, and re-layouts  1.91 us (1%)
  other arithmetic  1.82 us (1%)
    all_to_all x4, blocking collectives, exchange(): lax.all_to_all(block, axis, 0, 0, axis_index_groups=groups, tiled=True)  58.8 us
    ppermute x7, starting transfers between devices, z_shift(): lax.ppermute(block, 'seq', [(s, (s + 2 * step) % 16) for s in range(16)])  28.6 us
    all_gather x1, blocking collectives, local(): dvis = lax.all_gather(dvis_own, 'seq', axis=0, tiled=True)  18.6 us
    all_to_all x1, waiting for transfers between devices, local(): came = lax.all_to_all(sent, 'seq', 0, 0, tiled=True)  9.62 us
    all_to_all x1, starting transfers between devices, local(): came = lax.all_to_all(sent, 'seq', 0, 0, tiled=True)  8.38 us
    ppermute x7, waiting for transfers between devices, z_shift(): lax.ppermute(block, 'seq', [(s, (s + 2 * step) % 16) for s in range(16)])  7.02 us
    pallas_call x1, Pallas kernels, decode(): pl.pallas_call(decode_body, out_shape=[jax.ShapeDtypeStruct((FDEV, DD), B...  6.85 us
    pallas_call x1, Pallas kernels, attend(): pl.pallas_call(attend_body, out_shape=[pltpu.HBM((16, 64, 128), BF16), pl...  5.03 us
  transfers between devices with their start and end apart: 10, of which 4 were waited for; matrix products, arithmetic and copies ran while one was open for 1% of the time, Pallas kernels for 4%

profile of v4, /device:TPU:64, one launch (start us, length us, event | category | flops | bytes accessed | tf_op | source)
XLA Modules:
  0.0 177.1 jit_solution(10442747834737710237)
XLA Ops:
  7.2 0.0 all-gather.3.cloned.1.call-start
  7.2 0.7 broadcast_in_dim.32.gain
  7.9 0.0 copy-start.1
  7.9 0.7 copy-done.1
  8.6 1.3 shard_map.130
  9.9 2.7 %shard_map.132 = (bf16[48,512]{1,0:T(8,128)(2,1)S(1)}, bf16[96,512]{1,0:T(8,128)(2,1)S(1)}, bf16[352,512]{1,0:T(8,128)(2,1)}) custom-call(bf16[48,1408]{1,0:T(8,128)(2,1)S(1)} %get-tuple-element.22.x_slot, bf16[88,1408]{1,0:T(8,128)(2,1)} %w_out.1, bf16[1408,512]{1,0:T(8,128)(2,1)} %w_e2d.3, bf16[128,512]{1,0:T(8,128)(2,1)} %fc_in.1, bf16[128,512]{1,0:T(8,128)(2,1)} %fc_out.1), custom_call_target="tpu_custom_call" | custom-call | flops 209715200 | bytes 3145728 | tf_op jit(solution)/shard_map/pallas_call | solution.py:117
  12.6 0.0 copy-start.5
  12.6 0.0 copy-start.4
  12.6 0.0 all-gather.3.cloned.1.call-update
  12.6 6.2 %collective-permute-start.1 = (bf16[48,1408]{1,0:T(8,128)(2,1)S(1)}, bf16[48,1408]{1,0:T(8,128)(2,1)S(1)}, u32[]{:S(2)}, u32[]{:S(2)}) collective-permute-start(bf16[48,1408]{1,0:T(8,128)(2,1)S(1)} %get-tuple-element.21.refs_0_), channel_id=1, source_target_pairs={{0,4},{1,5},{2,6},{3,7},{4,8},{5,9},{6,10},{7,11},{8,12},{9,13},{1... | collective-permute-start | bytes 405512 | tf_op jit(solution)/shard_map/ppermute | solution.py:416
  18.9 5.9 %collective-permute-start.4 = (bf16[48,1408]{1,0:T(8,128)(2,1)S(1)}, bf16[48,1408]{1,0:T(8,128)(2,1)S(1)}, u32[]{:S(2)}, u32[]{:S(2)}) collective-permute-start(bf16[48,1408]{1,0:T(8,128)(2,1)S(1)} %get-tuple-element.21.refs_0_), channel_id=1, source_target_pairs={{0,12},{1,13},{2,14},{3,15},{4,0},{5,1},{6,2},{7,3},{8,4},{9,5},{1... | collective-permute-start | bytes 405512 | tf_op jit(solution)/shard_map/ppermute | solution.py:416
  24.8 1.9 %collective-permute-start = (bf16[48,1408]{1,0:T(8,128)(2,1)S(1)}, bf16[48,1408]{1,0:T(8,128)(2,1)S(1)}, u32[]{:S(2)}, u32[]{:S(2)}) collective-permute-start(bf16[48,1408]{1,0:T(8,128)(2,1)S(1)} %get-tuple-element.21.refs_0_), channel_id=1, source_target_pairs={{0,2},{1,3},{2,4},{3,5},{4,6},{5,7},{6,8},{7,9},{8,10},{9,11},{10,... | collective-permute-start | bytes 405512 | tf_op jit(solution)/shard_map/ppermute | solution.py:416
  26.7 3.9 %collective-permute-start.6 = (bf16[48,1408]{1,0:T(8,128)(2,1)S(1)}, bf16[48,1408]{1,0:T(8,128)(2,1)S(1)}, u32[]{:S(2)}, u32[]{:S(2)}) collective-permute-start(bf16[48,1408]{1,0:T(8,128)(2,1)S(1)} %get-tuple-element.21.refs_0_), channel_id=1, source_target_pairs={{0,14},{1,15},{2,0},{3,1},{4,2},{5,3},{6,4},{7,5},{8,6},{9,7},{10,... | collective-permute-start | bytes 405512 | tf_op jit(solution)/shard_map/ppermute | solution.py:416
  30.6 0.1 reshape.112
  30.7 0.1 slice_reduce_fusion
  30.8 0.1 reshape_squeeze.4
  30.9 0.1 pad.9.clone
  31.0 0.0 copy-done.5
  31.1 0.4 fusion.swap
  31.5 1.0 multiply_sine_fusion
  32.5 0.0 collective-permute-done.1.refs_2_
  32.5 3.6 %collective-permute-start.3 = (bf16[48,1408]{1,0:T(8,128)(2,1)S(1)}, bf16[48,1408]{1,0:T(8,128)(2,1)S(1)}, u32[]{:S(2)}, u32[]{:S(2)}) collective-permute-start(bf16[48,1408]{1,0:T(8,128)(2,1)S(1)} %collective-permute-done.1.refs_2_), channel_id=1, source_target_pairs={{0,4},{1,5},{2,6},{3,7},{4,8},{5,9},{6,10},{7,11},{8,12},{9,13},{1... | collective-permute-start | bytes 405512 | tf_op jit(solution)/shard_map/ppermute | solution.py:416
  36.2 5.1 %collective-permute-start.2 = (bf16[48,1408]{1,0:T(8,128)(2,1)S(1)}, bf16[48,1408]{1,0:T(8,128)(2,1)S(1)}, u32[]{:S(2)}, u32[]{:S(2)}) collective-permute-start(bf16[48,1408]{1,0:T(8,128)(2,1)S(1)} %collective-permute-done.1.refs_2_), channel_id=1, source_target_pairs={{0,2},{1,3},{2,4},{3,5},{4,6},{5,7},{6,8},{7,9},{8,10},{9,11},{10,... | collective-permute-start | bytes 405512 | tf_op jit(solution)/shard_map/ppermute | solution.py:416
  41.3 0.0 collective-permute-done.4.refs_6_
  41.3 1.9 %collective-permute-start.5 = (bf16[48,1408]{1,0:T(8,128)(2,1)S(1)}, bf16[48,1408]{1,0:T(8,128)(2,1)S(1)}, u32[]{:S(2)}, u32[]{:S(2)}) collective-permute-start(bf16[48,1408]{1,0:T(8,128)(2,1)S(1)} %collective-permute-done.4.refs_6_), channel_id=1, source_target_pairs={{0,14},{1,15},{2,0},{3,1},{4,2},{5,3},{6,4},{7,5},{8,6},{9,7},{10,... | collective-permute-start | bytes 405512 | tf_op jit(solution)/shard_map/ppermute | solution.py:416
  43.2 0.1 fusion.4.extra
  43.3 0.0 copy-done.4
  43.3 0.4 shard_map.131.w
  43.7 0.1 pad_maximum_fusion.table
  43.8 4.4 %collective-permute-done.3.refs_4_ = bf16[48,1408]{1,0:T(8,128)(2,1)S(1)} collective-permute-done((bf16[48,1408]{1,0:T(8,128)(2,1)S(1)}, bf16[48,1408]{1,0:T(8,128)(2,1)S(1)}, u32[]{:S(2)}, u32[]{:S(2)}) %collective-permute-start.3) | collective-permute-done | bytes 135200 | tf_op jit(solution)/shard_map/ppermute | solution.py:416
  48.2 0.0 collective-permute-done.refs_1_
  48.2 0.0 collective-permute-done.6.refs_7_
  48.2 2.6 %collective-permute-done.2.refs_3_ = bf16[48,1408]{1,0:T(8,128)(2,1)S(1)} collective-permute-done((bf16[48,1408]{1,0:T(8,128)(2,1)S(1)}, bf16[48,1408]{1,0:T(8,128)(2,1)S(1)}, u32[]{:S(2)}, u32[]{:S(2)}) %collective-permute-start.2) | collective-permute-done | bytes 135200 | tf_op jit(solution)/shard_map/ppermute | solution.py:416
  50.8 0.0 collective-permute-done.5.refs_5_
  50.8 1.5 shard_map.133.mine
  52.3 0.0 copy-start.10
  52.3 0.0 copy-start.7
  52.3 1.9 %collective-permute-start.7 = (bf16[384,1408]{1,0:T(8,128)(2,1)S(1)}, bf16[384,1408]{1,0:T(8,128)(2,1)S(1)}, u32[]{:S(2)}, u32[]{:S(2)}) collective-permute-start(bf16[384,1408]{1,0:T(8,128)(2,1)S(1)} %shard_map.133.mine), channel_id=1, source_target_pairs={{0,1},{1,0},{2,3},{3,2},{4,5},{5,4},{6,7},{7,6},{8,9},{9,8},{10,11... | collective-permute-start | bytes 3244040 | tf_op jit(solution)/shard_map/ppermute | solution.py:430
  54.2 2.7 %collective-permute-done.7.other = bf16[384,1408]{1,0:T(8,128)(2,1)S(1)} collective-permute-done((bf16[384,1408]{1,0:T(8,128)(2,1)S(1)}, bf16[384,1408]{1,0:T(8,128)(2,1)S(1)}, u32[]{:S(2)}, u32[]{:S(2)}) %collective-permute-start.7) | collective-permute-done | bytes 1081376 | tf_op jit(solution)/shard_map/ppermute | solution.py:430
  56.9 0.0 copy-start.2
  56.9 5.0 %shard_map.134 = (bf16[16,64,128]{2,1,0:T(8,128)(2,1)}, bf16[512,768]{1,0:T(8,128)(2,1)}, f32[8,768]{1,0:T(8,128)}) custom-call(bf16[384,1408]{1,0:T(8,128)(2,1)S(1)} %shard_map.133.mine, bf16[384,1408]{1,0:T(8,128)(2,1)S(1)} %collective-permute-done.7.other, bf16[1408,384]{1,0:T(8,128)(2,1)S(1)} %shard_map.131.w, bf16[768,768]{1,0:T(8,128)(2,1)S(1)} %fusion.swap, ...), custom_call_target="tpu_custom_call" | custom-call | flops 1782579200 | bytes 8388608 | tf_op jit(solution)/shard_map/pallas_call | solution.py:221
  61.9 0.0 copy-done.2
  61.9 8.4 %all-to-all-start = ((bf16[16,64,128]{2,1,0:T(8,128)(2,1)}), bf16[16,64,128]{2,1,0:T(8,128)(2,1)S(1)}, u32[]{:S(2)}, u32[]{:S(2)}) async-start(bf16[16,64,128]{2,1,0:T(8,128)(2,1)} %get-tuple-element.29), calls=%async_computation | async-start | bytes 524288 | tf_op jit(solution)/shard_map/all_to_all | solution.py:476
  70.3 0.0 copy-done.10
  70.3 9.6 %all-to-all-done.came = bf16[16,64,128]{2,1,0:T(8,128)(2,1)S(1)} async-done(((bf16[16,64,128]{2,1,0:T(8,128)(2,1)}), bf16[16,64,128]{2,1,0:T(8,128)(2,1)S(1)}, u32[]{:S(2)}, u32[]{:S(2)}) %all-to-all-start) | async-done | bytes 262176 | tf_op jit(solution)/shard_map/all_to_all | solution.py:476
  80.0 0.0 all-gather.3.cloned.1.call-done
  80.0 0.0 copy-done.7
  80.0 0.0 copy-start.8
  80.0 0.0 copy-start.9
  80.0 6.8 %shard_map.135 = (bf16[256,512]{1,0:T(8,128)(2,1)}, bf16[48,512]{1,0:T(8,128)(2,1)S(1)}) custom-call(bf16[16,64,128]{2,1,0:T(8,128)(2,1)S(1)} %all-to-all-done.came, bf16[16,352,512]{2,1,0:T(8,128)(2,1)} %bitcast.22, bf16[256,512]{1,0:T(8,128)(2,1)} %bitcast.24, bf16[1,512]{1,0:T(2,128)(2,1)S(1)} %broadcast_in_dim.34.mask, f32[1,512]{1,0:T(1,128)S(1)} %bitcast.18, ...), custom_call_target="tpu_custom_call" | custom-call | flops 2411724800 | bytes 8388608 | tf_op jit(solution)/shard_map/pallas_call | solution.py:304
  86.9 18.6 %all_gather.11.dvis = bf16[768,512]{1,0:T(8,128)(2,1)S(1)} all-gather(bf16[48,512]{1,0:T(8,128)(2,1)S(1)} %get-tuple-element.33), channel_id=1, replica_groups=mesh['dp'=32,'seq'=16] {'seq'}, dimensions={0}, use_global_device_ids=true | all-gather | bytes 835584 | tf_op jit(solution)/shard_map/all_gather | solution.py:478
  105.4 0.0 copy-done.3
  105.4 0.0 copy-done.6
  105.4 0.0 copy-done.8
  105.5 0.0 copy-done.9
  105.5 4.1 %shard_map.136 = bf16[3328,128]{1,0:T(8,128)(2,1)S(1)} custom-call(bf16[768,512]{1,0:T(8,128)(2,1)S(1)} %all_gather.11.dvis, bf16[96,512]{1,0:T(8,128)(2,1)S(1)} %copy-done.6, bf16[768,768]{1,0:T(8,128)(2,1)S(1)} %fusion.swap, bf16[512,768]{1,0:T(8,128)(2,1)S(1)} %copy-done.8, f32[8,768]{1,0:T(8,128)S(1)} %copy-done.9, ...), custom_call_target="tpu_custom_call" | custom-call | flops 2621440000 | bytes 8388608 | tf_op jit(solution)/shard_map/pallas_call | solution.py:363
  109.6 17.6 %all_to_all.25 = bf16[4,832,128]{2,1,0:T(8,128)(2,1)S(1)} all-to-all(bf16[4,832,128]{2,1,0:T(8,128)(2,1)S(1)} %bitcast.16), channel_id=1, replica_groups={{0,16,32,48},{64,80,96,112},{128,144,160,176},{192,208,224,240},{256,27..., dimensions={0} | all-to-all | bytes 1703936 | tf_op jit(solution)/shard_map/all_to_all | solution.py:406
  127.1 0.2 reduce_sum.24
  127.3 16.5 %all_to_all.26 = bf16[8,104,128]{2,1,0:T(8,128)(2,1)S(1)} all-to-all(bf16[8,104,128]{2,1,0:T(8,128)(2,1)S(1)} %bitcast.19), channel_id=1, replica_groups={{0,64,128,192,256,320,384,448},{16,80,144,208,272,336,400,464},{32,96,1..., dimensions={0} | all-to-all | bytes 425984 | tf_op jit(solution)/shard_map/all_to_all | solution.py:406
  143.9 12.4 %all_to_all.27 = bf16[8,104,128]{2,1,0:T(8,128)(2,1)S(1)} all-to-all(bf16[8,104,128]{2,1,0:T(8,128)(2,1)S(1)} %broadcast_in_dim.37), channel_id=1, replica_groups={{0,64,128,192,256,320,384,448},{16,80,144,208,272,336,400,464},{32,96,1..., dimensions={0} | all-to-all | bytes 425984 | tf_op jit(solution)/shard_map/all_to_all | solution.py:406
  156.3 0.1 broadcast_in_dim.39
  156.4 12.4 %all_to_all.28 = bf16[4,832,128]{2,1,0:T(8,128)(2,1)S(1)} all-to-all(bf16[4,832,128]{2,1,0:T(8,128)(2,1)S(1)} %broadcast_in_dim.39), channel_id=1, replica_groups={{0,16,32,48},{64,80,96,112},{128,144,160,176},{192,208,224,240},{256,27..., dimensions={0} | all-to-all | bytes 1703936 | tf_op jit(solution)/shard_map/all_to_all | solution.py:406
  168.7 0.0 copy-done
  168.7 1.5 shard_map.137
  (10 shorter events, 0.1 us)
Async XLA Ops:
  7.2 72.8 %all-gather.3.cloned.1.call-start = ((), (), s32[]{:S(2)}) async-start(), calls=%async_computation.5 | async-start | bytes 6127616 | tf_op jit(solution)/shard_map/all_gather | solution.py:456
  7.9 0.7 copy-start.1
  12.6 18.4 %copy-start.5 = (bf16[96,512]{1,0:T(8,128)(2,1)}, bf16[96,512]{1,0:T(8,128)(2,1)S(1)}, u32[]{:S(2)}) copy-start(bf16[96,512]{1,0:T(8,128)(2,1)S(1)} %get-tuple-element.34.w_oe) | copy-start | bytes 294916
  12.6 30.7 %copy-start.4 = (bf16[3,1408,88]{1,2,0:T(8,128)(2,1)S(1)}, bf16[3,1408,88]{1,2,0:T(8,128)(2,1)}, u32[]{:S(2)}) copy-start(bf16[3,1408,88]{1,2,0:T(8,128)(2,1)} %param.15) | copy-start | bytes 2230276
  12.6 19.8 %collective-permute-start.1 = (bf16[48,1408]{1,0:T(8,128)(2,1)S(1)}, bf16[48,1408]{1,0:T(8,128)(2,1)S(1)}, u32[]{:S(2)}, u32[]{:S(2)}) collective-permute-start(bf16[48,1408]{1,0:T(8,128)(2,1)S(1)} %get-tuple-element.21.refs_0_), channel_id=1, source_target_pairs={{0,4},{1,5},{2,6},{3,7},{4,8},{5,9},{6,10},{7,11},{8,12},{9,13},{1... | collective-permute-start | bytes 405512 | tf_op jit(solution)/shard_map/ppermute | solution.py:416
  18.9 22.4 %collective-permute-start.4 = (bf16[48,1408]{1,0:T(8,128)(2,1)S(1)}, bf16[48,1408]{1,0:T(8,128)(2,1)S(1)}, u32[]{:S(2)}, u32[]{:S(2)}) collective-permute-start(bf16[48,1408]{1,0:T(8,128)(2,1)S(1)} %get-tuple-element.21.refs_0_), channel_id=1, source_target_pairs={{0,12},{1,13},{2,14},{3,15},{4,0},{5,1},{6,2},{7,3},{8,4},{9,5},{1... | collective-permute-start | bytes 405512 | tf_op jit(solution)/shard_map/ppermute | solution.py:416
  24.8 23.4 %collective-permute-start = (bf16[48,1408]{1,0:T(8,128)(2,1)S(1)}, bf16[48,1408]{1,0:T(8,128)(2,1)S(1)}, u32[]{:S(2)}, u32[]{:S(2)}) collective-permute-start(bf16[48,1408]{1,0:T(8,128)(2,1)S(1)} %get-tuple-element.21.refs_0_), channel_id=1, source_target_pairs={{0,2},{1,3},{2,4},{3,5},{4,6},{5,7},{6,8},{7,9},{8,10},{9,11},{10,... | collective-permute-start | bytes 405512 | tf_op jit(solution)/shard_map/ppermute | solution.py:416
  26.7 21.5 %collective-permute-start.6 = (bf16[48,1408]{1,0:T(8,128)(2,1)S(1)}, bf16[48,1408]{1,0:T(8,128)(2,1)S(1)}, u32[]{:S(2)}, u32[]{:S(2)}) collective-permute-start(bf16[48,1408]{1,0:T(8,128)(2,1)S(1)} %get-tuple-element.21.refs_0_), channel_id=1, source_target_pairs={{0,14},{1,15},{2,0},{3,1},{4,2},{5,3},{6,4},{7,5},{8,6},{9,7},{10,... | collective-permute-start | bytes 405512 | tf_op jit(solution)/shard_map/ppermute | solution.py:416
  32.5 15.7 %collective-permute-start.3 = (bf16[48,1408]{1,0:T(8,128)(2,1)S(1)}, bf16[48,1408]{1,0:T(8,128)(2,1)S(1)}, u32[]{:S(2)}, u32[]{:S(2)}) collective-permute-start(bf16[48,1408]{1,0:T(8,128)(2,1)S(1)} %collective-permute-done.1.refs_2_), channel_id=1, source_target_pairs={{0,4},{1,5},{2,6},{3,7},{4,8},{5,9},{6,10},{7,11},{8,12},{9,13},{1... | collective-permute-start | bytes 405512 | tf_op jit(solution)/shard_map/ppermute | solution.py:416
  36.2 14.6 %collective-permute-start.2 = (bf16[48,1408]{1,0:T(8,128)(2,1)S(1)}, bf16[48,1408]{1,0:T(8,128)(2,1)S(1)}, u32[]{:S(2)}, u32[]{:S(2)}) collective-permute-start(bf16[48,1408]{1,0:T(8,128)(2,1)S(1)} %collective-permute-done.1.refs_2_), channel_id=1, source_target_pairs={{0,2},{1,3},{2,4},{3,5},{4,6},{5,7},{6,8},{7,9},{8,10},{9,11},{10,... | collective-permute-start | bytes 405512 | tf_op jit(solution)/shard_map/ppermute | solution.py:416
  41.3 9.5 %collective-permute-start.5 = (bf16[48,1408]{1,0:T(8,128)(2,1)S(1)}, bf16[48,1408]{1,0:T(8,128)(2,1)S(1)}, u32[]{:S(2)}, u32[]{:S(2)}) collective-permute-start(bf16[48,1408]{1,0:T(8,128)(2,1)S(1)} %collective-permute-done.4.refs_6_), channel_id=1, source_target_pairs={{0,14},{1,15},{2,0},{3,1},{4,2},{5,3},{6,4},{7,5},{8,6},{9,7},{10,... | collective-permute-start | bytes 405512 | tf_op jit(solution)/shard_map/ppermute | solution.py:416
  52.3 18.1 %copy-start.10 = (bf16[512]{0:T(512)(128)(2,1)S(1)}, bf16[512]{0:T(512)(128)(2,1)}, u32[]{:S(2)}) copy-start(bf16[512]{0:T(512)(128)(2,1)} %param.18) | copy-start | bytes 3076
  52.3 27.7 %copy-start.7 = (f32[512]{0:T(512)S(1)}, f32[512]{0:T(512)}, u32[]{:S(2)}) copy-start(f32[512]{0:T(512)} %param.19) | copy-start | bytes 6148
  52.3 4.6 %collective-permute-start.7 = (bf16[384,1408]{1,0:T(8,128)(2,1)S(1)}, bf16[384,1408]{1,0:T(8,128)(2,1)S(1)}, u32[]{:S(2)}, u32[]{:S(2)}) collective-permute-start(bf16[384,1408]{1,0:T(8,128)(2,1)S(1)} %shard_map.133.mine), channel_id=1, source_target_pairs={{0,1},{1,0},{2,3},{3,2},{4,5},{5,4},{6,7},{7,6},{8,9},{9,8},{10,11... | collective-permute-start | bytes 3244040 | tf_op jit(solution)/shard_map/ppermute | solution.py:430
  56.9 5.0 %copy-start.2 = (bf16[384,1408]{1,0:T(8,128)(2,1)}, bf16[384,1408]{1,0:T(8,128)(2,1)S(1)}, u32[]{:S(2)}) copy-start(bf16[384,1408]{1,0:T(8,128)(2,1)S(1)} %collective-permute-done.7.other) | copy-start | bytes 3244036
  61.9 18.0 %all-to-all-start = ((bf16[16,64,128]{2,1,0:T(8,128)(2,1)}), bf16[16,64,128]{2,1,0:T(8,128)(2,1)S(1)}, u32[]{:S(2)}, u32[]{:S(2)}) async-start(bf16[16,64,128]{2,1,0:T(8,128)(2,1)} %get-tuple-element.29), calls=%async_computation | async-start | bytes 524288 | tf_op jit(solution)/shard_map/all_to_all | solution.py:476
  80.0 25.5 %copy-start.3 = (bf16[384,1408]{1,0:T(8,128)(2,1)S(1)}, bf16[384,1408]{1,0:T(8,128)(2,1)}, u32[]{:S(2)}) copy-start(bf16[384,1408]{1,0:T(8,128)(2,1)} %copy-done.2) | copy-start | bytes 3244036
  80.0 25.5 %copy-start.6 = (bf16[96,512]{1,0:T(8,128)(2,1)S(1)}, bf16[96,512]{1,0:T(8,128)(2,1)}, u32[]{:S(2)}) copy-start(bf16[96,512]{1,0:T(8,128)(2,1)} %copy-done.5) | copy-start | bytes 294916
  80.0 25.5 %copy-start.8 = (bf16[512,768]{1,0:T(8,128)(2,1)S(1)}, bf16[512,768]{1,0:T(8,128)(2,1)}, u32[]{:S(2)}) copy-start(bf16[512,768]{1,0:T(8,128)(2,1)} %get-tuple-element.35.saved) | copy-start | bytes 2359300
  80.0 25.5 %copy-start.9 = (f32[8,768]{1,0:T(8,128)S(1)}, f32[8,768]{1,0:T(8,128)}, u32[]{:S(2)}) copy-start(f32[8,768]{1,0:T(8,128)} %get-tuple-element.36.stats) | copy-start | bytes 73732
  156.3 12.5 %copy-start = (bf16[1408,512]{1,0:T(8,128)(2,1)S(1)}, bf16[1408,512]{1,0:T(8,128)(2,1)}, u32[]{:S(2)}) copy-start(bf16[1408,512]{1,0:T(8,128)(2,1)} %w_e2d.3) | copy-start | bytes 4325380
Sparse Core Ops, SparseCore 0:
  12.8 59.4 all-gather.2

commit v5 on v4

--- a/solution.py
+++ b/solution.py
@@ -5,12 +5,14 @@
 from jax import lax
 from jax.experimental import pallas as pl
 from jax.experimental.pallas import tpu as pltpu
+from jax.sharding import Mesh
 from jax.sharding import PartitionSpec as P
 
 HD = 88
 HP = 96
 HL = 128
 DD = 512
+SEQ = ("z", "core")
 NZ = 8
 NX = 4
 NY = 8
@@ -53,12 +55,16 @@
     )(*args)
 
 
-def prep_body(keep, gain, patches, xn, x_slot, offsets, x_in, sem):
-    fetch = pltpu.make_async_copy(patches, x_in, sem.at[0])
-    fetch.start()
+def prep_body(keep, gain, patches, xn, x_slot, offsets, keep_in, gain_in, x_in, sems):
+    small = pltpu.make_async_copy(keep, keep_in, sems.at[0])
+    other = pltpu.make_async_copy(gain, gain_in, sems.at[1])
+    fetch = pltpu.make_async_copy(patches, x_in, sems.at[2])
+    for copy in (small, fetch, other):
+        copy.start()
+    small.wait()
     at_row = lax.broadcasted_iota(jnp.int32, (CAP, CAP), 0)
     at_col = lax.broadcasted_iota(jnp.int32, (CAP, CAP), 1)
-    own = jnp.broadcast_to(keep[...], (CAP, CAP))
+    own = jnp.broadcast_to(keep_in[...], (CAP, CAP))
     owner = lax.shift_right_arithmetic(own, 8)
     owner_col = jnp.sum(jnp.where(at_row == at_col, owner, 0), axis=1, keepdims=True)
     same = (owner_col == owner) & (at_row < at_col)
@@ -69,11 +75,12 @@
     spot = jnp.sum(jnp.where(pick, own - owner * FDEV, 0).astype(F32), axis=1, keepdims=True)
     offsets[...] = jnp.broadcast_to(jnp.where(live, spot, -1.0), (CAP, 128)).astype(BF16)
     fetch.wait()
+    other.wait()
     rows = dot(pick.astype(F32).astype(BF16), x_in[...])
     x_slot[...] = rows.astype(BF16)
     lane = lax.broadcasted_iota(jnp.int32, rows.shape, 1)
     dead_row = jnp.where(lane == 0, DEAD, 0.0)
-    xn[...] = jnp.where(live, layer_norm(rows, gain[...]), dead_row).astype(BF16)
+    xn[...] = jnp.where(live, layer_norm(rows, gain_in[...].reshape(1, rows.shape[1])), dead_row).astype(BF16)
 
 
 def prep(keep, gain, patches):
@@ -83,12 +90,13 @@
         prep_body,
         out_shape=[jax.ShapeDtypeStruct((cap, width), BF16), jax.ShapeDtypeStruct((cap, width), BF16),
                    jax.ShapeDtypeStruct((cap, 128), BF16)],
-        in_specs=[vmem, vmem, pl.BlockSpec(memory_space=pltpu.HBM)],
+        in_specs=[pl.BlockSpec(memory_space=pltpu.HBM)] * 3,
         out_specs=[vmem] * 3,
-        scratch_shapes=[pltpu.VMEM((cap, width), BF16), pltpu.SemaphoreType.DMA((1,))],
+        scratch_shapes=[pltpu.VMEM(keep.shape, keep.dtype), pltpu.VMEM(gain.shape, F32),
+                        pltpu.VMEM((cap, width), BF16), pltpu.SemaphoreType.DMA((3,))],
         compiler_params=pltpu.CompilerParams(vmem_limit_bytes=8 << 20),
         cost_estimate=pl.CostEstimate(flops=10 << 20, bytes_accessed=1 << 19, transcendentals=0),
-    )(keep, gain, pltpu.with_memory_space_constraint(patches, pltpu.HBM))
+    )(*[pltpu.with_memory_space_constraint(arg, pltpu.HBM) for arg in (keep, gain, patches)])
 
 
 def pack_body(x_slot, w_out, w_e2d, fc_in, fc_out, x_vis, w_oe, pack, out_in, e2d_in, packed, sems):
@@ -138,13 +146,10 @@
     return call(turn_body, [((w_t.shape[1], 3 * HL), BF16)], [], 1 << 20, 16, w_t)[0]
 
 
-def join_body(places, *refs):
-    blocks, out, sems = refs[:len(places)], refs[len(places)], refs[len(places) + 1]
-    copies = []
-    for i, (k, column) in enumerate(places):
-        rows, width = blocks[i].shape
-        part = out.at[pl.ds(rows * k, rows), pl.ds(column, width)]
-        copies.append(pltpu.make_async_copy(blocks[i], part, sems.at[i]))
+def join_body(*refs):
+    count = len(refs) - 2
+    blocks, out, sems = refs[:count], refs[count], refs[count + 1]
+    copies = [pltpu.make_async_copy(blocks[k], out.at[pl.ds(CAP * k, CAP)], sems.at[k]) for k in range(count)]
     for copy in copies:
         copy.start()
     for copy in copies:
@@ -152,34 +157,39 @@
 
 
 def join(blocks):
-    places = []
-    for k, parts in enumerate(blocks):
-        column = 0
-        for part in parts:
-            places.append((k, column))
-            column += part.shape[1]
-    flat = [part for parts in blocks for part in parts]
-    return pl.pallas_call(
-        functools.partial(join_body, places),
-        out_shape=jax.ShapeDtypeStruct((NZ * flat[0].shape[0], flat[0].shape[1]), flat[0].dtype),
-        in_specs=[pl.BlockSpec(memory_space=pl.ANY)] * len(flat),
+    rows, width = blocks[0].shape
+    return pl.pallas_call(
+        join_body,
+        out_shape=jax.ShapeDtypeStruct((len(blocks) * rows, width), blocks[0].dtype),
+        in_specs=[pl.BlockSpec(memory_space=pl.ANY)] * len(blocks),
         out_specs=pl.BlockSpec(memory_space=pl.ANY),
-        scratch_shapes=[pltpu.SemaphoreType.DMA((len(flat),))],
+        scratch_shapes=[pltpu.SemaphoreType.DMA((len(blocks),))],
         compiler_params=pltpu.CompilerParams(vmem_limit_bytes=4 << 20),
-        cost_estimate=pl.CostEstimate(flops=0, bytes_accessed=4 << 20, transcendentals=0),
-    )(*flat)
-
-
-def attend_body(mine, other, w, swap, extra, sent, saved, stats, xs, out, keep, keep_stats, sems):
+        cost_estimate=pl.CostEstimate(flops=0, bytes_accessed=2 << 20, transcendentals=0),
+    )(*blocks)
+
+
+def row_loads(rows_in, xs, sems, first):
+    copies = []
+    for d in range(2):
+        near, far = rows_in[2 * d], rows_in[2 * d + 1]
+        for source, start, place, count in ((near, 0, 0, 3), (near, 3, 6, 2), (far, 0, 3, 3)):
+            copies.append(pltpu.make_async_copy(
+                source.at[pl.ds(CAP * start, CAP * count)],
+                xs.at[pl.ds(CAP * (NZ * d + place), CAP * count)], sems.at[first + len(copies)]))
+    return copies
+
+
+def attend_body(w, swap, extra, *refs):
+    rows_in, (sent, saved, stats, xs, out, keep, keep_stats, sems) = refs[:4], refs[4:]
     half = ROWS // 2
-    loads = [
-        pltpu.make_async_copy(mine, xs.at[pl.ds(0, half)], sems.at[0]),
-        pltpu.make_async_copy(other, xs.at[pl.ds(half, half)], sems.at[1])]
+    loads = row_loads(rows_in, xs, sems, 6)
     for load in loads:
         load.start()
     parts = []
     for i in range(2):
-        loads[i].wait()
+        for load in loads[3 * i:3 * (i + 1)]:
+            load.wait()
         parts.append(dot(xs[half * i:half * (i + 1), :], w[...]))
     qkv = jnp.concatenate(parts, axis=0)
     k_rows = qkv[:, HL:2 * HL].astype(BF16)
@@ -204,8 +214,7 @@
     sums = pltpu.make_async_copy(keep_stats, stats, sems.at[3])
     sums.start()
     ctx = jnp.concatenate(ctx, axis=1).astype(BF16)
-    out[:, 0:CAP, :] = dot_nt(swap[...], ctx).astype(BF16).reshape(16, CAP, 128)
-    out[:, CAP:, :] = extra[...]
+    out[...] = dot_nt(swap[...], ctx).astype(BF16).reshape(16, CAP, 128) + extra[...]
     send = pltpu.make_async_copy(out, sent, sems.at[4])
     send.start()
     keep[3 * HL:, :] = dot_nt(ctx, swap[...]).astype(BF16)
@@ -220,11 +229,11 @@
     hbm = pl.BlockSpec(memory_space=pltpu.HBM)
     return pl.pallas_call(
         attend_body,
-        out_shape=[pltpu.HBM((16, 64, 128), BF16), pltpu.HBM((4 * HL, ROWS), BF16), pltpu.HBM((8, ROWS), F32)],
-        in_specs=[hbm, hbm, vmem, vmem, vmem],
+        out_shape=[pltpu.HBM((16, CAP, 128), BF16), pltpu.HBM((4 * HL, ROWS), BF16), pltpu.HBM((8, ROWS), F32)],
+        in_specs=[vmem] * 3 + [hbm] * 4,
         out_specs=[hbm, hbm, hbm],
-        scratch_shapes=[pltpu.VMEM((ROWS, args[0].shape[1]), BF16), pltpu.VMEM((16, 64, 128), BF16),
-                        pltpu.VMEM((4 * HL, ROWS), BF16), pltpu.VMEM((8, ROWS), F32), pltpu.SemaphoreType.DMA((6,))],
+        scratch_shapes=[pltpu.VMEM((ROWS, args[0].shape[0]), BF16), pltpu.VMEM((16, CAP, 128), BF16),
+                        pltpu.VMEM((4 * HL, ROWS), BF16), pltpu.VMEM((8, ROWS), F32), pltpu.SemaphoreType.DMA((12,))],
         compiler_params=pltpu.CompilerParams(vmem_limit_bytes=24 << 20),
         cost_estimate=pl.CostEstimate(flops=1700 << 20, bytes_accessed=8 << 20, transcendentals=1 << 20),
     )(*args)
@@ -239,24 +248,24 @@
     up = pltpu.make_async_copy(cot, cots, sems.at[3])
     for copy in (loads[0], up, *loads[1:]):
         copy.start()
-    flat = came[...].reshape(16 * 64, 128)
+    flat = came[...].reshape(16 * CAP, 128)
     vis = jnp.zeros((CAP, DD), F32)
     loads[0].wait()
     for g in range(16):
         vis += dot(came[g, 0:CAP, 0:HP], w_oe[g])
-    row = lax.broadcasted_iota(jnp.int32, (CAP, 1024), 0)
-    col = lax.broadcasted_iota(jnp.int32, (CAP, 1024), 1)
-    source = jnp.zeros((CAP, 1024), jnp.int32)
-    for g in range(1, 16):
-        source += (row >= SLOTS * g).astype(jnp.int32)
-    slot = row - SLOTS * source
-    base = 64 * source + CAP
-    x_part = jnp.concatenate(
-        [dot((col == base + 4 * slot + i).astype(F32).astype(BF16), flat) for i in range(4)], axis=1)
-    vis = (vis + x_part).astype(BF16)
-    spots = dot((col == base + 12).astype(F32).astype(BF16), flat)
+    row = lax.broadcasted_iota(jnp.int32, (CAP, 16 * CAP), 0)
+    col = lax.broadcasted_iota(jnp.int32, (CAP, 16 * CAP), 1)
+    own = ((col >= 16 * row) & (col < 16 * row + 16)).astype(F32).astype(BF16)
+    lane_in = lax.broadcasted_iota(jnp.int32, (128, DD), 0) - HP
+    lane_out = lax.broadcasted_iota(jnp.int32, (128, DD), 1)
+    repeat = (lane_in == (lane_out & 31)).astype(F32).astype(BF16)
+    turn_of = lax.broadcasted_iota(jnp.int32, (16 * CAP, DD), 0) & 15
+    piece = lax.shift_right_logical(lax.broadcasted_iota(jnp.int32, (16 * CAP, DD), 1), 5)
+    laid = jnp.where(turn_of == piece, dot(flat, repeat), 0.0).astype(BF16)
+    vis = (vis + dot(own, laid)).astype(BF16)
+    spots = dot((col == 16 * row).astype(F32).astype(BF16), flat)
     lane = lax.broadcasted_iota(jnp.int32, (CAP, 128), 1)
-    spot = jnp.sum(jnp.where(lane == slot[:, 0:128], spots, 0.0), axis=1, keepdims=True)
+    spot = jnp.sum(jnp.where(lane == HD, spots, 0.0), axis=1, keepdims=True)
     spot = jnp.concatenate([spot, jnp.full((128 - CAP, 1), -1.0, F32)], axis=0)
     vis = jnp.concatenate([vis.astype(F32), jnp.zeros((128 - CAP, DD), F32)], axis=0).astype(BF16)
     where_col = lax.broadcasted_iota(jnp.int32, (128, FDEV), 1).astype(F32)
@@ -315,12 +324,11 @@
       pltpu.with_memory_space_constraint(cot, pltpu.HBM), *args)
 
 
-def back_body(dvis, w_oe, swap, saved, stats, mine, other, parts, ds_all, pb_all, keep, keep_stats, xs, sems):
+def back_body(dvis, w_oe, swap, saved, stats, *refs):
+    rows_in, (parts, ds_all, pb_all, keep, keep_stats, xs, sems) = refs[:4], refs[4:]
     loads = [
         pltpu.make_async_copy(saved, keep, sems.at[0]),
-        pltpu.make_async_copy(stats, keep_stats, sems.at[1]),
-        pltpu.make_async_copy(mine, xs.at[pl.ds(0, ROWS // 2)], sems.at[2]),
-        pltpu.make_async_copy(other, xs.at[pl.ds(ROWS // 2, ROWS // 2)], sems.at[3])]
+        pltpu.make_async_copy(stats, keep_stats, sems.at[1])] + row_loads(rows_in, xs, sems, 2)
     for load in loads:
         load.start()
     dctx = dot(dot_nt(w_oe[...], dvis[...]).astype(BF16), swap[...])
@@ -357,20 +365,20 @@
     parts[...] = jnp.concatenate(pieces, axis=0).astype(BF16)
 
 
-def back(dvis, w_oe, swap, saved, stats, mine, other):
+def back(dvis, w_oe, swap, saved, stats, *rows_in):
     vmem = pl.BlockSpec(memory_space=pltpu.VMEM)
     hbm = pl.BlockSpec(memory_space=pltpu.HBM)
     return pl.pallas_call(
         back_body,
         out_shape=jax.ShapeDtypeStruct((GRAD_ROWS, 128), BF16),
-        in_specs=[vmem, vmem, vmem, hbm, hbm, hbm, hbm],
+        in_specs=[vmem, vmem, vmem] + [hbm] * 6,
         out_specs=vmem,
         scratch_shapes=[pltpu.VMEM((ROWS, ROWS), BF16), pltpu.VMEM((ROWS, ROWS), BF16),
                         pltpu.VMEM((4 * HL, ROWS), BF16), pltpu.VMEM((8, ROWS), F32),
-                        pltpu.VMEM((ROWS, mine.shape[1]), BF16), pltpu.SemaphoreType.DMA((4,))],
+                        pltpu.VMEM((ROWS, rows_in[0].shape[1]), BF16), pltpu.SemaphoreType.DMA((8,))],
         compiler_params=pltpu.CompilerParams(vmem_limit_bytes=24 << 20),
         cost_estimate=pl.CostEstimate(flops=2500 << 20, bytes_accessed=8 << 20, transcendentals=1 << 20),
-    )(dvis, w_oe, swap, saved, stats, mine, other)
+    )(dvis, w_oe, swap, saved, stats, *rows_in)
 
 
 def finish_body(total, w_e2d, grad_q, grad_o):
@@ -397,23 +405,16 @@
     return jnp.concatenate([jnp.sin(angle), jnp.cos(angle)], axis=1)
 
 
-Z_GROUPS = [[2 * z + c for z in range(NZ)] for c in range(2)]
-X_GROUPS = [[NX * y + x for x in range(NX)] for y in range(NY)]
-Y_GROUPS = [[NX * y + x for y in range(NY)] for x in range(NX)]
-
-
-def exchange(block, axis, groups):
-    return lax.all_to_all(block, axis, 0, 0, axis_index_groups=groups, tiled=True)
-
-
-def spread(block, axis, groups):
-    count = len(groups[0])
-    copies = jnp.broadcast_to(block[None], (count,) + block.shape)
-    return exchange(copies, axis, groups)
+def exchange(block, axis):
+    return lax.all_to_all(block, axis, 0, 0, tiled=True)
+
+
+def spread(block, axis):
+    return exchange(jnp.broadcast_to(block[None], (lax.axis_size(axis),) + block.shape), axis)
 
 
 def z_shift(block, step):
-    return lax.ppermute(block, "seq", [(s, (s + 2 * step) % 16) for s in range(16)])
+    return lax.ppermute(block, "z", [(z, (z + step) % NZ) for z in range(NZ)])
 
 
 def around(block):
@@ -423,11 +424,11 @@
     got[3] = z_shift(got[2], 1)
     got[5] = z_shift(got[6], -1)
     got[4] = z_shift(got[2], 2)
-    return [[got[k]] for k in range(NZ)]
+    return got
 
 
 def swap_core(block):
-    return lax.ppermute(block, "seq", [(s, s ^ 1) for s in range(16)])
+    return lax.ppermute(block, "core", [(0, 1), (1, 0)])
 
 
 def local(
@@ -444,20 +445,21 @@
     fc_out,
     cotangent,
 ):
-    me = lax.axis_index("seq")
+    me = lax.axis_index(SEQ)
     my_z, my_c = me // 2, me % 2
     fdev = cotangent.shape[1]
     cot = cotangent[0]
     cap = keep_pos.shape[1]
     rows = 16 * cap
 
-    xn_own, x_slot, offsets = prep(keep_pos, enc_gain[None], patches[0])
+    xn_own, x_slot, offsets = prep(keep_pos, enc_gain, patches[0])
     x_vis, w_oe_own, pack = pack_up(x_slot, w_out, w_e2d, fc_in, fc_out)
-    weights = lax.all_gather(pack, "seq", axis=0)
-
-    places = jnp.pad(offsets[:, 0].reshape(16, 1, SLOTS), ((0, 0), (0, 0), (0, 128 - SLOTS)))
+    weights = lax.all_gather(pack, SEQ, axis=0)
+
+    places = jnp.repeat(offsets[:, 0].reshape(16, SLOTS), 16, axis=1)[:, :, None]
     extra = jnp.concatenate(
-        [x_vis.reshape(16, 12, 128), places, jnp.zeros((16, 3, 128), BF16)], axis=1)
+        [jnp.zeros((16, cap, HD), BF16), places, jnp.zeros((16, cap, HP - HD - 1), BF16), x_vis.reshape(16, cap, 32)],
+        axis=2)
 
     tok = jnp.arange(rows, dtype=jnp.int32)
     block = tok // cap
@@ -468,44 +470,49 @@
     table = position_table((me * fdev + jnp.arange(fdev, dtype=jnp.int32)).astype(F32), DD)
 
     w = turn(w_qkv.transpose(0, 2, 1).reshape(3 * HD, -1))
-    blocks = around(xn_own)
-    blocks[4][0], w, swap, extra, table = lax.optimization_barrier((blocks[4][0], w, swap, extra, table))
-    mine = join(blocks)
-    other = swap_core(mine)
-    sent, saved, stats = attend(mine, other, w, swap, extra)
-    came = lax.all_to_all(sent, "seq", 0, 0, tiled=True)
+    got = around(xn_own)
+    got[0], got[5] = lax.optimization_barrier((got[0], got[5]))
+    near = join([got[k] for k in (0, 1, 2, 6, 7)])
+    near_other = swap_core(near)
+    got[4], w, swap, extra, table = lax.optimization_barrier((got[4], w, swap, extra, table))
+    far = join([got[k] for k in (3, 4, 5)])
+    rows_in = (near, far, near_other, swap_core(far))
+    sent, saved, stats = attend(w, swap, extra, *rows_in)
+    came = exchange(sent, SEQ)
     recon, dvis_own = decode(came, weights, cot, mask_token[None], dec_gain[None], table)
-    dvis = lax.all_gather(dvis_own, "seq", axis=0, tiled=True)
-    parts = back(dvis, w_oe_own, swap, saved, stats, mine, other)
-
-    parts = jnp.sum(exchange(parts.reshape(NX, 832, 128), "dp", X_GROUPS).astype(F32), axis=0).astype(BF16)
-    parts = jnp.sum(exchange(parts.reshape(NY, 104, 128), "dp", Y_GROUPS).astype(F32), axis=0).astype(BF16)
-    parts = spread(parts, "dp", Y_GROUPS).reshape(832, 128)
-    total = spread(parts, "dp", X_GROUPS).reshape(GRAD_ROWS, 128)
+    dvis = lax.all_gather(dvis_own, SEQ, axis=0, tiled=True)
+    parts = back(dvis, w_oe_own, swap, saved, stats, *rows_in)
+
+    parts = jnp.sum(exchange(parts.reshape(NX, 832, 128), "x").astype(F32), axis=0).astype(BF16)
+    parts = jnp.sum(exchange(parts.reshape(NY, 104, 128), "y").astype(F32), axis=0).astype(BF16)
+    parts = spread(parts, "y").reshape(832, 128)
+    total = spread(parts, "x").reshape(GRAD_ROWS, 128)
     grad_q, grad_o = finish(total, w_e2d)
     grad_q = grad_q.reshape(3, HD, -1).transpose(0, 2, 1)
     return (recon[None], grad_q, grad_o)
 
 
 def solution(mesh):
+    axes = Mesh(mesh.devices.reshape(NY, NX, NZ, 2), ("y", "x", "z", "core"))
+    dp = ("y", "x")
     placed = (
-        P("dp", "seq", None),
-        P("dp", "seq"),
-        P("dp", None),
+        P(dp, SEQ, None),
+        P(dp, SEQ),
+        P(dp, None),
         P(),
-        P(None, None, "seq"),
-        P("seq", None),
+        P(None, None, SEQ),
+        P(SEQ, None),
         P(),
         P(),
         P(),
-        P("seq", None),
-        P("seq", None),
-        P("dp", "seq", None),
+        P(SEQ, None),
+        P(SEQ, None),
+        P(dp, SEQ, None),
     )
     return jax.shard_map(
         local,
-        mesh=mesh,
+        mesh=axes,
         in_specs=placed,
-        out_specs=(P("dp", "seq", None), P(None, None, "seq"), P("seq", None)),
+        out_specs=(P(dp, SEQ, None), P(None, None, SEQ), P(SEQ, None)),
         check_vma=False,
     )

time: 178 us -> 180 us (1.011)
    ppermute x8 -> x9, starting transfers between devices: 30.6 us -> 32.6 us  [the longest x7 28.6 us: z_shift(): return lax.ppermute(block, 'z', [(z, (z + step) % NZ) for z in range(NZ)])]
    pallas_call x2 -> x3, Pallas kernels: 6.49 us -> 7.17 us  [the longest x1 5.72 us: attend(): pl.pallas_call(attend_body, out_shape=[pltpu.HBM((16, CAP, 128), BF16), p...]
    ppermute x8 -> x9, waiting for transfers between devices: 9.69 us -> 9.85 us  [the longest x7 8.14 us: z_shift(): return lax.ppermute(block, 'z', [(z, (z + step) % NZ) for z in range(NZ)])]
  transfers between devices with their start and end apart: 10 -> 11, of which waited for: 4 -> 4; matrix products, arithmetic and copies ran while one was open for 1% -> 2% of each run, Pallas kernels for 4% -> 4%
where the time goes in v5:
time: 180 us
  blocking collectives  77.4 us (43%)
  starting transfers between devices  40.2 us (22%)
  Pallas kernels  24.9 us (14%)
  waiting for transfers between devices  18.4 us (10%)
  between operations  14.4 us (8%)
  local copies, waits for them, and re-layouts  2.34 us (1%)
  other arithmetic  1.92 us (1%)
    all_to_all x4, blocking collectives, exchange(): return lax.all_to_all(block, axis, 0, 0, tiled=True)  59.1 us
    ppermute x7, starting transfers between devices, z_shift(): return lax.ppermute(block, 'z', [(z, (z + step) % NZ) for z in range(NZ)])  28.6 us
    all_gather x1, blocking collectives, local(): dvis = lax.all_gather(dvis_own, SEQ, axis=0, tiled=True)  18.3 us
    all_to_all x1, waiting for transfers between devices, exchange(): return lax.all_to_all(block, axis, 0, 0, tiled=True)  8.52 us
    ppermute x7, waiting for transfers between devices, z_shift(): return lax.ppermute(block, 'z', [(z, (z + step) % NZ) for z in range(NZ)])  8.14 us
    all_to_all x1, starting transfers between devices, exchange(): return lax.all_to_all(block, axis, 0, 0, tiled=True)  7.53 us
    pallas_call x1, Pallas kernels, decode(): pl.pallas_call(decode_body, out_shape=[jax.ShapeDtypeStruct((FDEV, DD), B...  7 us
    pallas_call x1, Pallas kernels, attend(): pl.pallas_call(attend_body, out_shape=[pltpu.HBM((16, CAP, 128), BF16), p...  5.72 us
  transfers between devices with their start and end apart: 11, of which 4 were waited for; matrix products, arithmetic and copies ran while one was open for 2% of the time, Pallas kernels for 4%

profile of v5, /device:TPU:64, one launch (start us, length us, event | category | flops | bytes accessed | tf_op | source)
XLA Modules:
  0.0 179.5 jit_solution(14340569355154660124)
XLA Ops:
  7.2 0.0 all-gather.3.cloned.1.call-start
  7.2 1.3 shard_map.130
  8.5 2.7 %shard_map.132 = (bf16[48,512]{1,0:T(8,128)(2,1)S(1)}, bf16[96,512]{1,0:T(8,128)(2,1)S(1)}, bf16[352,512]{1,0:T(8,128)(2,1)}) custom-call(bf16[48,1408]{1,0:T(8,128)(2,1)S(1)} %get-tuple-element.25.x_slot, bf16[88,1408]{1,0:T(8,128)(2,1)} %w_out.1, bf16[1408,512]{1,0:T(8,128)(2,1)} %w_e2d.3, bf16[128,512]{1,0:T(8,128)(2,1)} %fc_in.1, bf16[128,512]{1,0:T(8,128)(2,1)} %fc_out.1), custom_call_target="tpu_custom_call" | custom-call | flops 209715200 | bytes 3145728 | tf_op jit(solution)/shard_map/pallas_call | solution.py:125
  11.3 0.0 all-gather.3.cloned.1.call-update
  11.3 6.1 %collective-permute-start = (bf16[48,1408]{1,0:T(8,128)(2,1)S(1)}, bf16[48,1408]{1,0:T(8,128)(2,1)S(1)}, u32[]{:S(2)}, u32[]{:S(2)}) collective-permute-start(bf16[48,1408]{1,0:T(8,128)(2,1)S(1)} %get-tuple-element.30.refs_0_), channel_id=1, source_target_pairs={{0,4},{2,6},{4,8},{6,10},{8,12},{10,14},{12,0},{14,2},{1,5},{3,7},... | collective-permute-start | bytes 405512 | tf_op jit(solution)/shard_map/ppermute | solution.py:417
  17.4 5.9 %collective-permute-start.2 = (bf16[48,1408]{1,0:T(8,128)(2,1)S(1)}, bf16[48,1408]{1,0:T(8,128)(2,1)S(1)}, u32[]{:S(2)}, u32[]{:S(2)}) collective-permute-start(bf16[48,1408]{1,0:T(8,128)(2,1)S(1)} %get-tuple-element.30.refs_0_), channel_id=1, source_target_pairs={{0,12},{2,14},{4,0},{6,2},{8,4},{10,6},{12,8},{14,10},{1,13},{3,15... | collective-permute-start | bytes 405512 | tf_op jit(solution)/shard_map/ppermute | solution.py:417
  23.3 1.9 %collective-permute-start.4 = (bf16[48,1408]{1,0:T(8,128)(2,1)S(1)}, bf16[48,1408]{1,0:T(8,128)(2,1)S(1)}, u32[]{:S(2)}, u32[]{:S(2)}) collective-permute-start(bf16[48,1408]{1,0:T(8,128)(2,1)S(1)} %get-tuple-element.30.refs_0_), channel_id=1, source_target_pairs={{0,2},{2,4},{4,6},{6,8},{8,10},{10,12},{12,14},{14,0},{1,3},{3,5},... | collective-permute-start | bytes 405512 | tf_op jit(solution)/shard_map/ppermute | solution.py:417
  25.2 3.9 %collective-permute-start.5 = (bf16[48,1408]{1,0:T(8,128)(2,1)S(1)}, bf16[48,1408]{1,0:T(8,128)(2,1)S(1)}, u32[]{:S(2)}, u32[]{:S(2)}) collective-permute-start(bf16[48,1408]{1,0:T(8,128)(2,1)S(1)} %get-tuple-element.30.refs_0_), channel_id=1, source_target_pairs={{0,14},{2,0},{4,2},{6,4},{8,6},{10,8},{12,10},{14,12},{1,15},{3,1}... | collective-permute-start | bytes 405512 | tf_op jit(solution)/shard_map/ppermute | solution.py:417
  29.2 0.1 slice_reduce_fusion
  29.3 0.4 fusion.swap
  29.8 0.0 copy-start.1
  29.8 0.8 reshape.112
  30.6 0.1 reshape_squeeze.3
  30.7 0.1 broadcast_in_dim.36
  30.8 0.9 broadcast_in_dim_reshape.5
  31.7 0.0 copy-start.7
  31.7 0.0 copy-start.8
  31.7 0.1 pad.4.clone
  31.8 0.0 collective-permute-done.2.refs_3_
  31.8 4.3 %collective-permute-start.3 = (bf16[48,1408]{1,0:T(8,128)(2,1)S(1)}, bf16[48,1408]{1,0:T(8,128)(2,1)S(1)}, u32[]{:S(2)}, u32[]{:S(2)}) collective-permute-start(bf16[48,1408]{1,0:T(8,128)(2,1)S(1)} %collective-permute-done.2.refs_3_), channel_id=1, source_target_pairs={{0,14},{2,0},{4,2},{6,4},{8,6},{10,8},{12,10},{14,12},{1,15},{3,1}... | collective-permute-start | bytes 405512 | tf_op jit(solution)/shard_map/ppermute | solution.py:417
  36.1 1.0 multiply_sine_fusion
  37.1 0.0 collective-permute-done.refs_2_
  37.1 1.9 %collective-permute-start.1 = (bf16[48,1408]{1,0:T(8,128)(2,1)S(1)}, bf16[48,1408]{1,0:T(8,128)(2,1)S(1)}, u32[]{:S(2)}, u32[]{:S(2)}) collective-permute-start(bf16[48,1408]{1,0:T(8,128)(2,1)S(1)} %collective-permute-done.refs_2_), channel_id=1, source_target_pairs={{0,4},{2,6},{4,8},{6,10},{8,12},{10,14},{12,0},{14,2},{1,5},{3,7},... | collective-permute-start | bytes 405512 | tf_op jit(solution)/shard_map/ppermute | solution.py:417
  39.0 4.6 %collective-permute-start.6 = (bf16[48,1408]{1,0:T(8,128)(2,1)S(1)}, bf16[48,1408]{1,0:T(8,128)(2,1)S(1)}, u32[]{:S(2)}, u32[]{:S(2)}) collective-permute-start(bf16[48,1408]{1,0:T(8,128)(2,1)S(1)} %collective-permute-done.refs_2_), channel_id=1, source_target_pairs={{0,2},{2,4},{4,6},{6,8},{8,10},{10,12},{12,14},{14,0},{1,3},{3,5},... | collective-permute-start | bytes 405512 | tf_op jit(solution)/shard_map/ppermute | solution.py:417
  43.7 0.0 collective-permute-done.3.refs_2_
  43.7 0.0 collective-permute-done.4.refs_1_
  43.7 0.0 collective-permute-done.5.refs_4_
  43.7 0.9 shard_map.133.refs_0_
  44.6 1.9 %collective-permute-start.7 = (bf16[240,1408]{1,0:T(8,128)(2,1)S(1)}, bf16[240,1408]{1,0:T(8,128)(2,1)S(1)}, u32[]{:S(2)}, u32[]{:S(2)}) collective-permute-start(bf16[240,1408]{1,0:T(8,128)(2,1)S(1)} %shard_map.133.refs_0_), channel_id=1, source_target_pairs={{0,1},{1,0},{2,3},{3,2},{4,5},{5,4},{6,7},{7,6},{8,9},{9,8},{10,11... | collective-permute-start | bytes 2027528 | tf_op jit(solution)/shard_map/ppermute | solution.py:431
  46.6 0.0 copy-done.7
  46.6 0.0 copy-done.8
  46.6 0.2 pad_maximum_fusion.1.extra
  46.8 0.0 copy-done.1
  46.8 0.4 shard_map.131.w
  47.2 0.1 pad_maximum_fusion.table
  47.2 5.5 %collective-permute-done.1.refs_1_ = bf16[48,1408]{1,0:T(8,128)(2,1)S(1)} collective-permute-done((bf16[48,1408]{1,0:T(8,128)(2,1)S(1)}, bf16[48,1408]{1,0:T(8,128)(2,1)S(1)}, u32[]{:S(2)}, u32[]{:S(2)}) %collective-permute-start.1) | collective-permute-done | bytes 135200 | tf_op jit(solution)/shard_map/ppermute | solution.py:417
  52.7 2.6 %collective-permute-done.6.refs_0_ = bf16[48,1408]{1,0:T(8,128)(2,1)S(1)} collective-permute-done((bf16[48,1408]{1,0:T(8,128)(2,1)S(1)}, bf16[48,1408]{1,0:T(8,128)(2,1)S(1)}, u32[]{:S(2)}, u32[]{:S(2)}) %collective-permute-start.6) | collective-permute-done | bytes 135200 | tf_op jit(solution)/shard_map/ppermute | solution.py:417
  55.4 0.5 shard_map.134.refs_1_
  55.9 0.0 copy-start.9
  55.9 0.0 copy-start.4
  55.9 2.1 %collective-permute-start.8 = (bf16[144,1408]{1,0:T(8,128)(2,1)S(1)}, bf16[144,1408]{1,0:T(8,128)(2,1)S(1)}, u32[]{:S(2)}, u32[]{:S(2)}) collective-permute-start(bf16[144,1408]{1,0:T(8,128)(2,1)S(1)} %shard_map.134.refs_1_), channel_id=1, source_target_pairs={{0,1},{1,0},{2,3},{3,2},{4,5},{5,4},{6,7},{7,6},{8,9},{9,8},{10,11... | collective-permute-start | bytes 1216520 | tf_op jit(solution)/shard_map/ppermute | solution.py:431
  58.0 1.7 collective-permute-done.8.refs_3_
  59.7 0.0 collective-permute-done.7.refs_2_
  59.7 5.7 %shard_map.135 = (bf16[16,48,128]{2,1,0:T(8,128)(2,1)}, bf16[512,768]{1,0:T(8,128)(2,1)}, f32[8,768]{1,0:T(8,128)}) custom-call(bf16[1408,384]{1,0:T(8,128)(2,1)S(1)} %shard_map.131.w, bf16[768,768]{1,0:T(8,128)(2,1)S(1)} %fusion.swap, bf16[16,48,128]{2,1,0:T(8,128)(2,1)S(1)} %pad_maximum_fusion.1.extra, bf16[240,1408]{1,0:T(8,128)(2,1)S(1)} %shard_map.133.refs_0_, ...), custom_call_target="tpu_custom_call" | custom-call | flops 1782579200 | bytes 8388608 | tf_op jit(solution)/shard_map/pallas_call | solution.py:230
  65.4 0.0 copy-done.2
  65.4 7.5 %all-to-all-start = ((bf16[16,48,128]{2,1,0:T(8,128)(2,1)}), bf16[16,48,128]{2,1,0:T(8,128)(2,1)S(1)}, u32[]{:S(2)}, u32[]{:S(2)}) async-start(bf16[16,48,128]{2,1,0:T(8,128)(2,1)} %get-tuple-element.33), calls=%async_computation | async-start | bytes 393216 | tf_op jit(solution)/shard_map/all_to_all | solution.py:409
  73.0 0.0 copy-done.9
  73.0 8.5 %all-to-all-done.came = bf16[16,48,128]{2,1,0:T(8,128)(2,1)S(1)} async-done(((bf16[16,48,128]{2,1,0:T(8,128)(2,1)}), bf16[16,48,128]{2,1,0:T(8,128)(2,1)S(1)}, u32[]{:S(2)}, u32[]{:S(2)}) %all-to-all-start) | async-done | bytes 196640 | tf_op jit(solution)/shard_map/all_to_all | solution.py:409
  81.5 0.0 copy-done.4
  81.5 0.0 copy-start.6
  81.5 7.0 %shard_map.136 = (bf16[256,512]{1,0:T(8,128)(2,1)}, bf16[48,512]{1,0:T(8,128)(2,1)S(1)}) custom-call(bf16[16,48,128]{2,1,0:T(8,128)(2,1)S(1)} %all-to-all-done.came, bf16[16,352,512]{2,1,0:T(8,128)(2,1)} %bitcast.22, bf16[256,512]{1,0:T(8,128)(2,1)} %bitcast.24, bf16[1,512]{1,0:T(2,128)(2,1)S(1)} %broadcast_in_dim.38.mask, f32[1,512]{1,0:T(1,128)S(1)} %bitcast.18, ...), custom_call_target="tpu_custom_call" | custom-call | flops 2411724800 | bytes 8388608 | tf_op jit(solution)/shard_map/pallas_call | solution.py:313
  88.5 18.3 %all_gather.11.dvis = bf16[768,512]{1,0:T(8,128)(2,1)S(1)} all-gather(bf16[48,512]{1,0:T(8,128)(2,1)S(1)} %get-tuple-element.37), channel_id=1, replica_groups=mesh['y'=8,'x'=4,'z'=8,'core'=2] {'z','core'}, dimensions={0}, use_global_device_ids=true | all-gather | bytes 835584 | tf_op jit(solution)/shard_map/all_gather | solution.py:483
  106.9 0.0 copy-done.3
  106.9 0.0 copy-done.5
  106.9 0.0 copy-done.6
  106.9 4.8 %shard_map.137 = bf16[3328,128]{1,0:T(8,128)(2,1)S(1)} custom-call(bf16[768,512]{1,0:T(8,128)(2,1)S(1)} %all_gather.11.dvis, bf16[96,512]{1,0:T(8,128)(2,1)S(1)} %get-tuple-element.38.w_oe, bf16[768,768]{1,0:T(8,128)(2,1)S(1)} %fusion.swap, bf16[512,768]{1,0:T(8,128)(2,1)S(1)} %copy-done.5, f32[8,768]{1,0:T(8,128)S(1)} %copy-done.6, ...), custom_call_target="tpu_custom_call" | custom-call | flops 2621440000 | bytes 8388608 | tf_op jit(solution)/shard_map/pallas_call | solution.py:371
  111.7 17.5 %all_to_all.25 = bf16[4,832,128]{2,1,0:T(8,128)(2,1)S(1)} all-to-all(bf16[4,832,128]{2,1,0:T(8,128)(2,1)S(1)} %bitcast.16), channel_id=1, replica_groups=mesh['y'=8,'x'=4,'z'=8,'core'=2] {'x'}, dimensions={0} | all-to-all | bytes 1703936 | tf_op jit(solution)/shard_map/all_to_all | solution.py:409
  129.2 0.2 reduce_sum.24
  129.4 16.8 %all_to_all.26 = bf16[8,104,128]{2,1,0:T(8,128)(2,1)S(1)} all-to-all(bf16[8,104,128]{2,1,0:T(8,128)(2,1)S(1)} %bitcast.19), channel_id=1, replica_groups=mesh['y'=8,'x'=4,'z'=8,'core'=2] {'y'}, dimensions={0} | all-to-all | bytes 425984 | tf_op jit(solution)/shard_map/all_to_all | solution.py:409
  146.3 12.4 %all_to_all.27 = bf16[8,104,128]{2,1,0:T(8,128)(2,1)S(1)} all-to-all(bf16[8,104,128]{2,1,0:T(8,128)(2,1)S(1)} %broadcast_in_dim.41), channel_id=1, replica_groups=mesh['y'=8,'x'=4,'z'=8,'core'=2] {'y'}, dimensions={0} | all-to-all | bytes 425984 | tf_op jit(solution)/shard_map/all_to_all | solution.py:409
  158.7 0.1 broadcast_in_dim.43
  158.8 12.4 %all_to_all.28 = bf16[4,832,128]{2,1,0:T(8,128)(2,1)S(1)} all-to-all(bf16[4,832,128]{2,1,0:T(8,128)(2,1)S(1)} %broadcast_in_dim.43), channel_id=1, replica_groups=mesh['y'=8,'x'=4,'z'=8,'core'=2] {'x'}, dimensions={0} | all-to-all | bytes 1703936 | tf_op jit(solution)/shard_map/all_to_all | solution.py:409
  171.1 0.0 copy-done
  171.1 1.5 shard_map.138
  (14 shorter events, 0.1 us)
Async XLA Ops:
  7.2 74.3 %all-gather.3.cloned.1.call-start = ((), (), s32[]{:S(2)}) async-start(), calls=%async_computation.5 | async-start | bytes 6127616 | tf_op jit(solution)/shard_map/all_gather | solution.py:457
  11.3 25.8 %collective-permute-start = (bf16[48,1408]{1,0:T(8,128)(2,1)S(1)}, bf16[48,1408]{1,0:T(8,128)(2,1)S(1)}, u32[]{:S(2)}, u32[]{:S(2)}) collective-permute-start(bf16[48,1408]{1,0:T(8,128)(2,1)S(1)} %get-tuple-element.30.refs_0_), channel_id=1, source_target_pairs={{0,4},{2,6},{4,8},{6,10},{8,12},{10,14},{12,0},{14,2},{1,5},{3,7},... | collective-permute-start | bytes 405512 | tf_op jit(solution)/shard_map/ppermute | solution.py:417
  17.4 14.4 %collective-permute-start.2 = (bf16[48,1408]{1,0:T(8,128)(2,1)S(1)}, bf16[48,1408]{1,0:T(8,128)(2,1)S(1)}, u32[]{:S(2)}, u32[]{:S(2)}) collective-permute-start(bf16[48,1408]{1,0:T(8,128)(2,1)S(1)} %get-tuple-element.30.refs_0_), channel_id=1, source_target_pairs={{0,12},{2,14},{4,0},{6,2},{8,4},{10,6},{12,8},{14,10},{1,13},{3,15... | collective-permute-start | bytes 405512 | tf_op jit(solution)/shard_map/ppermute | solution.py:417
  23.3 20.4 %collective-permute-start.4 = (bf16[48,1408]{1,0:T(8,128)(2,1)S(1)}, bf16[48,1408]{1,0:T(8,128)(2,1)S(1)}, u32[]{:S(2)}, u32[]{:S(2)}) collective-permute-start(bf16[48,1408]{1,0:T(8,128)(2,1)S(1)} %get-tuple-element.30.refs_0_), channel_id=1, source_target_pairs={{0,2},{2,4},{4,6},{6,8},{8,10},{10,12},{12,14},{14,0},{1,3},{3,5},... | collective-permute-start | bytes 405512 | tf_op jit(solution)/shard_map/ppermute | solution.py:417
  25.2 18.5 %collective-permute-start.5 = (bf16[48,1408]{1,0:T(8,128)(2,1)S(1)}, bf16[48,1408]{1,0:T(8,128)(2,1)S(1)}, u32[]{:S(2)}, u32[]{:S(2)}) collective-permute-start(bf16[48,1408]{1,0:T(8,128)(2,1)S(1)} %get-tuple-element.30.refs_0_), channel_id=1, source_target_pairs={{0,14},{2,0},{4,2},{6,4},{8,6},{10,8},{12,10},{14,12},{1,15},{3,1}... | collective-permute-start | bytes 405512 | tf_op jit(solution)/shard_map/ppermute | solution.py:417
  29.8 17.0 %copy-start.1 = (bf16[3,1408,88]{1,2,0:T(8,128)(2,1)S(1)}, bf16[3,1408,88]{1,2,0:T(8,128)(2,1)}, u32[]{:S(2)}) copy-start(bf16[3,1408,88]{1,2,0:T(8,128)(2,1)} %param.15) | copy-start | bytes 2230276
  31.7 14.9 %copy-start.7 = (bf16[16,48,32]{2,1,0:T(8,128)(2,1)S(1)}, bf16[16,48,32]{2,1,0:T(8,128)(2,1)}, u32[]{:S(2)}) copy-start(bf16[16,48,32]{2,1,0:T(8,128)(2,1)} %reshape.112) | copy-start | bytes 147460
  31.7 14.9 %copy-start.8 = (bf16[16,48,1]{2,1,0:T(8,128)(2,1)S(1)}, bf16[16,48,1]{2,1,0:T(8,128)(2,1)}, u32[]{:S(2)}) copy-start(bf16[16,48,1]{2,1,0:T(8,128)(2,1)} %broadcast_in_dim_reshape.5) | copy-start | bytes 4612
  31.8 11.9 %collective-permute-start.3 = (bf16[48,1408]{1,0:T(8,128)(2,1)S(1)}, bf16[48,1408]{1,0:T(8,128)(2,1)S(1)}, u32[]{:S(2)}, u32[]{:S(2)}) collective-permute-start(bf16[48,1408]{1,0:T(8,128)(2,1)S(1)} %collective-permute-done.2.refs_3_), channel_id=1, source_target_pairs={{0,14},{2,0},{4,2},{6,4},{8,6},{10,8},{12,10},{14,12},{1,15},{3,1}... | collective-permute-start | bytes 405512 | tf_op jit(solution)/shard_map/ppermute | solution.py:417
  37.1 15.6 %collective-permute-start.1 = (bf16[48,1408]{1,0:T(8,128)(2,1)S(1)}, bf16[48,1408]{1,0:T(8,128)(2,1)S(1)}, u32[]{:S(2)}, u32[]{:S(2)}) collective-permute-start(bf16[48,1408]{1,0:T(8,128)(2,1)S(1)} %collective-permute-done.refs_2_), channel_id=1, source_target_pairs={{0,4},{2,6},{4,8},{6,10},{8,12},{10,14},{12,0},{14,2},{1,5},{3,7},... | collective-permute-start | bytes 405512 | tf_op jit(solution)/shard_map/ppermute | solution.py:417
  39.0 16.3 %collective-permute-start.6 = (bf16[48,1408]{1,0:T(8,128)(2,1)S(1)}, bf16[48,1408]{1,0:T(8,128)(2,1)S(1)}, u32[]{:S(2)}, u32[]{:S(2)}) collective-permute-start(bf16[48,1408]{1,0:T(8,128)(2,1)S(1)} %collective-permute-done.refs_2_), channel_id=1, source_target_pairs={{0,2},{2,4},{4,6},{6,8},{8,10},{10,12},{12,14},{14,0},{1,3},{3,5},... | collective-permute-start | bytes 405512 | tf_op jit(solution)/shard_map/ppermute | solution.py:417
  44.6 15.0 %collective-permute-start.7 = (bf16[240,1408]{1,0:T(8,128)(2,1)S(1)}, bf16[240,1408]{1,0:T(8,128)(2,1)S(1)}, u32[]{:S(2)}, u32[]{:S(2)}) collective-permute-start(bf16[240,1408]{1,0:T(8,128)(2,1)S(1)} %shard_map.133.refs_0_), channel_id=1, source_target_pairs={{0,1},{1,0},{2,3},{3,2},{4,5},{5,4},{6,7},{7,6},{8,9},{9,8},{10,11... | collective-permute-start | bytes 2027528 | tf_op jit(solution)/shard_map/ppermute | solution.py:431
  55.9 17.1 %copy-start.9 = (bf16[512]{0:T(512)(128)(2,1)S(1)}, bf16[512]{0:T(512)(128)(2,1)}, u32[]{:S(2)}) copy-start(bf16[512]{0:T(512)(128)(2,1)} %param.18) | copy-start | bytes 3076
  55.9 25.6 %copy-start.4 = (f32[512]{0:T(512)S(1)}, f32[512]{0:T(512)}, u32[]{:S(2)}) copy-start(f32[512]{0:T(512)} %param.19) | copy-start | bytes 6148
  55.9 3.8 %collective-permute-start.8 = (bf16[144,1408]{1,0:T(8,128)(2,1)S(1)}, bf16[144,1408]{1,0:T(8,128)(2,1)S(1)}, u32[]{:S(2)}, u32[]{:S(2)}) collective-permute-start(bf16[144,1408]{1,0:T(8,128)(2,1)S(1)} %shard_map.134.refs_1_), channel_id=1, source_target_pairs={{0,1},{1,0},{2,3},{3,2},{4,5},{5,4},{6,7},{7,6},{8,9},{9,8},{10,11... | collective-permute-start | bytes 1216520 | tf_op jit(solution)/shard_map/ppermute | solution.py:431
  59.7 5.7 %copy-start.2 = (bf16[240,1408]{1,0:T(8,128)(2,1)}, bf16[240,1408]{1,0:T(8,128)(2,1)S(1)}, u32[]{:S(2)}) copy-start(bf16[240,1408]{1,0:T(8,128)(2,1)S(1)} %collective-permute-done.7.refs_2_) | copy-start | bytes 2027524
  65.4 16.1 %all-to-all-start = ((bf16[16,48,128]{2,1,0:T(8,128)(2,1)}), bf16[16,48,128]{2,1,0:T(8,128)(2,1)S(1)}, u32[]{:S(2)}, u32[]{:S(2)}) async-start(bf16[16,48,128]{2,1,0:T(8,128)(2,1)} %get-tuple-element.33), calls=%async_computation | async-start | bytes 393216 | tf_op jit(solution)/shard_map/all_to_all | solution.py:409
  81.5 25.4 %copy-start.3 = (bf16[240,1408]{1,0:T(8,128)(2,1)S(1)}, bf16[240,1408]{1,0:T(8,128)(2,1)}, u32[]{:S(2)}) copy-start(bf16[240,1408]{1,0:T(8,128)(2,1)} %copy-done.2) | copy-start | bytes 2027524
  81.5 25.4 %copy-start.5 = (bf16[512,768]{1,0:T(8,128)(2,1)S(1)}, bf16[512,768]{1,0:T(8,128)(2,1)}, u32[]{:S(2)}) copy-start(bf16[512,768]{1,0:T(8,128)(2,1)} %get-tuple-element.39.saved) | copy-start | bytes 2359300
  81.5 25.4 %copy-start.6 = (f32[8,768]{1,0:T(8,128)S(1)}, f32[8,768]{1,0:T(8,128)}, u32[]{:S(2)}) copy-start(f32[8,768]{1,0:T(8,128)} %get-tuple-element.40.stats) | copy-start | bytes 73732
  158.7 12.5 %copy-start = (bf16[1408,512]{1,0:T(8,128)(2,1)S(1)}, bf16[1408,512]{1,0:T(8,128)(2,1)}, u32[]{:S(2)}) copy-start(bf16[1408,512]{1,0:T(8,128)(2,1)} %w_e2d.3) | copy-start | bytes 4325380
Sparse Core Ops, SparseCore 0:
  11.4 60.7 all-gather.2

commit v6 on v5

--- a/solution.py
+++ b/solution.py
@@ -1,5 +1,3 @@
-import functools
-
 import jax
 import jax.numpy as jnp
 from jax import lax
@@ -169,27 +167,16 @@
     )(*blocks)
 
 
-def row_loads(rows_in, xs, sems, first):
-    copies = []
-    for d in range(2):
-        near, far = rows_in[2 * d], rows_in[2 * d + 1]
-        for source, start, place, count in ((near, 0, 0, 3), (near, 3, 6, 2), (far, 0, 3, 3)):
-            copies.append(pltpu.make_async_copy(
-                source.at[pl.ds(CAP * start, CAP * count)],
-                xs.at[pl.ds(CAP * (NZ * d + place), CAP * count)], sems.at[first + len(copies)]))
-    return copies
-
-
-def attend_body(w, swap, extra, *refs):
-    rows_in, (sent, saved, stats, xs, out, keep, keep_stats, sems) = refs[:4], refs[4:]
+def attend_body(mine, other, w, swap, extra, sent, saved, stats, xs, out, keep, keep_stats, sems):
     half = ROWS // 2
-    loads = row_loads(rows_in, xs, sems, 6)
+    loads = [
+        pltpu.make_async_copy(mine, xs.at[pl.ds(0, half)], sems.at[0]),
+        pltpu.make_async_copy(other, xs.at[pl.ds(half, half)], sems.at[1])]
     for load in loads:
         load.start()
     parts = []
     for i in range(2):
-        for load in loads[3 * i:3 * (i + 1)]:
-            load.wait()
+        loads[i].wait()
         parts.append(dot(xs[half * i:half * (i + 1), :], w[...]))
     qkv = jnp.concatenate(parts, axis=0)
     k_rows = qkv[:, HL:2 * HL].astype(BF16)
@@ -214,7 +201,8 @@
     sums = pltpu.make_async_copy(keep_stats, stats, sems.at[3])
     sums.start()
     ctx = jnp.concatenate(ctx, axis=1).astype(BF16)
-    out[...] = dot_nt(swap[...], ctx).astype(BF16).reshape(16, CAP, 128) + extra[...]
+    out[:, 0:CAP, :] = dot_nt(swap[...], ctx).astype(BF16).reshape(16, CAP, 128)
+    out[:, CAP:, :] = extra[...]
     send = pltpu.make_async_copy(out, sent, sems.at[4])
     send.start()
     keep[3 * HL:, :] = dot_nt(ctx, swap[...]).astype(BF16)
@@ -229,11 +217,11 @@
     hbm = pl.BlockSpec(memory_space=pltpu.HBM)
     return pl.pallas_call(
         attend_body,
-        out_shape=[pltpu.HBM((16, CAP, 128), BF16), pltpu.HBM((4 * HL, ROWS), BF16), pltpu.HBM((8, ROWS), F32)],
-        in_specs=[vmem] * 3 + [hbm] * 4,
+        out_shape=[pltpu.HBM((16, 64, 128), BF16), pltpu.HBM((4 * HL, ROWS), BF16), pltpu.HBM((8, ROWS), F32)],
+        in_specs=[hbm, hbm, vmem, vmem, vmem],
         out_specs=[hbm, hbm, hbm],
-        scratch_shapes=[pltpu.VMEM((ROWS, args[0].shape[0]), BF16), pltpu.VMEM((16, CAP, 128), BF16),
-                        pltpu.VMEM((4 * HL, ROWS), BF16), pltpu.VMEM((8, ROWS), F32), pltpu.SemaphoreType.DMA((12,))],
+        scratch_shapes=[pltpu.VMEM((ROWS, args[0].shape[1]), BF16), pltpu.VMEM((16, 64, 128), BF16),
+                        pltpu.VMEM((4 * HL, ROWS), BF16), pltpu.VMEM((8, ROWS), F32), pltpu.SemaphoreType.DMA((6,))],
         compiler_params=pltpu.CompilerParams(vmem_limit_bytes=24 << 20),
         cost_estimate=pl.CostEstimate(flops=1700 << 20, bytes_accessed=8 << 20, transcendentals=1 << 20),
     )(*args)
@@ -248,24 +236,24 @@
     up = pltpu.make_async_copy(cot, cots, sems.at[3])
     for copy in (loads[0], up, *loads[1:]):
         copy.start()
-    flat = came[...].reshape(16 * CAP, 128)
+    flat = came[...].reshape(16 * 64, 128)
     vis = jnp.zeros((CAP, DD), F32)
     loads[0].wait()
     for g in range(16):
         vis += dot(came[g, 0:CAP, 0:HP], w_oe[g])
-    row = lax.broadcasted_iota(jnp.int32, (CAP, 16 * CAP), 0)
-    col = lax.broadcasted_iota(jnp.int32, (CAP, 16 * CAP), 1)
-    own = ((col >= 16 * row) & (col < 16 * row + 16)).astype(F32).astype(BF16)
-    lane_in = lax.broadcasted_iota(jnp.int32, (128, DD), 0) - HP
-    lane_out = lax.broadcasted_iota(jnp.int32, (128, DD), 1)
-    repeat = (lane_in == (lane_out & 31)).astype(F32).astype(BF16)
-    turn_of = lax.broadcasted_iota(jnp.int32, (16 * CAP, DD), 0) & 15
-    piece = lax.shift_right_logical(lax.broadcasted_iota(jnp.int32, (16 * CAP, DD), 1), 5)
-    laid = jnp.where(turn_of == piece, dot(flat, repeat), 0.0).astype(BF16)
-    vis = (vis + dot(own, laid)).astype(BF16)
-    spots = dot((col == 16 * row).astype(F32).astype(BF16), flat)
+    row = lax.broadcasted_iota(jnp.int32, (CAP, 1024), 0)
+    col = lax.broadcasted_iota(jnp.int32, (CAP, 1024), 1)
+    source = jnp.zeros((CAP, 1024), jnp.int32)
+    for g in range(1, 16):
+        source += (row >= SLOTS * g).astype(jnp.int32)
+    slot = row - SLOTS * source
+    base = 64 * source + CAP
+    x_part = jnp.concatenate(
+        [dot((col == base + 4 * slot + i).astype(F32).astype(BF16), flat) for i in range(4)], axis=1)
+    vis = (vis + x_part).astype(BF16)
+    spots = dot((col == base + 12).astype(F32).astype(BF16), flat)
     lane = lax.broadcasted_iota(jnp.int32, (CAP, 128), 1)
-    spot = jnp.sum(jnp.where(lane == HD, spots, 0.0), axis=1, keepdims=True)
+    spot = jnp.sum(jnp.where(lane == slot[:, 0:128], spots, 0.0), axis=1, keepdims=True)
     spot = jnp.concatenate([spot, jnp.full((128 - CAP, 1), -1.0, F32)], axis=0)
     vis = jnp.concatenate([vis.astype(F32), jnp.zeros((128 - CAP, DD), F32)], axis=0).astype(BF16)
     where_col = lax.broadcasted_iota(jnp.int32, (128, FDEV), 1).astype(F32)
@@ -324,11 +312,12 @@
       pltpu.with_memory_space_constraint(cot, pltpu.HBM), *args)
 
 
-def back_body(dvis, w_oe, swap, saved, stats, *refs):
-    rows_in, (parts, ds_all, pb_all, keep, keep_stats, xs, sems) = refs[:4], refs[4:]
+def back_body(dvis, w_oe, swap, saved, stats, mine, other, parts, ds_all, pb_all, keep, keep_stats, xs, sems):
     loads = [
         pltpu.make_async_copy(saved, keep, sems.at[0]),
-        pltpu.make_async_copy(stats, keep_stats, sems.at[1])] + row_loads(rows_in, xs, sems, 2)
+        pltpu.make_async_copy(stats, keep_stats, sems.at[1]),
+        pltpu.make_async_copy(mine, xs.at[pl.ds(0, ROWS // 2)], sems.at[2]),
+        pltpu.make_async_copy(other, xs.at[pl.ds(ROWS // 2, ROWS // 2)], sems.at[3])]
     for load in loads:
         load.start()
     dctx = dot(dot_nt(w_oe[...], dvis[...]).astype(BF16), swap[...])
@@ -365,20 +354,20 @@
     parts[...] = jnp.concatenate(pieces, axis=0).astype(BF16)
 
 
-def back(dvis, w_oe, swap, saved, stats, *rows_in):
+def back(dvis, w_oe, swap, saved, stats, mine, other):
     vmem = pl.BlockSpec(memory_space=pltpu.VMEM)
     hbm = pl.BlockSpec(memory_space=pltpu.HBM)
     return pl.pallas_call(
         back_body,
         out_shape=jax.ShapeDtypeStruct((GRAD_ROWS, 128), BF16),
-        in_specs=[vmem, vmem, vmem] + [hbm] * 6,
+        in_specs=[vmem, vmem, vmem, hbm, hbm, hbm, hbm],
         out_specs=vmem,
         scratch_shapes=[pltpu.VMEM((ROWS, ROWS), BF16), pltpu.VMEM((ROWS, ROWS), BF16),
                         pltpu.VMEM((4 * HL, ROWS), BF16), pltpu.VMEM((8, ROWS), F32),
-                        pltpu.VMEM((ROWS, rows_in[0].shape[1]), BF16), pltpu.SemaphoreType.DMA((8,))],
+                        pltpu.VMEM((ROWS, mine.shape[1]), BF16), pltpu.SemaphoreType.DMA((4,))],
         compiler_params=pltpu.CompilerParams(vmem_limit_bytes=24 << 20),
         cost_estimate=pl.CostEstimate(flops=2500 << 20, bytes_accessed=8 << 20, transcendentals=1 << 20),
-    )(dvis, w_oe, swap, saved, stats, *rows_in)
+    )(dvis, w_oe, swap, saved, stats, mine, other)
 
 
 def finish_body(total, w_e2d, grad_q, grad_o):
@@ -424,7 +413,7 @@
     got[3] = z_shift(got[2], 1)
     got[5] = z_shift(got[6], -1)
     got[4] = z_shift(got[2], 2)
-    return got
+    return [got[k] for k in range(NZ)]
 
 
 def swap_core(block):
@@ -446,7 +435,6 @@
     cotangent,
 ):
     me = lax.axis_index(SEQ)
-    my_z, my_c = me // 2, me % 2
     fdev = cotangent.shape[1]
     cot = cotangent[0]
     cap = keep_pos.shape[1]
@@ -456,10 +444,13 @@
     x_vis, w_oe_own, pack = pack_up(x_slot, w_out, w_e2d, fc_in, fc_out)
     weights = lax.all_gather(pack, SEQ, axis=0)
 
-    places = jnp.repeat(offsets[:, 0].reshape(16, SLOTS), 16, axis=1)[:, :, None]
+    blocks = around(xn_own)
+    blocks[4], spot, x_vis, offsets = lax.optimization_barrier((blocks[4], me, x_vis, offsets))
+    my_z, my_c = spot // 2, spot % 2
+
+    places = jnp.pad(offsets[:, 0].reshape(16, 1, SLOTS), ((0, 0), (0, 0), (0, 128 - SLOTS)))
     extra = jnp.concatenate(
-        [jnp.zeros((16, cap, HD), BF16), places, jnp.zeros((16, cap, HP - HD - 1), BF16), x_vis.reshape(16, cap, 32)],
-        axis=2)
+        [x_vis.reshape(16, 12, 128), places, jnp.zeros((16, 3, 128), BF16)], axis=1)
 
     tok = jnp.arange(rows, dtype=jnp.int32)
     block = tok // cap
@@ -467,21 +458,16 @@
     inside = tok % cap
     dest = inside // SLOTS * cap + source * SLOTS + inside % SLOTS
     swap = (dest[None, :] == tok[:, None]).astype(BF16)
-    table = position_table((me * fdev + jnp.arange(fdev, dtype=jnp.int32)).astype(F32), DD)
+    table = position_table((spot * fdev + jnp.arange(fdev, dtype=jnp.int32)).astype(F32), DD)
 
     w = turn(w_qkv.transpose(0, 2, 1).reshape(3 * HD, -1))
-    got = around(xn_own)
-    got[0], got[5] = lax.optimization_barrier((got[0], got[5]))
-    near = join([got[k] for k in (0, 1, 2, 6, 7)])
-    near_other = swap_core(near)
-    got[4], w, swap, extra, table = lax.optimization_barrier((got[4], w, swap, extra, table))
-    far = join([got[k] for k in (3, 4, 5)])
-    rows_in = (near, far, near_other, swap_core(far))
-    sent, saved, stats = attend(w, swap, extra, *rows_in)
+    mine = join(blocks)
+    other = swap_core(mine)
+    sent, saved, stats = attend(mine, other, w, swap, extra)
     came = exchange(sent, SEQ)
     recon, dvis_own = decode(came, weights, cot, mask_token[None], dec_gain[None], table)
     dvis = lax.all_gather(dvis_own, SEQ, axis=0, tiled=True)
-    parts = back(dvis, w_oe_own, swap, saved, stats, *rows_in)
+    parts = back(dvis, w_oe_own, swap, saved, stats, mine, other)
 
     parts = jnp.sum(exchange(parts.reshape(NX, 832, 128), "x").astype(F32), axis=0).astype(BF16)
     parts = jnp.sum(exchange(parts.reshape(NY, 104, 128), "y").astype(F32), axis=0).astype(BF16)

time: 180 us -> 180 us (level)
  waiting for transfers between devices: 18.4 us -> 20.5 us
    ppermute x7, waiting for transfers between devices: 8.14 us -> 12 us  [z_shift(): return lax.ppermute(block, 'z', [(z, (z + step) % NZ) for z in range(NZ)])]
    all_to_all x1, starting transfers between devices: 7.53 us -> 10.6 us  [exchange(): return lax.all_to_all(block, axis, 0, 0, tiled=True)]
    unnamed x20, local copies, waits for them, and re-layouts: 0.05 us -> 2.85 us
    ppermute x7, starting transfers between devices: 28.6 us -> 26.5 us  [z_shift(): return lax.ppermute(block, 'z', [(z, (z + step) % NZ) for z in range(NZ)])]
    ppermute x2 -> x1, starting transfers between devices: 3.97 us -> 1.92 us  [swap_core(): return lax.ppermute(block, 'core', [(0, 1), (1, 0)])]
  transfers between devices with their start and end apart: 11 -> 10, of which waited for: 4 -> 6; matrix products, arithmetic and copies ran while one was open for 2% -> 1% of each run, Pallas kernels for 4% -> 4%
where the time goes in v6:
time: 180 us; the launch traced here: 179 us
  blocking collectives  77.1 us (43%)
  starting transfers between devices  39 us (22%)
  Pallas kernels  23.4 us (13%)
  waiting for transfers between devices  20.5 us (11%)
  between operations  14.3 us (8%)
  local copies, waits for them, and re-layouts  3.35 us (2%)
  other arithmetic  1.81 us (1%)
    all_to_all x4, blocking collectives, exchange(): return lax.all_to_all(block, axis, 0, 0, tiled=True)  58.5 us
    ppermute x7, starting transfers between devices, z_shift(): return lax.ppermute(block, 'z', [(z, (z + step) % NZ) for z in range(NZ)])  26.5 us
    all_gather x1, blocking collectives, local(): dvis = lax.all_gather(dvis_own, SEQ, axis=0, tiled=True)  18.6 us
    ppermute x7, waiting for transfers between devices, z_shift(): return lax.ppermute(block, 'z', [(z, (z + step) % NZ) for z in range(NZ)])  12 us
    all_to_all x1, starting transfers between devices, exchange(): return lax.all_to_all(block, axis, 0, 0, tiled=True)  10.6 us
    all_to_all x1, waiting for transfers between devices, exchange(): return lax.all_to_all(block, axis, 0, 0, tiled=True)  8.55 us
    pallas_call x1, Pallas kernels, decode(): pl.pallas_call(decode_body, out_shape=[jax.ShapeDtypeStruct((FDEV, DD), B...  6.84 us
    pallas_call x1, Pallas kernels, attend(): pl.pallas_call(attend_body, out_shape=[pltpu.HBM((16, 64, 128), BF16), pl...  5.03 us
  transfers between devices with their start and end apart: 10, of which 6 were waited for; matrix products, arithmetic and copies ran while one was open for 1% of the time, Pallas kernels for 4%

profile of v6, /device:TPU:64, one launch (start us, length us, event | category | flops | bytes accessed | tf_op | source)
XLA Modules:
  0.0 179.5 jit_solution(15206501848897715758)
XLA Ops:
  7.2 0.0 all-gather.3.cloned.1.call-start
  7.2 1.3 shard_map.130
  8.5 2.7 %shard_map.131 = (bf16[48,512]{1,0:T(8,128)(2,1)S(1)}, bf16[96,512]{1,0:T(8,128)(2,1)S(1)}, bf16[352,512]{1,0:T(8,128)(2,1)}) custom-call(bf16[48,1408]{1,0:T(8,128)(2,1)S(1)} %get-tuple-element.21.x_slot, bf16[88,1408]{1,0:T(8,128)(2,1)} %w_out.1, bf16[1408,512]{1,0:T(8,128)(2,1)} %w_e2d.3, bf16[128,512]{1,0:T(8,128)(2,1)} %fc_in.1, bf16[128,512]{1,0:T(8,128)(2,1)} %fc_out.1), custom_call_target="tpu_custom_call" | custom-call | flops 209715200 | bytes 3145728 | tf_op jit(solution)/shard_map/pallas_call | solution.py:123
  11.3 0.0 all-gather.3.cloned.1.call-update
  11.3 6.1 %collective-permute-start.1 = (bf16[48,1408]{1,0:T(8,128)(2,1)S(1)}, bf16[48,1408]{1,0:T(8,128)(2,1)S(1)}, u32[]{:S(2)}, u32[]{:S(2)}) collective-permute-start(bf16[48,1408]{1,0:T(8,128)(2,1)S(1)} %get-tuple-element.20.refs_0_), channel_id=1, source_target_pairs={{0,4},{2,6},{4,8},{6,10},{8,12},{10,14},{12,0},{14,2},{1,5},{3,7},... | collective-permute-start | bytes 405512 | tf_op jit(solution)/shard_map/ppermute | solution.py:406
  17.4 5.9 %collective-permute-start.4 = (bf16[48,1408]{1,0:T(8,128)(2,1)S(1)}, bf16[48,1408]{1,0:T(8,128)(2,1)S(1)}, u32[]{:S(2)}, u32[]{:S(2)}) collective-permute-start(bf16[48,1408]{1,0:T(8,128)(2,1)S(1)} %get-tuple-element.20.refs_0_), channel_id=1, source_target_pairs={{0,12},{2,14},{4,0},{6,2},{8,4},{10,6},{12,8},{14,10},{1,13},{3,15... | collective-permute-start | bytes 405512 | tf_op jit(solution)/shard_map/ppermute | solution.py:406
  23.3 4.5 %collective-permute-done.1.refs_2_ = bf16[48,1408]{1,0:T(8,128)(2,1)S(1)} collective-permute-done((bf16[48,1408]{1,0:T(8,128)(2,1)S(1)}, bf16[48,1408]{1,0:T(8,128)(2,1)S(1)}, u32[]{:S(2)}, u32[]{:S(2)}) %collective-permute-start.1) | collective-permute-done | bytes 135200 | tf_op jit(solution)/shard_map/ppermute | solution.py:406
  27.8 1.9 %collective-permute-start.3 = (bf16[48,1408]{1,0:T(8,128)(2,1)S(1)}, bf16[48,1408]{1,0:T(8,128)(2,1)S(1)}, u32[]{:S(2)}, u32[]{:S(2)}) collective-permute-start(bf16[48,1408]{1,0:T(8,128)(2,1)S(1)} %collective-permute-done.1.refs_2_), channel_id=1, source_target_pairs={{0,4},{2,6},{4,8},{6,10},{8,12},{10,14},{12,0},{14,2},{1,5},{3,7},... | collective-permute-start | bytes 405512 | tf_op jit(solution)/shard_map/ppermute | solution.py:406
  29.7 4.5 %collective-permute-start = (bf16[48,1408]{1,0:T(8,128)(2,1)S(1)}, bf16[48,1408]{1,0:T(8,128)(2,1)S(1)}, u32[]{:S(2)}, u32[]{:S(2)}) collective-permute-start(bf16[48,1408]{1,0:T(8,128)(2,1)S(1)} %get-tuple-element.20.refs_0_), channel_id=1, source_target_pairs={{0,2},{2,4},{4,6},{6,8},{8,10},{10,12},{12,14},{14,0},{1,3},{3,5},... | collective-permute-start | bytes 405512 | tf_op jit(solution)/shard_map/ppermute | solution.py:406
  34.2 1.9 %collective-permute-start.6 = (bf16[48,1408]{1,0:T(8,128)(2,1)S(1)}, bf16[48,1408]{1,0:T(8,128)(2,1)S(1)}, u32[]{:S(2)}, u32[]{:S(2)}) collective-permute-start(bf16[48,1408]{1,0:T(8,128)(2,1)S(1)} %get-tuple-element.20.refs_0_), channel_id=1, source_target_pairs={{0,14},{2,0},{4,2},{6,4},{8,6},{10,8},{12,10},{14,12},{1,15},{3,1}... | collective-permute-start | bytes 405512 | tf_op jit(solution)/shard_map/ppermute | solution.py:406
  36.2 4.2 %collective-permute-start.2 = (bf16[48,1408]{1,0:T(8,128)(2,1)S(1)}, bf16[48,1408]{1,0:T(8,128)(2,1)S(1)}, u32[]{:S(2)}, u32[]{:S(2)}) collective-permute-start(bf16[48,1408]{1,0:T(8,128)(2,1)S(1)} %collective-permute-done.1.refs_2_), channel_id=1, source_target_pairs={{0,2},{2,4},{4,6},{6,8},{8,10},{10,12},{12,14},{14,0},{1,3},{3,5},... | collective-permute-start | bytes 405512 | tf_op jit(solution)/shard_map/ppermute | solution.py:406
  40.4 0.0 collective-permute-done.4.refs_6_
  40.4 1.9 %collective-permute-start.5 = (bf16[48,1408]{1,0:T(8,128)(2,1)S(1)}, bf16[48,1408]{1,0:T(8,128)(2,1)S(1)}, u32[]{:S(2)}, u32[]{:S(2)}) collective-permute-start(bf16[48,1408]{1,0:T(8,128)(2,1)S(1)} %collective-permute-done.4.refs_6_), channel_id=1, source_target_pairs={{0,14},{2,0},{4,2},{6,4},{8,6},{10,8},{12,10},{14,12},{1,15},{3,1}... | collective-permute-start | bytes 405512 | tf_op jit(solution)/shard_map/ppermute | solution.py:406
  42.4 0.0 collective-permute-done.3.refs_4_
  42.4 0.8 collective-permute-done.refs_1_
  43.1 0.9 collective-permute-done.6.refs_7_
  44.0 4.7 %collective-permute-done.2.refs_3_ = bf16[48,1408]{1,0:T(8,128)(2,1)S(1)} collective-permute-done((bf16[48,1408]{1,0:T(8,128)(2,1)S(1)}, bf16[48,1408]{1,0:T(8,128)(2,1)S(1)}, u32[]{:S(2)}, u32[]{:S(2)}) %collective-permute-start.2) | collective-permute-done | bytes 135200 | tf_op jit(solution)/shard_map/ppermute | solution.py:406
  48.7 1.1 collective-permute-done.5.refs_5_
  49.8 1.4 shard_map.132.mine
  51.3 1.9 %collective-permute-start.7 = (bf16[384,1408]{1,0:T(8,128)(2,1)S(1)}, bf16[384,1408]{1,0:T(8,128)(2,1)S(1)}, u32[]{:S(2)}, u32[]{:S(2)}) collective-permute-start(bf16[384,1408]{1,0:T(8,128)(2,1)S(1)} %shard_map.132.mine), channel_id=1, source_target_pairs={{0,1},{1,0},{2,3},{3,2},{4,5},{5,4},{6,7},{7,6},{8,9},{9,8},{10,11... | collective-permute-start | bytes 3244040 | tf_op jit(solution)/shard_map/ppermute | solution.py:420
  53.2 0.1 pad.9.clone
  53.3 0.0 copy-start.3
  53.3 1.1 copy-done.3
  54.4 0.4 shard_map.133.w
  54.8 0.0 copy-start.5
  54.8 1.0 copy-done.5
  55.8 0.1 reshape.112
  55.9 0.1 slice_reduce_fusion
  56.0 0.1 reshape_squeeze.4
  56.1 0.0 copy-start.6
  56.2 0.1 fusion.4.extra
  56.2 0.4 fusion.swap
  56.7 0.0 copy-start.9
  56.7 0.0 collective-permute-done.7.other
  56.7 0.7 copy-done.6
  57.3 0.0 copy-start.1
  57.4 5.0 %shard_map.134 = (bf16[16,64,128]{2,1,0:T(8,128)(2,1)}, bf16[512,768]{1,0:T(8,128)(2,1)}, f32[8,768]{1,0:T(8,128)}) custom-call(bf16[384,1408]{1,0:T(8,128)(2,1)S(1)} %shard_map.132.mine, bf16[384,1408]{1,0:T(8,128)(2,1)S(1)} %collective-permute-done.7.other, bf16[1408,384]{1,0:T(8,128)(2,1)S(1)} %copy-done.6, bf16[768,768]{1,0:T(8,128)(2,1)S(1)} %fusion.swap, ...), custom_call_target="tpu_custom_call" | custom-call | flops 1782579200 | bytes 8388608 | tf_op jit(solution)/shard_map/pallas_call | solution.py:218
  62.4 0.0 copy-done.1
  62.4 0.0 copy-start.4
  62.4 10.6 %all-to-all-start = ((bf16[16,64,128]{2,1,0:T(8,128)(2,1)}), bf16[16,64,128]{2,1,0:T(8,128)(2,1)S(1)}, u32[]{:S(2)}, u32[]{:S(2)}) async-start(bf16[16,64,128]{2,1,0:T(8,128)(2,1)} %get-tuple-element.28), calls=%async_computation | async-start | bytes 524288 | tf_op jit(solution)/shard_map/all_to_all | solution.py:398
  73.0 0.0 copy-done.9
  73.1 1.0 multiply_sine_fusion
  74.1 0.1 pad_maximum_fusion.table
  74.1 8.5 %all-to-all-done.came = bf16[16,64,128]{2,1,0:T(8,128)(2,1)S(1)} async-done(((bf16[16,64,128]{2,1,0:T(8,128)(2,1)}), bf16[16,64,128]{2,1,0:T(8,128)(2,1)S(1)}, u32[]{:S(2)}, u32[]{:S(2)}) %all-to-all-start) | async-done | bytes 262176 | tf_op jit(solution)/shard_map/all_to_all | solution.py:398
  82.7 0.0 all-gather.3.cloned.1.call-done
  82.7 0.0 copy-done.4
  82.7 0.0 copy-start.2
  82.7 0.0 copy-start.7
  82.7 0.0 copy-start.8
  82.7 6.8 %shard_map.135 = (bf16[256,512]{1,0:T(8,128)(2,1)}, bf16[48,512]{1,0:T(8,128)(2,1)S(1)}) custom-call(bf16[16,64,128]{2,1,0:T(8,128)(2,1)S(1)} %all-to-all-done.came, bf16[16,352,512]{2,1,0:T(8,128)(2,1)} %bitcast.22, bf16[256,512]{1,0:T(8,128)(2,1)} %bitcast.24, bf16[1,512]{1,0:T(2,128)(2,1)S(1)} %broadcast_in_dim.30.mask, f32[1,512]{1,0:T(1,128)S(1)} %bitcast.18, ...), custom_call_target="tpu_custom_call" | custom-call | flops 2411724800 | bytes 8388608 | tf_op jit(solution)/shard_map/pallas_call | solution.py:301
  89.5 18.6 %all_gather.11.dvis = bf16[768,512]{1,0:T(8,128)(2,1)S(1)} all-gather(bf16[48,512]{1,0:T(8,128)(2,1)S(1)} %get-tuple-element.31), channel_id=1, replica_groups=mesh['y'=8,'x'=4,'z'=8,'core'=2] {'z','core'}, dimensions={0}, use_global_device_ids=true | all-gather | bytes 835584 | tf_op jit(solution)/shard_map/all_gather | solution.py:469
  108.1 0.0 copy-done.2
  108.1 0.0 copy-done.7
  108.2 0.0 copy-done.8
  108.2 4.1 %shard_map.136 = bf16[3328,128]{1,0:T(8,128)(2,1)S(1)} custom-call(bf16[768,512]{1,0:T(8,128)(2,1)S(1)} %all_gather.11.dvis, bf16[96,512]{1,0:T(8,128)(2,1)S(1)} %get-tuple-element.32.w_oe, bf16[768,768]{1,0:T(8,128)(2,1)S(1)} %fusion.swap, bf16[512,768]{1,0:T(8,128)(2,1)S(1)} %copy-done.7, f32[8,768]{1,0:T(8,128)S(1)} %copy-done.8, ...), custom_call_target="tpu_custom_call" | custom-call | flops 2621440000 | bytes 8388608 | tf_op jit(solution)/shard_map/pallas_call | solution.py:360
  112.3 16.9 %all_to_all.25 = bf16[4,832,128]{2,1,0:T(8,128)(2,1)S(1)} all-to-all(bf16[4,832,128]{2,1,0:T(8,128)(2,1)S(1)} %bitcast.16), channel_id=1, replica_groups=mesh['y'=8,'x'=4,'z'=8,'core'=2] {'x'}, dimensions={0} | all-to-all | bytes 1703936 | tf_op jit(solution)/shard_map/all_to_all | solution.py:398
  129.1 0.2 reduce_sum.24
  129.3 16.9 %all_to_all.26 = bf16[8,104,128]{2,1,0:T(8,128)(2,1)S(1)} all-to-all(bf16[8,104,128]{2,1,0:T(8,128)(2,1)S(1)} %bitcast.19), channel_id=1, replica_groups=mesh['y'=8,'x'=4,'z'=8,'core'=2] {'y'}, dimensions={0} | all-to-all | bytes 425984 | tf_op jit(solution)/shard_map/all_to_all | solution.py:398
  146.3 12.4 %all_to_all.27 = bf16[8,104,128]{2,1,0:T(8,128)(2,1)S(1)} all-to-all(bf16[8,104,128]{2,1,0:T(8,128)(2,1)S(1)} %broadcast_in_dim.33), channel_id=1, replica_groups=mesh['y'=8,'x'=4,'z'=8,'core'=2] {'y'}, dimensions={0} | all-to-all | bytes 425984 | tf_op jit(solution)/shard_map/all_to_all | solution.py:398
  158.6 0.0 copy-start
  158.6 0.1 broadcast_in_dim.35
  158.8 12.4 %all_to_all.28 = bf16[4,832,128]{2,1,0:T(8,128)(2,1)S(1)} all-to-all(bf16[4,832,128]{2,1,0:T(8,128)(2,1)S(1)} %broadcast_in_dim.35), channel_id=1, replica_groups=mesh['y'=8,'x'=4,'z'=8,'core'=2] {'x'}, dimensions={0} | all-to-all | bytes 1703936 | tf_op jit(solution)/shard_map/all_to_all | solution.py:398
  171.1 0.0 copy-done
  171.1 1.5 shard_map.137
  (7 shorter events, 0.1 us)
Async XLA Ops:
  7.2 75.5 %all-gather.3.cloned.1.call-start = ((), (), s32[]{:S(2)}) async-start(), calls=%async_computation.5 | async-start | bytes 6127616 | tf_op jit(solution)/shard_map/all_gather | solution.py:445
  11.3 16.5 %collective-permute-start.1 = (bf16[48,1408]{1,0:T(8,128)(2,1)S(1)}, bf16[48,1408]{1,0:T(8,128)(2,1)S(1)}, u32[]{:S(2)}, u32[]{:S(2)}) collective-permute-start(bf16[48,1408]{1,0:T(8,128)(2,1)S(1)} %get-tuple-element.20.refs_0_), channel_id=1, source_target_pairs={{0,4},{2,6},{4,8},{6,10},{8,12},{10,14},{12,0},{14,2},{1,5},{3,7},... | collective-permute-start | bytes 405512 | tf_op jit(solution)/shard_map/ppermute | solution.py:406
  17.4 23.0 %collective-permute-start.4 = (bf16[48,1408]{1,0:T(8,128)(2,1)S(1)}, bf16[48,1408]{1,0:T(8,128)(2,1)S(1)}, u32[]{:S(2)}, u32[]{:S(2)}) collective-permute-start(bf16[48,1408]{1,0:T(8,128)(2,1)S(1)} %get-tuple-element.20.refs_0_), channel_id=1, source_target_pairs={{0,12},{2,14},{4,0},{6,2},{8,4},{10,6},{12,8},{14,10},{1,13},{3,15... | collective-permute-start | bytes 405512 | tf_op jit(solution)/shard_map/ppermute | solution.py:406
  27.8 14.6 %collective-permute-start.3 = (bf16[48,1408]{1,0:T(8,128)(2,1)S(1)}, bf16[48,1408]{1,0:T(8,128)(2,1)S(1)}, u32[]{:S(2)}, u32[]{:S(2)}) collective-permute-start(bf16[48,1408]{1,0:T(8,128)(2,1)S(1)} %collective-permute-done.1.refs_2_), channel_id=1, source_target_pairs={{0,4},{2,6},{4,8},{6,10},{8,12},{10,14},{12,0},{14,2},{1,5},{3,7},... | collective-permute-start | bytes 405512 | tf_op jit(solution)/shard_map/ppermute | solution.py:406
  29.7 13.4 %collective-permute-start = (bf16[48,1408]{1,0:T(8,128)(2,1)S(1)}, bf16[48,1408]{1,0:T(8,128)(2,1)S(1)}, u32[]{:S(2)}, u32[]{:S(2)}) collective-permute-start(bf16[48,1408]{1,0:T(8,128)(2,1)S(1)} %get-tuple-element.20.refs_0_), channel_id=1, source_target_pairs={{0,2},{2,4},{4,6},{6,8},{8,10},{10,12},{12,14},{14,0},{1,3},{3,5},... | collective-permute-start | bytes 405512 | tf_op jit(solution)/shard_map/ppermute | solution.py:406
  34.2 9.8 %collective-permute-start.6 = (bf16[48,1408]{1,0:T(8,128)(2,1)S(1)}, bf16[48,1408]{1,0:T(8,128)(2,1)S(1)}, u32[]{:S(2)}, u32[]{:S(2)}) collective-permute-start(bf16[48,1408]{1,0:T(8,128)(2,1)S(1)} %get-tuple-element.20.refs_0_), channel_id=1, source_target_pairs={{0,14},{2,0},{4,2},{6,4},{8,6},{10,8},{12,10},{14,12},{1,15},{3,1}... | collective-permute-start | bytes 405512 | tf_op jit(solution)/shard_map/ppermute | solution.py:406
  36.2 12.6 %collective-permute-start.2 = (bf16[48,1408]{1,0:T(8,128)(2,1)S(1)}, bf16[48,1408]{1,0:T(8,128)(2,1)S(1)}, u32[]{:S(2)}, u32[]{:S(2)}) collective-permute-start(bf16[48,1408]{1,0:T(8,128)(2,1)S(1)} %collective-permute-done.1.refs_2_), channel_id=1, source_target_pairs={{0,2},{2,4},{4,6},{6,8},{8,10},{10,12},{12,14},{14,0},{1,3},{3,5},... | collective-permute-start | bytes 405512 | tf_op jit(solution)/shard_map/ppermute | solution.py:406
  40.4 9.4 %collective-permute-start.5 = (bf16[48,1408]{1,0:T(8,128)(2,1)S(1)}, bf16[48,1408]{1,0:T(8,128)(2,1)S(1)}, u32[]{:S(2)}, u32[]{:S(2)}) collective-permute-start(bf16[48,1408]{1,0:T(8,128)(2,1)S(1)} %collective-permute-done.4.refs_6_), channel_id=1, source_target_pairs={{0,14},{2,0},{4,2},{6,4},{8,6},{10,8},{12,10},{14,12},{1,15},{3,1}... | collective-permute-start | bytes 405512 | tf_op jit(solution)/shard_map/ppermute | solution.py:406
  51.3 5.4 %collective-permute-start.7 = (bf16[384,1408]{1,0:T(8,128)(2,1)S(1)}, bf16[384,1408]{1,0:T(8,128)(2,1)S(1)}, u32[]{:S(2)}, u32[]{:S(2)}) collective-permute-start(bf16[384,1408]{1,0:T(8,128)(2,1)S(1)} %shard_map.132.mine), channel_id=1, source_target_pairs={{0,1},{1,0},{2,3},{3,2},{4,5},{5,4},{6,7},{7,6},{8,9},{9,8},{10,11... | collective-permute-start | bytes 3244040 | tf_op jit(solution)/shard_map/ppermute | solution.py:420
  53.3 1.1 copy-start.3
  54.8 1.0 copy-start.5
  56.1 1.2 copy-start.6
  56.7 16.4 %copy-start.9 = (bf16[512]{0:T(512)(128)(2,1)S(1)}, bf16[512]{0:T(512)(128)(2,1)}, u32[]{:S(2)}) copy-start(bf16[512]{0:T(512)(128)(2,1)} %param.18) | copy-start | bytes 3076
  57.3 5.0 %copy-start.1 = (bf16[384,1408]{1,0:T(8,128)(2,1)}, bf16[384,1408]{1,0:T(8,128)(2,1)S(1)}, u32[]{:S(2)}) copy-start(bf16[384,1408]{1,0:T(8,128)(2,1)S(1)} %collective-permute-done.7.other) | copy-start | bytes 3244036
  62.4 20.3 %copy-start.4 = (f32[512]{0:T(512)S(1)}, f32[512]{0:T(512)}, u32[]{:S(2)}) copy-start(f32[512]{0:T(512)} %param.19) | copy-start | bytes 6148
  62.4 20.3 %all-to-all-start = ((bf16[16,64,128]{2,1,0:T(8,128)(2,1)}), bf16[16,64,128]{2,1,0:T(8,128)(2,1)S(1)}, u32[]{:S(2)}, u32[]{:S(2)}) async-start(bf16[16,64,128]{2,1,0:T(8,128)(2,1)} %get-tuple-element.28), calls=%async_computation | async-start | bytes 524288 | tf_op jit(solution)/shard_map/all_to_all | solution.py:398
  82.7 25.5 %copy-start.2 = (bf16[384,1408]{1,0:T(8,128)(2,1)S(1)}, bf16[384,1408]{1,0:T(8,128)(2,1)}, u32[]{:S(2)}) copy-start(bf16[384,1408]{1,0:T(8,128)(2,1)} %copy-done.1) | copy-start | bytes 3244036
  82.7 25.5 %copy-start.7 = (bf16[512,768]{1,0:T(8,128)(2,1)S(1)}, bf16[512,768]{1,0:T(8,128)(2,1)}, u32[]{:S(2)}) copy-start(bf16[512,768]{1,0:T(8,128)(2,1)} %get-tuple-element.33.saved) | copy-start | bytes 2359300
  82.7 25.5 %copy-start.8 = (f32[8,768]{1,0:T(8,128)S(1)}, f32[8,768]{1,0:T(8,128)}, u32[]{:S(2)}) copy-start(f32[8,768]{1,0:T(8,128)} %get-tuple-element.34.stats) | copy-start | bytes 73732
  158.6 12.5 %copy-start = (bf16[1408,512]{1,0:T(8,128)(2,1)S(1)}, bf16[1408,512]{1,0:T(8,128)(2,1)}, u32[]{:S(2)}) copy-start(bf16[1408,512]{1,0:T(8,128)(2,1)} %w_e2d.3) | copy-start | bytes 4325380
Sparse Core Ops, SparseCore 0:
  11.4 61.5 all-gather.2

commit v7 on v6

--- a/solution.py
+++ b/solution.py
@@ -1,3 +1,5 @@
+import functools
+
 import jax
 import jax.numpy as jnp
 from jax import lax
@@ -144,10 +146,13 @@
     return call(turn_body, [((w_t.shape[1], 3 * HL), BF16)], [], 1 << 20, 16, w_t)[0]
 
 
-def join_body(*refs):
-    count = len(refs) - 2
-    blocks, out, sems = refs[:count], refs[count], refs[count + 1]
-    copies = [pltpu.make_async_copy(blocks[k], out.at[pl.ds(CAP * k, CAP)], sems.at[k]) for k in range(count)]
+def join_body(places, *refs):
+    blocks, out, sems = refs[:len(places)], refs[len(places)], refs[len(places) + 1]
+    copies = []
+    for i, (k, column) in enumerate(places):
+        rows, width = blocks[i].shape
+        part = out.at[pl.ds(rows * k, rows), pl.ds(column, width)]
+        copies.append(pltpu.make_async_copy(blocks[i], part, sems.at[i]))
     for copy in copies:
         copy.start()
     for copy in copies:
@@ -155,16 +160,22 @@
 
 
 def join(blocks):
-    rows, width = blocks[0].shape
-    return pl.pallas_call(
-        join_body,
-        out_shape=jax.ShapeDtypeStruct((len(blocks) * rows, width), blocks[0].dtype),
-        in_specs=[pl.BlockSpec(memory_space=pl.ANY)] * len(blocks),
+    places = []
+    for k, parts in enumerate(blocks):
+        column = 0
+        for part in parts:
+            places.append((k, column))
+            column += part.shape[1]
+    flat = [part for parts in blocks for part in parts]
+    return pl.pallas_call(
+        functools.partial(join_body, places),
+        out_shape=jax.ShapeDtypeStruct((NZ * flat[0].shape[0], flat[0].shape[1]), flat[0].dtype),
+        in_specs=[pl.BlockSpec(memory_space=pl.ANY)] * len(flat),
         out_specs=pl.BlockSpec(memory_space=pl.ANY),
-        scratch_shapes=[pltpu.SemaphoreType.DMA((len(blocks),))],
+        scratch_shapes=[pltpu.SemaphoreType.DMA((len(flat),))],
         compiler_params=pltpu.CompilerParams(vmem_limit_bytes=4 << 20),
-        cost_estimate=pl.CostEstimate(flops=0, bytes_accessed=2 << 20, transcendentals=0),
-    )(*blocks)
+        cost_estimate=pl.CostEstimate(flops=0, bytes_accessed=4 << 20, transcendentals=0),
+    )(*flat)
 
 
 def attend_body(mine, other, w, swap, extra, sent, saved, stats, xs, out, keep, keep_stats, sems):
@@ -413,7 +424,7 @@
     got[3] = z_shift(got[2], 1)
     got[5] = z_shift(got[6], -1)
     got[4] = z_shift(got[2], 2)
-    return [got[k] for k in range(NZ)]
+    return [[got[k]] for k in range(NZ)]
 
 
 def swap_core(block):
@@ -435,6 +446,7 @@
     cotangent,
 ):
     me = lax.axis_index(SEQ)
+    my_z, my_c = me // 2, me % 2
     fdev = cotangent.shape[1]
     cot = cotangent[0]
     cap = keep_pos.shape[1]
@@ -443,10 +455,6 @@
     xn_own, x_slot, offsets = prep(keep_pos, enc_gain, patches[0])
     x_vis, w_oe_own, pack = pack_up(x_slot, w_out, w_e2d, fc_in, fc_out)
     weights = lax.all_gather(pack, SEQ, axis=0)
-
-    blocks = around(xn_own)
-    blocks[4], spot, x_vis, offsets = lax.optimization_barrier((blocks[4], me, x_vis, offsets))
-    my_z, my_c = spot // 2, spot % 2
 
     places = jnp.pad(offsets[:, 0].reshape(16, 1, SLOTS), ((0, 0), (0, 0), (0, 128 - SLOTS)))
     extra = jnp.concatenate(
@@ -458,9 +466,11 @@
     inside = tok % cap
     dest = inside // SLOTS * cap + source * SLOTS + inside % SLOTS
     swap = (dest[None, :] == tok[:, None]).astype(BF16)
-    table = position_table((spot * fdev + jnp.arange(fdev, dtype=jnp.int32)).astype(F32), DD)
+    table = position_table((me * fdev + jnp.arange(fdev, dtype=jnp.int32)).astype(F32), DD)
 
     w = turn(w_qkv.transpose(0, 2, 1).reshape(3 * HD, -1))
+    blocks = around(xn_own)
+    blocks[4][0], w, swap, extra = lax.optimization_barrier((blocks[4][0], w, swap, extra))
     mine = join(blocks)
     other = swap_core(mine)
     sent, saved, stats = attend(mine, other, w, swap, extra)

time: 180 us -> 176 us (0.978)
  local copies, waits for them, and re-layouts: 3.35 us -> 0.54 us
    ppermute x7, waiting for transfers between devices: 12 us -> 7.52 us  [z_shift(): return lax.ppermute(block, 'z', [(z, (z + step) % NZ) for z in range(NZ)])]
    unnamed x20 -> x16, local copies, waits for them, and re-layouts: 2.85 us -> 0.04 us
    ppermute x1, waiting for transfers between devices: 0.01 us -> 2.67 us  [swap_core(): return lax.ppermute(block, 'core', [(0, 1), (1, 0)])]
    all_to_all x1, starting transfers between devices: 10.6 us -> 8.41 us  [exchange(): return lax.all_to_all(block, axis, 0, 0, tiled=True)]
    ppermute x7, starting transfers between devices: 26.5 us -> 28.5 us  [z_shift(): return lax.ppermute(block, 'z', [(z, (z + step) % NZ) for z in range(NZ)])]
  transfers between devices with their start and end apart: 10 -> 10, of which waited for: 6 -> 4; matrix products, arithmetic and copies ran while one was open for 1% -> 1% of each run, Pallas kernels for 4% -> 4%
where the time goes in v7:
time: 176 us; the launch traced here: 175 us
  blocking collectives  77.5 us (44%)
  starting transfers between devices  38.9 us (22%)
  Pallas kernels  23.4 us (13%)
  waiting for transfers between devices  18.8 us (11%)
  between operations  14.3 us (8%)
  other arithmetic  1.81 us (1%)
    all_to_all x4, blocking collectives, exchange(): return lax.all_to_all(block, axis, 0, 0, tiled=True)  58.9 us
    ppermute x7, starting transfers between devices, z_shift(): return lax.ppermute(block, 'z', [(z, (z + step) % NZ) for z in range(NZ)])  28.5 us
    all_gather x1, blocking collectives, local(): dvis = lax.all_gather(dvis_own, SEQ, axis=0, tiled=True)  18.6 us
    all_to_all x1, waiting for transfers between devices, exchange(): return lax.all_to_all(block, axis, 0, 0, tiled=True)  8.55 us
    all_to_all x1, starting transfers between devices, exchange(): return lax.all_to_all(block, axis, 0, 0, tiled=True)  8.41 us
    ppermute x7, waiting for transfers between devices, z_shift(): return lax.ppermute(block, 'z', [(z, (z + step) % NZ) for z in range(NZ)])  7.52 us
    pallas_call x1, Pallas kernels, decode(): pl.pallas_call(decode_body, out_shape=[jax.ShapeDtypeStruct((FDEV, DD), B...  6.83 us
    pallas_call x1, Pallas kernels, attend(): pl.pallas_call(attend_body, out_shape=[pltpu.HBM((16, 64, 128), BF16), pl...  5.03 us
  transfers between devices with their start and end apart: 10, of which 4 were waited for; matrix products, arithmetic and copies ran while one was open for 1% of the time, Pallas kernels for 4%

profile of v7, /device:TPU:64, one launch (start us, length us, event | category | flops | bytes accessed | tf_op | source)
XLA Modules:
  0.0 175.3 jit_solution(3982906114067330658)
XLA Ops:
  7.2 0.0 all-gather.3.cloned.1.call-start
  7.2 1.3 shard_map.130
  8.5 0.0 copy-start.3
  8.6 2.8 %shard_map.132 = (bf16[48,512]{1,0:T(8,128)(2,1)S(1)}, bf16[96,512]{1,0:T(8,128)(2,1)S(1)}, bf16[352,512]{1,0:T(8,128)(2,1)}) custom-call(bf16[48,1408]{1,0:T(8,128)(2,1)S(1)} %get-tuple-element.21.x_slot, bf16[88,1408]{1,0:T(8,128)(2,1)} %w_out.1, bf16[1408,512]{1,0:T(8,128)(2,1)} %w_e2d.3, bf16[128,512]{1,0:T(8,128)(2,1)} %fc_in.1, bf16[128,512]{1,0:T(8,128)(2,1)} %fc_out.1), custom_call_target="tpu_custom_call" | custom-call | flops 209715200 | bytes 3145728 | tf_op jit(solution)/shard_map/pallas_call | solution.py:125
  11.3 0.0 all-gather.3.cloned.1.call-update
  11.4 6.1 %collective-permute-start.1 = (bf16[48,1408]{1,0:T(8,128)(2,1)S(1)}, bf16[48,1408]{1,0:T(8,128)(2,1)S(1)}, u32[]{:S(2)}, u32[]{:S(2)}) collective-permute-start(bf16[48,1408]{1,0:T(8,128)(2,1)S(1)} %get-tuple-element.20.refs_0_), channel_id=1, source_target_pairs={{0,4},{2,6},{4,8},{6,10},{8,12},{10,14},{12,0},{14,2},{1,5},{3,7},... | collective-permute-start | bytes 405512 | tf_op jit(solution)/shard_map/ppermute | solution.py:417
  17.5 5.9 %collective-permute-start.4 = (bf16[48,1408]{1,0:T(8,128)(2,1)S(1)}, bf16[48,1408]{1,0:T(8,128)(2,1)S(1)}, u32[]{:S(2)}, u32[]{:S(2)}) collective-permute-start(bf16[48,1408]{1,0:T(8,128)(2,1)S(1)} %get-tuple-element.20.refs_0_), channel_id=1, source_target_pairs={{0,12},{2,14},{4,0},{6,2},{8,4},{10,6},{12,8},{14,10},{1,13},{3,15... | collective-permute-start | bytes 405512 | tf_op jit(solution)/shard_map/ppermute | solution.py:417
  23.3 1.9 %collective-permute-start = (bf16[48,1408]{1,0:T(8,128)(2,1)S(1)}, bf16[48,1408]{1,0:T(8,128)(2,1)S(1)}, u32[]{:S(2)}, u32[]{:S(2)}) collective-permute-start(bf16[48,1408]{1,0:T(8,128)(2,1)S(1)} %get-tuple-element.20.refs_0_), channel_id=1, source_target_pairs={{0,2},{2,4},{4,6},{6,8},{8,10},{10,12},{12,14},{14,0},{1,3},{3,5},... | collective-permute-start | bytes 405512 | tf_op jit(solution)/shard_map/ppermute | solution.py:417
  25.3 3.9 %collective-permute-start.6 = (bf16[48,1408]{1,0:T(8,128)(2,1)S(1)}, bf16[48,1408]{1,0:T(8,128)(2,1)S(1)}, u32[]{:S(2)}, u32[]{:S(2)}) collective-permute-start(bf16[48,1408]{1,0:T(8,128)(2,1)S(1)} %get-tuple-element.20.refs_0_), channel_id=1, source_target_pairs={{0,14},{2,0},{4,2},{6,4},{8,6},{10,8},{12,10},{14,12},{1,15},{3,1}... | collective-permute-start | bytes 405512 | tf_op jit(solution)/shard_map/ppermute | solution.py:417
  29.2 0.1 reshape.112
  29.3 0.1 slice_reduce_fusion
  29.4 0.1 reshape_squeeze.4
  29.5 0.1 pad.9.clone
  29.6 0.0 copy-done.3
  29.6 0.4 shard_map.131.w
  30.0 0.4 fusion.swap
  30.4 0.0 collective-permute-done.1.refs_2_
  30.5 3.6 %collective-permute-start.3 = (bf16[48,1408]{1,0:T(8,128)(2,1)S(1)}, bf16[48,1408]{1,0:T(8,128)(2,1)S(1)}, u32[]{:S(2)}, u32[]{:S(2)}) collective-permute-start(bf16[48,1408]{1,0:T(8,128)(2,1)S(1)} %collective-permute-done.1.refs_2_), channel_id=1, source_target_pairs={{0,4},{2,6},{4,8},{6,10},{8,12},{10,14},{12,0},{14,2},{1,5},{3,7},... | collective-permute-start | bytes 405512 | tf_op jit(solution)/shard_map/ppermute | solution.py:417
  34.1 5.1 %collective-permute-start.2 = (bf16[48,1408]{1,0:T(8,128)(2,1)S(1)}, bf16[48,1408]{1,0:T(8,128)(2,1)S(1)}, u32[]{:S(2)}, u32[]{:S(2)}) collective-permute-start(bf16[48,1408]{1,0:T(8,128)(2,1)S(1)} %collective-permute-done.1.refs_2_), channel_id=1, source_target_pairs={{0,2},{2,4},{4,6},{6,8},{8,10},{10,12},{12,14},{14,0},{1,3},{3,5},... | collective-permute-start | bytes 405512 | tf_op jit(solution)/shard_map/ppermute | solution.py:417
  39.3 0.0 collective-permute-done.4.refs_6_
  39.3 1.9 %collective-permute-start.5 = (bf16[48,1408]{1,0:T(8,128)(2,1)S(1)}, bf16[48,1408]{1,0:T(8,128)(2,1)S(1)}, u32[]{:S(2)}, u32[]{:S(2)}) collective-permute-start(bf16[48,1408]{1,0:T(8,128)(2,1)S(1)} %collective-permute-done.4.refs_6_), channel_id=1, source_target_pairs={{0,14},{2,0},{4,2},{6,4},{8,6},{10,8},{12,10},{14,12},{1,15},{3,1}... | collective-permute-start | bytes 405512 | tf_op jit(solution)/shard_map/ppermute | solution.py:417
  41.2 0.1 fusion.4.extra
  41.3 4.8 %collective-permute-done.3.refs_4_ = bf16[48,1408]{1,0:T(8,128)(2,1)S(1)} collective-permute-done((bf16[48,1408]{1,0:T(8,128)(2,1)S(1)}, bf16[48,1408]{1,0:T(8,128)(2,1)S(1)}, u32[]{:S(2)}, u32[]{:S(2)}) %collective-permute-start.3) | collective-permute-done | bytes 135200 | tf_op jit(solution)/shard_map/ppermute | solution.py:417
  46.1 0.0 collective-permute-done.refs_1_
  46.1 0.0 collective-permute-done.6.refs_7_
  46.1 2.7 %collective-permute-done.2.refs_3_ = bf16[48,1408]{1,0:T(8,128)(2,1)S(1)} collective-permute-done((bf16[48,1408]{1,0:T(8,128)(2,1)S(1)}, bf16[48,1408]{1,0:T(8,128)(2,1)S(1)}, u32[]{:S(2)}, u32[]{:S(2)}) %collective-permute-start.2) | collective-permute-done | bytes 135200 | tf_op jit(solution)/shard_map/ppermute | solution.py:417
  48.8 0.0 collective-permute-done.5.refs_5_
  48.8 1.5 shard_map.133.mine
  50.3 0.0 copy-start.7
  50.3 1.9 %collective-permute-start.7 = (bf16[384,1408]{1,0:T(8,128)(2,1)S(1)}, bf16[384,1408]{1,0:T(8,128)(2,1)S(1)}, u32[]{:S(2)}, u32[]{:S(2)}) collective-permute-start(bf16[384,1408]{1,0:T(8,128)(2,1)S(1)} %shard_map.133.mine), channel_id=1, source_target_pairs={{0,1},{1,0},{2,3},{3,2},{4,5},{5,4},{6,7},{7,6},{8,9},{9,8},{10,11... | collective-permute-start | bytes 3244040 | tf_op jit(solution)/shard_map/ppermute | solution.py:431
  52.2 2.7 %collective-permute-done.7.other = bf16[384,1408]{1,0:T(8,128)(2,1)S(1)} collective-permute-done((bf16[384,1408]{1,0:T(8,128)(2,1)S(1)}, bf16[384,1408]{1,0:T(8,128)(2,1)S(1)}, u32[]{:S(2)}, u32[]{:S(2)}) %collective-permute-start.7) | collective-permute-done | bytes 1081376 | tf_op jit(solution)/shard_map/ppermute | solution.py:431
  54.9 0.0 copy-start.1
  54.9 5.0 %shard_map.134 = (bf16[16,64,128]{2,1,0:T(8,128)(2,1)}, bf16[512,768]{1,0:T(8,128)(2,1)}, f32[8,768]{1,0:T(8,128)}) custom-call(bf16[384,1408]{1,0:T(8,128)(2,1)S(1)} %shard_map.133.mine, bf16[384,1408]{1,0:T(8,128)(2,1)S(1)} %collective-permute-done.7.other, bf16[1408,384]{1,0:T(8,128)(2,1)S(1)} %shard_map.131.w, bf16[768,768]{1,0:T(8,128)(2,1)S(1)} %fusion.swap, ...), custom_call_target="tpu_custom_call" | custom-call | flops 1782579200 | bytes 8388608 | tf_op jit(solution)/shard_map/pallas_call | solution.py:229
  59.9 0.0 copy-done.1
  59.9 0.0 copy-start.4
  59.9 8.4 %all-to-all-start = ((bf16[16,64,128]{2,1,0:T(8,128)(2,1)}), bf16[16,64,128]{2,1,0:T(8,128)(2,1)S(1)}, u32[]{:S(2)}, u32[]{:S(2)}) async-start(bf16[16,64,128]{2,1,0:T(8,128)(2,1)} %get-tuple-element.28), calls=%async_computation | async-start | bytes 524288 | tf_op jit(solution)/shard_map/all_to_all | solution.py:409
  68.3 0.0 copy-done.7
  68.4 1.0 multiply_sine_fusion
  69.4 0.1 pad_maximum_fusion.table
  69.4 8.5 %all-to-all-done.came = bf16[16,64,128]{2,1,0:T(8,128)(2,1)S(1)} async-done(((bf16[16,64,128]{2,1,0:T(8,128)(2,1)}), bf16[16,64,128]{2,1,0:T(8,128)(2,1)S(1)}, u32[]{:S(2)}, u32[]{:S(2)}) %all-to-all-start) | async-done | bytes 262176 | tf_op jit(solution)/shard_map/all_to_all | solution.py:409
  78.0 0.0 all-gather.3.cloned.1.call-done
  78.0 0.0 copy-done.4
  78.0 0.0 copy-start.2
  78.0 0.0 copy-start.5
  78.0 0.0 copy-start.6
  78.0 6.8 %shard_map.135 = (bf16[256,512]{1,0:T(8,128)(2,1)}, bf16[48,512]{1,0:T(8,128)(2,1)S(1)}) custom-call(bf16[16,64,128]{2,1,0:T(8,128)(2,1)S(1)} %all-to-all-done.came, bf16[16,352,512]{2,1,0:T(8,128)(2,1)} %bitcast.22, bf16[256,512]{1,0:T(8,128)(2,1)} %bitcast.24, bf16[1,512]{1,0:T(2,128)(2,1)S(1)} %broadcast_in_dim.30.mask, f32[1,512]{1,0:T(1,128)S(1)} %bitcast.18, ...), custom_call_target="tpu_custom_call" | custom-call | flops 2411724800 | bytes 8388608 | tf_op jit(solution)/shard_map/pallas_call | solution.py:312
  84.8 18.6 %all_gather.11.dvis = bf16[768,512]{1,0:T(8,128)(2,1)S(1)} all-gather(bf16[48,512]{1,0:T(8,128)(2,1)S(1)} %get-tuple-element.31), channel_id=1, replica_groups=mesh['y'=8,'x'=4,'z'=8,'core'=2] {'z','core'}, dimensions={0}, use_global_device_ids=true | all-gather | bytes 835584 | tf_op jit(solution)/shard_map/all_gather | solution.py:479
  103.4 0.0 copy-done.2
  103.4 0.0 copy-done.5
  103.4 0.0 copy-done.6
  103.4 4.1 %shard_map.136 = bf16[3328,128]{1,0:T(8,128)(2,1)S(1)} custom-call(bf16[768,512]{1,0:T(8,128)(2,1)S(1)} %all_gather.11.dvis, bf16[96,512]{1,0:T(8,128)(2,1)S(1)} %get-tuple-element.32.w_oe, bf16[768,768]{1,0:T(8,128)(2,1)S(1)} %fusion.swap, bf16[512,768]{1,0:T(8,128)(2,1)S(1)} %copy-done.5, f32[8,768]{1,0:T(8,128)S(1)} %copy-done.6, ...), custom_call_target="tpu_custom_call" | custom-call | flops 2621440000 | bytes 8388608 | tf_op jit(solution)/shard_map/pallas_call | solution.py:371
  107.6 17.6 %all_to_all.25 = bf16[4,832,128]{2,1,0:T(8,128)(2,1)S(1)} all-to-all(bf16[4,832,128]{2,1,0:T(8,128)(2,1)S(1)} %bitcast.16), channel_id=1, replica_groups=mesh['y'=8,'x'=4,'z'=8,'core'=2] {'x'}, dimensions={0} | all-to-all | bytes 1703936 | tf_op jit(solution)/shard_map/all_to_all | solution.py:409
  125.2 0.2 reduce_sum.24
  125.4 16.6 %all_to_all.26 = bf16[8,104,128]{2,1,0:T(8,128)(2,1)S(1)} all-to-all(bf16[8,104,128]{2,1,0:T(8,128)(2,1)S(1)} %bitcast.19), channel_id=1, replica_groups=mesh['y'=8,'x'=4,'z'=8,'core'=2] {'y'}, dimensions={0} | all-to-all | bytes 425984 | tf_op jit(solution)/shard_map/all_to_all | solution.py:409
  142.0 12.4 %all_to_all.27 = bf16[8,104,128]{2,1,0:T(8,128)(2,1)S(1)} all-to-all(bf16[8,104,128]{2,1,0:T(8,128)(2,1)S(1)} %broadcast_in_dim.33), channel_id=1, replica_groups=mesh['y'=8,'x'=4,'z'=8,'core'=2] {'y'}, dimensions={0} | all-to-all | bytes 425984 | tf_op jit(solution)/shard_map/all_to_all | solution.py:409
  154.4 0.0 copy-start
  154.4 0.1 broadcast_in_dim.35
  154.5 12.4 %all_to_all.28 = bf16[4,832,128]{2,1,0:T(8,128)(2,1)S(1)} all-to-all(bf16[4,832,128]{2,1,0:T(8,128)(2,1)S(1)} %broadcast_in_dim.35), channel_id=1, replica_groups=mesh['y'=8,'x'=4,'z'=8,'core'=2] {'x'}, dimensions={0} | all-to-all | bytes 1703936 | tf_op jit(solution)/shard_map/all_to_all | solution.py:409
  166.9 0.0 copy-done
  166.9 1.5 shard_map.137
  (7 shorter events, 0.1 us)
Async XLA Ops:
  7.2 70.8 %all-gather.3.cloned.1.call-start = ((), (), s32[]{:S(2)}) async-start(), calls=%async_computation.5 | async-start | bytes 6127616 | tf_op jit(solution)/shard_map/all_gather | solution.py:457
  8.5 21.1 %copy-start.3 = (bf16[3,1408,88]{1,2,0:T(8,128)(2,1)S(1)}, bf16[3,1408,88]{1,2,0:T(8,128)(2,1)}, u32[]{:S(2)}) copy-start(bf16[3,1408,88]{1,2,0:T(8,128)(2,1)} %param.15) | copy-start | bytes 2230276
  11.4 19.1 %collective-permute-start.1 = (bf16[48,1408]{1,0:T(8,128)(2,1)S(1)}, bf16[48,1408]{1,0:T(8,128)(2,1)S(1)}, u32[]{:S(2)}, u32[]{:S(2)}) collective-permute-start(bf16[48,1408]{1,0:T(8,128)(2,1)S(1)} %get-tuple-element.20.refs_0_), channel_id=1, source_target_pairs={{0,4},{2,6},{4,8},{6,10},{8,12},{10,14},{12,0},{14,2},{1,5},{3,7},... | collective-permute-start | bytes 405512 | tf_op jit(solution)/shard_map/ppermute | solution.py:417
  17.5 21.8 %collective-permute-start.4 = (bf16[48,1408]{1,0:T(8,128)(2,1)S(1)}, bf16[48,1408]{1,0:T(8,128)(2,1)S(1)}, u32[]{:S(2)}, u32[]{:S(2)}) collective-permute-start(bf16[48,1408]{1,0:T(8,128)(2,1)S(1)} %get-tuple-element.20.refs_0_), channel_id=1, source_target_pairs={{0,12},{2,14},{4,0},{6,2},{8,4},{10,6},{12,8},{14,10},{1,13},{3,15... | collective-permute-start | bytes 405512 | tf_op jit(solution)/shard_map/ppermute | solution.py:417
  23.3 22.8 %collective-permute-start = (bf16[48,1408]{1,0:T(8,128)(2,1)S(1)}, bf16[48,1408]{1,0:T(8,128)(2,1)S(1)}, u32[]{:S(2)}, u32[]{:S(2)}) collective-permute-start(bf16[48,1408]{1,0:T(8,128)(2,1)S(1)} %get-tuple-element.20.refs_0_), channel_id=1, source_target_pairs={{0,2},{2,4},{4,6},{6,8},{8,10},{10,12},{12,14},{14,0},{1,3},{3,5},... | collective-permute-start | bytes 405512 | tf_op jit(solution)/shard_map/ppermute | solution.py:417
  25.3 20.9 %collective-permute-start.6 = (bf16[48,1408]{1,0:T(8,128)(2,1)S(1)}, bf16[48,1408]{1,0:T(8,128)(2,1)S(1)}, u32[]{:S(2)}, u32[]{:S(2)}) collective-permute-start(bf16[48,1408]{1,0:T(8,128)(2,1)S(1)} %get-tuple-element.20.refs_0_), channel_id=1, source_target_pairs={{0,14},{2,0},{4,2},{6,4},{8,6},{10,8},{12,10},{14,12},{1,15},{3,1}... | collective-permute-start | bytes 405512 | tf_op jit(solution)/shard_map/ppermute | solution.py:417
  30.5 15.7 %collective-permute-start.3 = (bf16[48,1408]{1,0:T(8,128)(2,1)S(1)}, bf16[48,1408]{1,0:T(8,128)(2,1)S(1)}, u32[]{:S(2)}, u32[]{:S(2)}) collective-permute-start(bf16[48,1408]{1,0:T(8,128)(2,1)S(1)} %collective-permute-done.1.refs_2_), channel_id=1, source_target_pairs={{0,4},{2,6},{4,8},{6,10},{8,12},{10,14},{12,0},{14,2},{1,5},{3,7},... | collective-permute-start | bytes 405512 | tf_op jit(solution)/shard_map/ppermute | solution.py:417
  34.1 14.7 %collective-permute-start.2 = (bf16[48,1408]{1,0:T(8,128)(2,1)S(1)}, bf16[48,1408]{1,0:T(8,128)(2,1)S(1)}, u32[]{:S(2)}, u32[]{:S(2)}) collective-permute-start(bf16[48,1408]{1,0:T(8,128)(2,1)S(1)} %collective-permute-done.1.refs_2_), channel_id=1, source_target_pairs={{0,2},{2,4},{4,6},{6,8},{8,10},{10,12},{12,14},{14,0},{1,3},{3,5},... | collective-permute-start | bytes 405512 | tf_op jit(solution)/shard_map/ppermute | solution.py:417
  39.3 9.5 %collective-permute-start.5 = (bf16[48,1408]{1,0:T(8,128)(2,1)S(1)}, bf16[48,1408]{1,0:T(8,128)(2,1)S(1)}, u32[]{:S(2)}, u32[]{:S(2)}) collective-permute-start(bf16[48,1408]{1,0:T(8,128)(2,1)S(1)} %collective-permute-done.4.refs_6_), channel_id=1, source_target_pairs={{0,14},{2,0},{4,2},{6,4},{8,6},{10,8},{12,10},{14,12},{1,15},{3,1}... | collective-permute-start | bytes 405512 | tf_op jit(solution)/shard_map/ppermute | solution.py:417
  50.3 18.1 %copy-start.7 = (bf16[512]{0:T(512)(128)(2,1)S(1)}, bf16[512]{0:T(512)(128)(2,1)}, u32[]{:S(2)}) copy-start(bf16[512]{0:T(512)(128)(2,1)} %param.18) | copy-start | bytes 3076
  50.3 4.6 %collective-permute-start.7 = (bf16[384,1408]{1,0:T(8,128)(2,1)S(1)}, bf16[384,1408]{1,0:T(8,128)(2,1)S(1)}, u32[]{:S(2)}, u32[]{:S(2)}) collective-permute-start(bf16[384,1408]{1,0:T(8,128)(2,1)S(1)} %shard_map.133.mine), channel_id=1, source_target_pairs={{0,1},{1,0},{2,3},{3,2},{4,5},{5,4},{6,7},{7,6},{8,9},{9,8},{10,11... | collective-permute-start | bytes 3244040 | tf_op jit(solution)/shard_map/ppermute | solution.py:431
  54.9 5.0 %copy-start.1 = (bf16[384,1408]{1,0:T(8,128)(2,1)}, bf16[384,1408]{1,0:T(8,128)(2,1)S(1)}, u32[]{:S(2)}) copy-start(bf16[384,1408]{1,0:T(8,128)(2,1)S(1)} %collective-permute-done.7.other) | copy-start | bytes 3244036
  59.9 18.1 %copy-start.4 = (f32[512]{0:T(512)S(1)}, f32[512]{0:T(512)}, u32[]{:S(2)}) copy-start(f32[512]{0:T(512)} %param.19) | copy-start | bytes 6148
  59.9 18.0 %all-to-all-start = ((bf16[16,64,128]{2,1,0:T(8,128)(2,1)}), bf16[16,64,128]{2,1,0:T(8,128)(2,1)S(1)}, u32[]{:S(2)}, u32[]{:S(2)}) async-start(bf16[16,64,128]{2,1,0:T(8,128)(2,1)} %get-tuple-element.28), calls=%async_computation | async-start | bytes 524288 | tf_op jit(solution)/shard_map/all_to_all | solution.py:409
  78.0 25.5 %copy-start.2 = (bf16[384,1408]{1,0:T(8,128)(2,1)S(1)}, bf16[384,1408]{1,0:T(8,128)(2,1)}, u32[]{:S(2)}) copy-start(bf16[384,1408]{1,0:T(8,128)(2,1)} %copy-done.1) | copy-start | bytes 3244036
  78.0 25.5 %copy-start.5 = (bf16[512,768]{1,0:T(8,128)(2,1)S(1)}, bf16[512,768]{1,0:T(8,128)(2,1)}, u32[]{:S(2)}) copy-start(bf16[512,768]{1,0:T(8,128)(2,1)} %get-tuple-element.33.saved) | copy-start | bytes 2359300
  78.0 25.5 %copy-start.6 = (f32[8,768]{1,0:T(8,128)S(1)}, f32[8,768]{1,0:T(8,128)}, u32[]{:S(2)}) copy-start(f32[8,768]{1,0:T(8,128)} %get-tuple-element.34.stats) | copy-start | bytes 73732
  154.4 12.5 %copy-start = (bf16[1408,512]{1,0:T(8,128)(2,1)S(1)}, bf16[1408,512]{1,0:T(8,128)(2,1)}, u32[]{:S(2)}) copy-start(bf16[1408,512]{1,0:T(8,128)(2,1)} %w_e2d.3) | copy-start | bytes 4325380
Sparse Core Ops, SparseCore 0:
  11.5 59.4 all-gather.2

commit v8 on v7

--- a/solution.py
+++ b/solution.py
@@ -11,6 +11,7 @@
 HD = 88
 HP = 96
 HL = 128
+CUT = 768
 DD = 512
 SEQ = ("z", "core")
 NZ = 8
@@ -423,8 +424,10 @@
         got[step % NZ] = z_shift(block, step)
     got[3] = z_shift(got[2], 1)
     got[5] = z_shift(got[6], -1)
-    got[4] = z_shift(got[2], 2)
-    return [[got[k]] for k in range(NZ)]
+    back_two, got[1], got[7] = lax.optimization_barrier((got[6], got[1], got[7]))
+    blocks = [[got.get(k)] for k in range(NZ)]
+    blocks[4] = [z_shift(got[2][:, :CUT], 2), z_shift(back_two[:, CUT:], -2)]
+    return blocks
 
 
 def swap_core(block):

time: 176 us -> 179 us (1.017)
  starting transfers between devices: 38.9 us -> 43.1 us
    ppermute x7 -> x8, starting transfers between devices: 28.5 us -> 34.3 us  [z_shift(): return lax.ppermute(block, 'z', [(z, (z + step) % NZ) for z in range(NZ)])]
    ppermute x7 -> x8, waiting for transfers between devices: 7.52 us -> 6.38 us  [z_shift(): return lax.ppermute(block, 'z', [(z, (z + step) % NZ) for z in range(NZ)])]
  transfers between devices with their start and end apart: 10 -> 11, of which waited for: 4 -> 5; matrix products, arithmetic and copies ran while one was open for 1% -> 1% of each run, Pallas kernels for 4% -> 4%
where the time goes in v8:
time: 179 us; the launch traced here: 178 us
  blocking collectives  77.6 us (43%)
  starting transfers between devices  43.1 us (24%)
  Pallas kernels  23.2 us (13%)
  waiting for transfers between devices  17.7 us (10%)
  between operations  14.4 us (8%)
  other arithmetic  1.81 us (1%)
    all_to_all x4, blocking collectives, exchange(): return lax.all_to_all(block, axis, 0, 0, tiled=True)  59 us
    ppermute x8, starting transfers between devices, z_shift(): return lax.ppermute(block, 'z', [(z, (z + step) % NZ) for z in range(NZ)])  34.3 us
    all_gather x1, blocking collectives, local(): dvis = lax.all_gather(dvis_own, SEQ, axis=0, tiled=True)  18.6 us
    all_to_all x1, waiting for transfers between devices, exchange(): return lax.all_to_all(block, axis, 0, 0, tiled=True)  8.55 us
    all_to_all x1, starting transfers between devices, exchange(): return lax.all_to_all(block, axis, 0, 0, tiled=True)  6.85 us
    pallas_call x1, Pallas kernels, decode(): pl.pallas_call(decode_body, out_shape=[jax.ShapeDtypeStruct((FDEV, DD), B...  6.84 us
    ppermute x8, waiting for transfers between devices, z_shift(): return lax.ppermute(block, 'z', [(z, (z + step) % NZ) for z in range(NZ)])  6.38 us
    pallas_call x1, Pallas kernels, attend(): pl.pallas_call(attend_body, out_shape=[pltpu.HBM((16, 64, 128), BF16), pl...  5.03 us
  transfers between devices with their start and end apart: 11, of which 5 were waited for; matrix products, arithmetic and copies ran while one was open for 1% of the time, Pallas kernels for 4%

profile of v8, /device:TPU:64, one launch (start us, length us, event | category | flops | bytes accessed | tf_op | source)
XLA Modules:
  0.0 178.4 jit_solution(7961648117486922)
XLA Ops:
  7.2 0.0 all-gather.3.cloned.1.call-start
  7.2 1.3 shard_map.130
  8.5 2.7 %shard_map.132 = (bf16[48,512]{1,0:T(8,128)(2,1)S(1)}, bf16[96,512]{1,0:T(8,128)(2,1)S(1)}, bf16[352,512]{1,0:T(8,128)(2,1)}) custom-call(bf16[48,1408]{1,0:T(8,128)(2,1)S(1)} %get-tuple-element.25.x_slot, bf16[88,1408]{1,0:T(8,128)(2,1)} %w_out.1, bf16[1408,512]{1,0:T(8,128)(2,1)} %w_e2d.3, bf16[128,512]{1,0:T(8,128)(2,1)} %fc_in.1, bf16[128,512]{1,0:T(8,128)(2,1)} %fc_out.1), custom_call_target="tpu_custom_call" | custom-call | flops 209715200 | bytes 3145728 | tf_op jit(solution)/shard_map/pallas_call | solution.py:126
  11.3 0.0 copy-start.3
  11.3 0.0 all-gather.3.cloned.1.call-update
  11.3 6.2 %collective-permute-start.3 = (bf16[48,1408]{1,0:T(8,128)(2,1)S(1)}, bf16[48,1408]{1,0:T(8,128)(2,1)S(1)}, u32[]{:S(2)}, u32[]{:S(2)}) collective-permute-start(bf16[48,1408]{1,0:T(8,128)(2,1)S(1)} %get-tuple-element.23.refs_0_), channel_id=1, source_target_pairs={{0,4},{2,6},{4,8},{6,10},{8,12},{10,14},{12,0},{14,2},{1,5},{3,7},... | collective-permute-start | bytes 405512 | tf_op jit(solution)/shard_map/ppermute | solution.py:418
  17.5 5.9 %collective-permute-start = (bf16[48,1408]{1,0:T(8,128)(2,1)S(1)}, bf16[48,1408]{1,0:T(8,128)(2,1)S(1)}, u32[]{:S(2)}, u32[]{:S(2)}) collective-permute-start(bf16[48,1408]{1,0:T(8,128)(2,1)S(1)} %get-tuple-element.23.refs_0_), channel_id=1, source_target_pairs={{0,12},{2,14},{4,0},{6,2},{8,4},{10,6},{12,8},{14,10},{1,13},{3,15... | collective-permute-start | bytes 405512 | tf_op jit(solution)/shard_map/ppermute | solution.py:418
  23.4 1.9 %collective-permute-start.1 = (bf16[48,1408]{1,0:T(8,128)(2,1)S(1)}, bf16[48,1408]{1,0:T(8,128)(2,1)S(1)}, u32[]{:S(2)}, u32[]{:S(2)}) collective-permute-start(bf16[48,1408]{1,0:T(8,128)(2,1)S(1)} %get-tuple-element.23.refs_0_), channel_id=1, source_target_pairs={{0,2},{2,4},{4,6},{6,8},{8,10},{10,12},{12,14},{14,0},{1,3},{3,5},... | collective-permute-start | bytes 405512 | tf_op jit(solution)/shard_map/ppermute | solution.py:418
  25.3 3.9 %collective-permute-start.2 = (bf16[48,1408]{1,0:T(8,128)(2,1)S(1)}, bf16[48,1408]{1,0:T(8,128)(2,1)S(1)}, u32[]{:S(2)}, u32[]{:S(2)}) collective-permute-start(bf16[48,1408]{1,0:T(8,128)(2,1)S(1)} %get-tuple-element.23.refs_0_), channel_id=1, source_target_pairs={{0,14},{2,0},{4,2},{6,4},{8,6},{10,8},{12,10},{14,12},{1,15},{3,1}... | collective-permute-start | bytes 405512 | tf_op jit(solution)/shard_map/ppermute | solution.py:418
  29.3 0.1 reshape.112
  29.4 0.1 slice_reduce_fusion
  29.5 0.1 reshape_squeeze.4
  29.6 0.1 pad.9.clone
  29.7 0.4 fusion.swap
  30.1 0.0 collective-permute-done.3.refs_2_
  30.2 3.6 %collective-permute-start.5 = (bf16[48,768]{1,0:T(8,128)(2,1)S(1)}, bf16[48,768]{1,0:T(8,128)(2,1)S(1)}, u32[]{:S(2)}, u32[]{:S(2)}) collective-permute-start(bf16[48,768]{1,0:T(8,128)(2,1)S(1)} %slice.12), channel_id=1, source_target_pairs={{0,4},{2,6},{4,8},{6,10},{8,12},{10,14},{12,0},{14,2},{1,5},{3,7},... | collective-permute-start | bytes 221192 | tf_op jit(solution)/shard_map/ppermute | solution.py:418
  33.8 0.0 collective-permute-done.refs_7_
  33.8 0.0 collective-permute-done.1.refs_1_
  33.8 1.2 collective-permute-done.2.refs_8_
  35.1 6.8 %collective-permute-start.6 = (bf16[48,640]{1,0:T(8,128)(2,1)S(1)}, bf16[48,640]{1,0:T(8,128)(2,1)S(1)}, u32[]{:S(2)}, u32[]{:S(2)}) collective-permute-start(bf16[48,640]{1,0:T(8,128)(2,1)S(1)} %slice.11), channel_id=1, source_target_pairs={{0,12},{2,14},{4,0},{6,2},{8,4},{10,6},{12,8},{14,10},{1,13},{3,15... | collective-permute-start | bytes 184328 | tf_op jit(solution)/shard_map/ppermute | solution.py:418
  41.9 1.9 %collective-permute-start.4 = (bf16[48,1408]{1,0:T(8,128)(2,1)S(1)}, bf16[48,1408]{1,0:T(8,128)(2,1)S(1)}, u32[]{:S(2)}, u32[]{:S(2)}) collective-permute-start(bf16[48,1408]{1,0:T(8,128)(2,1)S(1)} %collective-permute-done.3.refs_2_), channel_id=1, source_target_pairs={{0,2},{2,4},{4,6},{6,8},{8,10},{10,12},{12,14},{14,0},{1,3},{3,5},... | collective-permute-start | bytes 405512 | tf_op jit(solution)/shard_map/ppermute | solution.py:418
  43.9 3.9 %collective-permute-start.7 = (bf16[48,1408]{1,0:T(8,128)(2,1)S(1)}, bf16[48,1408]{1,0:T(8,128)(2,1)S(1)}, u32[]{:S(2)}, u32[]{:S(2)}) collective-permute-start(bf16[48,1408]{1,0:T(8,128)(2,1)S(1)} %collective-permute-done.refs_7_), channel_id=1, source_target_pairs={{0,14},{2,0},{4,2},{6,4},{8,6},{10,8},{12,10},{14,12},{1,15},{3,1}... | collective-permute-start | bytes 405512 | tf_op jit(solution)/shard_map/ppermute | solution.py:418
  47.8 0.1 fusion.4.extra
  47.9 0.0 copy-done.3
  47.9 0.4 shard_map.131.w
  48.3 0.0 collective-permute-done.5.refs_4_
  48.3 0.0 collective-permute-done.6.refs_5_
  48.3 3.7 %collective-permute-done.4.refs_3_ = bf16[48,1408]{1,0:T(8,128)(2,1)S(1)} collective-permute-done((bf16[48,1408]{1,0:T(8,128)(2,1)S(1)}, bf16[48,1408]{1,0:T(8,128)(2,1)S(1)}, u32[]{:S(2)}, u32[]{:S(2)}) %collective-permute-start.4) | collective-permute-done | bytes 135200 | tf_op jit(solution)/shard_map/ppermute | solution.py:418
  52.0 1.4 collective-permute-done.7.refs_6_
  53.4 1.3 shard_map.133.mine
  54.7 0.0 copy-start.7
  54.8 1.9 %collective-permute-start.8 = (bf16[384,1408]{1,0:T(8,128)(2,1)S(1)}, bf16[384,1408]{1,0:T(8,128)(2,1)S(1)}, u32[]{:S(2)}, u32[]{:S(2)}) collective-permute-start(bf16[384,1408]{1,0:T(8,128)(2,1)S(1)} %shard_map.133.mine), channel_id=1, source_target_pairs={{0,1},{1,0},{2,3},{3,2},{4,5},{5,4},{6,7},{7,6},{8,9},{9,8},{10,11... | collective-permute-start | bytes 3244040 | tf_op jit(solution)/shard_map/ppermute | solution.py:434
  56.7 2.8 %collective-permute-done.8.other = bf16[384,1408]{1,0:T(8,128)(2,1)S(1)} collective-permute-done((bf16[384,1408]{1,0:T(8,128)(2,1)S(1)}, bf16[384,1408]{1,0:T(8,128)(2,1)S(1)}, u32[]{:S(2)}, u32[]{:S(2)}) %collective-permute-start.8) | collective-permute-done | bytes 1081376 | tf_op jit(solution)/shard_map/ppermute | solution.py:434
  59.5 0.0 copy-start.1
  59.5 5.0 %shard_map.134 = (bf16[16,64,128]{2,1,0:T(8,128)(2,1)}, bf16[512,768]{1,0:T(8,128)(2,1)}, f32[8,768]{1,0:T(8,128)}) custom-call(bf16[384,1408]{1,0:T(8,128)(2,1)S(1)} %shard_map.133.mine, bf16[384,1408]{1,0:T(8,128)(2,1)S(1)} %collective-permute-done.8.other, bf16[1408,384]{1,0:T(8,128)(2,1)S(1)} %shard_map.131.w, bf16[768,768]{1,0:T(8,128)(2,1)S(1)} %fusion.swap, ...), custom_call_target="tpu_custom_call" | custom-call | flops 1782579200 | bytes 8388608 | tf_op jit(solution)/shard_map/pallas_call | solution.py:230
  64.5 0.0 copy-done.1
  64.5 0.0 copy-start.4
  64.5 6.9 %all-to-all-start = ((bf16[16,64,128]{2,1,0:T(8,128)(2,1)}), bf16[16,64,128]{2,1,0:T(8,128)(2,1)S(1)}, u32[]{:S(2)}, u32[]{:S(2)}) async-start(bf16[16,64,128]{2,1,0:T(8,128)(2,1)} %get-tuple-element.34), calls=%async_computation | async-start | bytes 524288 | tf_op jit(solution)/shard_map/all_to_all | solution.py:410
  71.4 0.0 copy-done.7
  71.4 1.0 multiply_sine_fusion
  72.4 0.1 pad_maximum_fusion.table
  72.5 8.5 %all-to-all-done.came = bf16[16,64,128]{2,1,0:T(8,128)(2,1)S(1)} async-done(((bf16[16,64,128]{2,1,0:T(8,128)(2,1)}), bf16[16,64,128]{2,1,0:T(8,128)(2,1)S(1)}, u32[]{:S(2)}, u32[]{:S(2)}) %all-to-all-start) | async-done | bytes 262176 | tf_op jit(solution)/shard_map/all_to_all | solution.py:410
  81.0 0.0 all-gather.3.cloned.1.call-done
  81.0 0.0 copy-done.4
  81.0 0.0 copy-start.2
  81.0 0.0 copy-start.5
  81.1 0.0 copy-start.6
  81.1 6.8 %shard_map.135 = (bf16[256,512]{1,0:T(8,128)(2,1)}, bf16[48,512]{1,0:T(8,128)(2,1)S(1)}) custom-call(bf16[16,64,128]{2,1,0:T(8,128)(2,1)S(1)} %all-to-all-done.came, bf16[16,352,512]{2,1,0:T(8,128)(2,1)} %bitcast.22, bf16[256,512]{1,0:T(8,128)(2,1)} %bitcast.24, bf16[1,512]{1,0:T(2,128)(2,1)S(1)} %broadcast_in_dim.30.mask, f32[1,512]{1,0:T(1,128)S(1)} %bitcast.18, ...), custom_call_target="tpu_custom_call" | custom-call | flops 2411724800 | bytes 8388608 | tf_op jit(solution)/shard_map/pallas_call | solution.py:313
  87.9 18.6 %all_gather.11.dvis = bf16[768,512]{1,0:T(8,128)(2,1)S(1)} all-gather(bf16[48,512]{1,0:T(8,128)(2,1)S(1)} %get-tuple-element.37), channel_id=1, replica_groups=mesh['y'=8,'x'=4,'z'=8,'core'=2] {'z','core'}, dimensions={0}, use_global_device_ids=true | all-gather | bytes 835584 | tf_op jit(solution)/shard_map/all_gather | solution.py:482
  106.5 0.0 copy-done.2
  106.5 0.0 copy-done.5
  106.5 0.0 copy-done.6
  106.5 4.1 %shard_map.136 = bf16[3328,128]{1,0:T(8,128)(2,1)S(1)} custom-call(bf16[768,512]{1,0:T(8,128)(2,1)S(1)} %all_gather.11.dvis, bf16[96,512]{1,0:T(8,128)(2,1)S(1)} %get-tuple-element.38.w_oe, bf16[768,768]{1,0:T(8,128)(2,1)S(1)} %fusion.swap, bf16[512,768]{1,0:T(8,128)(2,1)S(1)} %copy-done.5, f32[8,768]{1,0:T(8,128)S(1)} %copy-done.6, ...), custom_call_target="tpu_custom_call" | custom-call | flops 2621440000 | bytes 8388608 | tf_op jit(solution)/shard_map/pallas_call | solution.py:372
  110.6 17.6 %all_to_all.25 = bf16[4,832,128]{2,1,0:T(8,128)(2,1)S(1)} all-to-all(bf16[4,832,128]{2,1,0:T(8,128)(2,1)S(1)} %bitcast.16), channel_id=1, replica_groups=mesh['y'=8,'x'=4,'z'=8,'core'=2] {'x'}, dimensions={0} | all-to-all | bytes 1703936 | tf_op jit(solution)/shard_map/all_to_all | solution.py:410
  128.2 0.2 reduce_sum.24
  128.4 16.8 %all_to_all.26 = bf16[8,104,128]{2,1,0:T(8,128)(2,1)S(1)} all-to-all(bf16[8,104,128]{2,1,0:T(8,128)(2,1)S(1)} %bitcast.19), channel_id=1, replica_groups=mesh['y'=8,'x'=4,'z'=8,'core'=2] {'y'}, dimensions={0} | all-to-all | bytes 425984 | tf_op jit(solution)/shard_map/all_to_all | solution.py:410
  145.2 12.4 %all_to_all.27 = bf16[8,104,128]{2,1,0:T(8,128)(2,1)S(1)} all-to-all(bf16[8,104,128]{2,1,0:T(8,128)(2,1)S(1)} %broadcast_in_dim.33), channel_id=1, replica_groups=mesh['y'=8,'x'=4,'z'=8,'core'=2] {'y'}, dimensions={0} | all-to-all | bytes 425984 | tf_op jit(solution)/shard_map/all_to_all | solution.py:410
  157.6 0.0 copy-start
  157.6 0.1 broadcast_in_dim.35
  157.7 12.4 %all_to_all.28 = bf16[4,832,128]{2,1,0:T(8,128)(2,1)S(1)} all-to-all(bf16[4,832,128]{2,1,0:T(8,128)(2,1)S(1)} %broadcast_in_dim.35), channel_id=1, replica_groups=mesh['y'=8,'x'=4,'z'=8,'core'=2] {'x'}, dimensions={0} | all-to-all | bytes 1703936 | tf_op jit(solution)/shard_map/all_to_all | solution.py:410
  170.0 0.0 copy-done
  170.0 1.5 shard_map.137
  (9 shorter events, 0.1 us)
Async XLA Ops:
  7.2 73.9 %all-gather.3.cloned.1.call-start = ((), (), s32[]{:S(2)}) async-start(), calls=%async_computation.5 | async-start | bytes 6127616 | tf_op jit(solution)/shard_map/all_gather | solution.py:460
  11.3 36.6 %copy-start.3 = (bf16[3,1408,88]{1,2,0:T(8,128)(2,1)S(1)}, bf16[3,1408,88]{1,2,0:T(8,128)(2,1)}, u32[]{:S(2)}) copy-start(bf16[3,1408,88]{1,2,0:T(8,128)(2,1)} %param.15) | copy-start | bytes 2230276
  11.3 18.8 %collective-permute-start.3 = (bf16[48,1408]{1,0:T(8,128)(2,1)S(1)}, bf16[48,1408]{1,0:T(8,128)(2,1)S(1)}, u32[]{:S(2)}, u32[]{:S(2)}) collective-permute-start(bf16[48,1408]{1,0:T(8,128)(2,1)S(1)} %get-tuple-element.23.refs_0_), channel_id=1, source_target_pairs={{0,4},{2,6},{4,8},{6,10},{8,12},{10,14},{12,0},{14,2},{1,5},{3,7},... | collective-permute-start | bytes 405512 | tf_op jit(solution)/shard_map/ppermute | solution.py:418
  17.5 16.3 %collective-permute-start = (bf16[48,1408]{1,0:T(8,128)(2,1)S(1)}, bf16[48,1408]{1,0:T(8,128)(2,1)S(1)}, u32[]{:S(2)}, u32[]{:S(2)}) collective-permute-start(bf16[48,1408]{1,0:T(8,128)(2,1)S(1)} %get-tuple-element.23.refs_0_), channel_id=1, source_target_pairs={{0,12},{2,14},{4,0},{6,2},{8,4},{10,6},{12,8},{14,10},{1,13},{3,15... | collective-permute-start | bytes 405512 | tf_op jit(solution)/shard_map/ppermute | solution.py:418
  23.4 10.4 %collective-permute-start.1 = (bf16[48,1408]{1,0:T(8,128)(2,1)S(1)}, bf16[48,1408]{1,0:T(8,128)(2,1)S(1)}, u32[]{:S(2)}, u32[]{:S(2)}) collective-permute-start(bf16[48,1408]{1,0:T(8,128)(2,1)S(1)} %get-tuple-element.23.refs_0_), channel_id=1, source_target_pairs={{0,2},{2,4},{4,6},{6,8},{8,10},{10,12},{12,14},{14,0},{1,3},{3,5},... | collective-permute-start | bytes 405512 | tf_op jit(solution)/shard_map/ppermute | solution.py:418
  25.3 9.7 %collective-permute-start.2 = (bf16[48,1408]{1,0:T(8,128)(2,1)S(1)}, bf16[48,1408]{1,0:T(8,128)(2,1)S(1)}, u32[]{:S(2)}, u32[]{:S(2)}) collective-permute-start(bf16[48,1408]{1,0:T(8,128)(2,1)S(1)} %get-tuple-element.23.refs_0_), channel_id=1, source_target_pairs={{0,14},{2,0},{4,2},{6,4},{8,6},{10,8},{12,10},{14,12},{1,15},{3,1}... | collective-permute-start | bytes 405512 | tf_op jit(solution)/shard_map/ppermute | solution.py:418
  30.2 18.1 %collective-permute-start.5 = (bf16[48,768]{1,0:T(8,128)(2,1)S(1)}, bf16[48,768]{1,0:T(8,128)(2,1)S(1)}, u32[]{:S(2)}, u32[]{:S(2)}) collective-permute-start(bf16[48,768]{1,0:T(8,128)(2,1)S(1)} %slice.12), channel_id=1, source_target_pairs={{0,4},{2,6},{4,8},{6,10},{8,12},{10,14},{12,0},{14,2},{1,5},{3,7},... | collective-permute-start | bytes 221192 | tf_op jit(solution)/shard_map/ppermute | solution.py:418
  35.1 13.2 %collective-permute-start.6 = (bf16[48,640]{1,0:T(8,128)(2,1)S(1)}, bf16[48,640]{1,0:T(8,128)(2,1)S(1)}, u32[]{:S(2)}, u32[]{:S(2)}) collective-permute-start(bf16[48,640]{1,0:T(8,128)(2,1)S(1)} %slice.11), channel_id=1, source_target_pairs={{0,12},{2,14},{4,0},{6,2},{8,4},{10,6},{12,8},{14,10},{1,13},{3,15... | collective-permute-start | bytes 184328 | tf_op jit(solution)/shard_map/ppermute | solution.py:418
  41.9 10.1 %collective-permute-start.4 = (bf16[48,1408]{1,0:T(8,128)(2,1)S(1)}, bf16[48,1408]{1,0:T(8,128)(2,1)S(1)}, u32[]{:S(2)}, u32[]{:S(2)}) collective-permute-start(bf16[48,1408]{1,0:T(8,128)(2,1)S(1)} %collective-permute-done.3.refs_2_), channel_id=1, source_target_pairs={{0,2},{2,4},{4,6},{6,8},{8,10},{10,12},{12,14},{14,0},{1,3},{3,5},... | collective-permute-start | bytes 405512 | tf_op jit(solution)/shard_map/ppermute | solution.py:418
  43.9 9.6 %collective-permute-start.7 = (bf16[48,1408]{1,0:T(8,128)(2,1)S(1)}, bf16[48,1408]{1,0:T(8,128)(2,1)S(1)}, u32[]{:S(2)}, u32[]{:S(2)}) collective-permute-start(bf16[48,1408]{1,0:T(8,128)(2,1)S(1)} %collective-permute-done.refs_7_), channel_id=1, source_target_pairs={{0,14},{2,0},{4,2},{6,4},{8,6},{10,8},{12,10},{14,12},{1,15},{3,1}... | collective-permute-start | bytes 405512 | tf_op jit(solution)/shard_map/ppermute | solution.py:418
  54.7 16.7 %copy-start.7 = (bf16[512]{0:T(512)(128)(2,1)S(1)}, bf16[512]{0:T(512)(128)(2,1)}, u32[]{:S(2)}) copy-start(bf16[512]{0:T(512)(128)(2,1)} %param.18) | copy-start | bytes 3076
  54.8 4.7 %collective-permute-start.8 = (bf16[384,1408]{1,0:T(8,128)(2,1)S(1)}, bf16[384,1408]{1,0:T(8,128)(2,1)S(1)}, u32[]{:S(2)}, u32[]{:S(2)}) collective-permute-start(bf16[384,1408]{1,0:T(8,128)(2,1)S(1)} %shard_map.133.mine), channel_id=1, source_target_pairs={{0,1},{1,0},{2,3},{3,2},{4,5},{5,4},{6,7},{7,6},{8,9},{9,8},{10,11... | collective-permute-start | bytes 3244040 | tf_op jit(solution)/shard_map/ppermute | solution.py:434
  59.5 5.0 %copy-start.1 = (bf16[384,1408]{1,0:T(8,128)(2,1)}, bf16[384,1408]{1,0:T(8,128)(2,1)S(1)}, u32[]{:S(2)}) copy-start(bf16[384,1408]{1,0:T(8,128)(2,1)S(1)} %collective-permute-done.8.other) | copy-start | bytes 3244036
  64.5 16.5 %copy-start.4 = (f32[512]{0:T(512)S(1)}, f32[512]{0:T(512)}, u32[]{:S(2)}) copy-start(f32[512]{0:T(512)} %param.19) | copy-start | bytes 6148
  64.5 16.5 %all-to-all-start = ((bf16[16,64,128]{2,1,0:T(8,128)(2,1)}), bf16[16,64,128]{2,1,0:T(8,128)(2,1)S(1)}, u32[]{:S(2)}, u32[]{:S(2)}) async-start(bf16[16,64,128]{2,1,0:T(8,128)(2,1)} %get-tuple-element.34), calls=%async_computation | async-start | bytes 524288 | tf_op jit(solution)/shard_map/all_to_all | solution.py:410
  81.0 25.5 %copy-start.2 = (bf16[384,1408]{1,0:T(8,128)(2,1)S(1)}, bf16[384,1408]{1,0:T(8,128)(2,1)}, u32[]{:S(2)}) copy-start(bf16[384,1408]{1,0:T(8,128)(2,1)} %copy-done.1) | copy-start | bytes 3244036
  81.0 25.5 %copy-start.5 = (bf16[512,768]{1,0:T(8,128)(2,1)S(1)}, bf16[512,768]{1,0:T(8,128)(2,1)}, u32[]{:S(2)}) copy-start(bf16[512,768]{1,0:T(8,128)(2,1)} %get-tuple-element.39.saved) | copy-start | bytes 2359300
  81.1 25.5 %copy-start.6 = (f32[8,768]{1,0:T(8,128)S(1)}, f32[8,768]{1,0:T(8,128)}, u32[]{:S(2)}) copy-start(f32[8,768]{1,0:T(8,128)} %get-tuple-element.40.stats) | copy-start | bytes 73732
  157.6 12.5 %copy-start = (bf16[1408,512]{1,0:T(8,128)(2,1)S(1)}, bf16[1408,512]{1,0:T(8,128)(2,1)}, u32[]{:S(2)}) copy-start(bf16[1408,512]{1,0:T(8,128)(2,1)} %w_e2d.3) | copy-start | bytes 4325380
Sparse Core Ops, SparseCore 0:
  11.4 57.9 all-gather.2

commit v9 on v7

--- a/solution.py
+++ b/solution.py
@@ -103,19 +103,20 @@
     loads = [
         pltpu.make_async_copy(w_out, out_in, sems.at[0]),
         pltpu.make_async_copy(w_e2d, e2d_in, sems.at[1]),
-        pltpu.make_async_copy(fc_in, packed.at[pl.ds(0, HID)], sems.at[2]),
-        pltpu.make_async_copy(fc_out, packed.at[pl.ds(HID, HID)], sems.at[3])]
+        pltpu.make_async_copy(fc_in, pack.at[pl.ds(0, HID)], sems.at[2]),
+        pltpu.make_async_copy(fc_out, pack.at[pl.ds(HID, HID)], sems.at[3])]
     for copy in loads:
         copy.start()
-    for copy in loads:
+    for copy in loads[:2]:
         copy.wait()
     both = jnp.concatenate([dot(out_in[...], e2d_in[...]), jnp.zeros((HP - HD, DD), F32)], axis=0).astype(BF16)
     w_oe[...] = both
-    packed[2 * HID:, :] = both
-    done = pltpu.make_async_copy(packed, pack, sems.at[4])
+    packed[...] = both
+    done = pltpu.make_async_copy(packed, pack.at[pl.ds(2 * HID, HP)], sems.at[4])
     done.start()
     x_vis[...] = dot(x_slot[...], e2d_in[...]).astype(BF16)
-    done.wait()
+    for copy in (*loads[2:], done):
+        copy.wait()
 
 
 def pack_up(x_slot, *args):
@@ -129,7 +130,7 @@
         in_specs=[vmem] + [hbm] * len(args),
         out_specs=[vmem, vmem, hbm],
         scratch_shapes=[pltpu.VMEM((HD, width), BF16), pltpu.VMEM((width, DD), BF16),
-                        pltpu.VMEM((2 * HID + HP, DD), BF16), pltpu.SemaphoreType.DMA((5,))],
+                        pltpu.VMEM((HP, DD), BF16), pltpu.SemaphoreType.DMA((5,))],
         compiler_params=pltpu.CompilerParams(vmem_limit_bytes=12 << 20),
         cost_estimate=pl.CostEstimate(flops=200 << 20, bytes_accessed=3 << 20, transcendentals=0),
     )(x_slot, *[pltpu.with_memory_space_constraint(arg, pltpu.HBM) for arg in args])
@@ -208,7 +209,7 @@
         total = jnp.sum(expo, axis=0, keepdims=True)
         keep_stats[0:1, cols] = top
         keep_stats[1:2, cols] = total
-        ctx.append(dot(vt, (expo / total).astype(BF16)))
+        ctx.append(dot(vt, (expo * (1.0 / total)).astype(BF16)))
     sums = pltpu.make_async_copy(keep_stats, stats, sems.at[3])
     sums.start()
     ctx = jnp.concatenate(ctx, axis=1).astype(BF16)
@@ -345,7 +346,7 @@
     for i in range(3):
         cols = slice(256 * i, 256 * (i + 1))
         scores = dot(k, q[:, cols]) + dead
-        probs = jnp.exp(scores - keep_stats[0:1, cols]) / keep_stats[1:2, cols]
+        probs = jnp.exp(scores - keep_stats[0:1, cols]) * (1.0 / keep_stats[1:2, cols])
         dprob = dot(v, dctx[:, cols])
         inner = jnp.sum(probs * dprob, axis=0, keepdims=True)
         ds = (probs * (dprob - inner)).astype(BF16)

time: 176 us -> 182 us (1.034)
  Pallas kernels: 23.4 us -> 29.8 us
    pallas_call x1, Pallas kernels: 2.77 us -> 9.09 us  [pack_up(): pl.pallas_call(pack_body, out_shape=[jax.ShapeDtypeStruct((CAP, DD), BF16...]
where the time goes in v9:
time: 182 us
  blocking collectives  77.5 us (43%)
  starting transfers between devices  38.9 us (21%)
  Pallas kernels  29.8 us (16%)
  waiting for transfers between devices  18.8 us (10%)
  between operations  14.3 us (8%)
    all_to_all x4, blocking collectives, exchange(): return lax.all_to_all(block, axis, 0, 0, tiled=True)  58.9 us
    ppermute x7, starting transfers between devices, z_shift(): return lax.ppermute(block, 'z', [(z, (z + step) % NZ) for z in range(NZ)])  28.5 us
    all_gather x1, blocking collectives, local(): dvis = lax.all_gather(dvis_own, SEQ, axis=0, tiled=True)  18.6 us
    pallas_call x1, Pallas kernels, pack_up(): pl.pallas_call(pack_body, out_shape=[jax.ShapeDtypeStruct((CAP, DD), BF16...  9.09 us
    all_to_all x1, waiting for transfers between devices, exchange(): return lax.all_to_all(block, axis, 0, 0, tiled=True)  8.55 us
    all_to_all x1, starting transfers between devices, exchange(): return lax.all_to_all(block, axis, 0, 0, tiled=True)  8.4 us
    ppermute x7, waiting for transfers between devices, z_shift(): return lax.ppermute(block, 'z', [(z, (z + step) % NZ) for z in range(NZ)])  7.52 us
    pallas_call x1, Pallas kernels, decode(): pl.pallas_call(decode_body, out_shape=[jax.ShapeDtypeStruct((FDEV, DD), B...  6.83 us
  transfers between devices with their start and end apart: 10, of which 4 were waited for; matrix products, arithmetic and copies ran while one was open for 1% of the time, Pallas kernels for 4%

profile of v9, /device:TPU:64, one launch (start us, length us, event | category | flops | bytes accessed | tf_op | source)
XLA Modules:
  0.0 181.6 jit_solution(3256141205522534834)
XLA Ops:
  7.2 0.0 all-gather.3.cloned.1.call-start
  7.2 1.3 shard_map.130
  8.5 0.0 copy-start.3
  8.6 9.1 %shard_map.132 = (bf16[48,512]{1,0:T(8,128)(2,1)S(1)}, bf16[96,512]{1,0:T(8,128)(2,1)S(1)}, bf16[352,512]{1,0:T(8,128)(2,1)}) custom-call(bf16[48,1408]{1,0:T(8,128)(2,1)S(1)} %get-tuple-element.21.x_slot, bf16[88,1408]{1,0:T(8,128)(2,1)} %w_out.1, bf16[1408,512]{1,0:T(8,128)(2,1)} %w_e2d.3, bf16[128,512]{1,0:T(8,128)(2,1)} %fc_in.1, bf16[128,512]{1,0:T(8,128)(2,1)} %fc_out.1), custom_call_target="tpu_custom_call" | custom-call | flops 209715200 | bytes 3145728 | tf_op jit(solution)/shard_map/pallas_call | solution.py:126
  17.7 0.0 all-gather.3.cloned.1.call-update
  17.7 6.1 %collective-permute-start.1 = (bf16[48,1408]{1,0:T(8,128)(2,1)S(1)}, bf16[48,1408]{1,0:T(8,128)(2,1)S(1)}, u32[]{:S(2)}, u32[]{:S(2)}) collective-permute-start(bf16[48,1408]{1,0:T(8,128)(2,1)S(1)} %get-tuple-element.20.refs_0_), channel_id=1, source_target_pairs={{0,4},{2,6},{4,8},{6,10},{8,12},{10,14},{12,0},{14,2},{1,5},{3,7},... | collective-permute-start | bytes 405512 | tf_op jit(solution)/shard_map/ppermute | solution.py:418
  23.8 5.9 %collective-permute-start.4 = (bf16[48,1408]{1,0:T(8,128)(2,1)S(1)}, bf16[48,1408]{1,0:T(8,128)(2,1)S(1)}, u32[]{:S(2)}, u32[]{:S(2)}) collective-permute-start(bf16[48,1408]{1,0:T(8,128)(2,1)S(1)} %get-tuple-element.20.refs_0_), channel_id=1, source_target_pairs={{0,12},{2,14},{4,0},{6,2},{8,4},{10,6},{12,8},{14,10},{1,13},{3,15... | collective-permute-start | bytes 405512 | tf_op jit(solution)/shard_map/ppermute | solution.py:418
  29.7 1.9 %collective-permute-start = (bf16[48,1408]{1,0:T(8,128)(2,1)S(1)}, bf16[48,1408]{1,0:T(8,128)(2,1)S(1)}, u32[]{:S(2)}, u32[]{:S(2)}) collective-permute-start(bf16[48,1408]{1,0:T(8,128)(2,1)S(1)} %get-tuple-element.20.refs_0_), channel_id=1, source_target_pairs={{0,2},{2,4},{4,6},{6,8},{8,10},{10,12},{12,14},{14,0},{1,3},{3,5},... | collective-permute-start | bytes 405512 | tf_op jit(solution)/shard_map/ppermute | solution.py:418
  31.6 3.9 %collective-permute-start.6 = (bf16[48,1408]{1,0:T(8,128)(2,1)S(1)}, bf16[48,1408]{1,0:T(8,128)(2,1)S(1)}, u32[]{:S(2)}, u32[]{:S(2)}) collective-permute-start(bf16[48,1408]{1,0:T(8,128)(2,1)S(1)} %get-tuple-element.20.refs_0_), channel_id=1, source_target_pairs={{0,14},{2,0},{4,2},{6,4},{8,6},{10,8},{12,10},{14,12},{1,15},{3,1}... | collective-permute-start | bytes 405512 | tf_op jit(solution)/shard_map/ppermute | solution.py:418
  35.5 0.1 reshape.112
  35.6 0.1 slice_reduce_fusion
  35.7 0.1 reshape_squeeze.4
  35.9 0.1 pad.9.clone
  35.9 0.0 copy-done.3
  35.9 0.4 shard_map.131.w
  36.3 0.4 fusion.swap
  36.8 0.0 collective-permute-done.1.refs_2_
  36.8 3.6 %collective-permute-start.3 = (bf16[48,1408]{1,0:T(8,128)(2,1)S(1)}, bf16[48,1408]{1,0:T(8,128)(2,1)S(1)}, u32[]{:S(2)}, u32[]{:S(2)}) collective-permute-start(bf16[48,1408]{1,0:T(8,128)(2,1)S(1)} %collective-permute-done.1.refs_2_), channel_id=1, source_target_pairs={{0,4},{2,6},{4,8},{6,10},{8,12},{10,14},{12,0},{14,2},{1,5},{3,7},... | collective-permute-start | bytes 405512 | tf_op jit(solution)/shard_map/ppermute | solution.py:418
  40.4 5.1 %collective-permute-start.2 = (bf16[48,1408]{1,0:T(8,128)(2,1)S(1)}, bf16[48,1408]{1,0:T(8,128)(2,1)S(1)}, u32[]{:S(2)}, u32[]{:S(2)}) collective-permute-start(bf16[48,1408]{1,0:T(8,128)(2,1)S(1)} %collective-permute-done.1.refs_2_), channel_id=1, source_target_pairs={{0,2},{2,4},{4,6},{6,8},{8,10},{10,12},{12,14},{14,0},{1,3},{3,5},... | collective-permute-start | bytes 405512 | tf_op jit(solution)/shard_map/ppermute | solution.py:418
  45.6 0.0 collective-permute-done.4.refs_6_
  45.6 1.9 %collective-permute-start.5 = (bf16[48,1408]{1,0:T(8,128)(2,1)S(1)}, bf16[48,1408]{1,0:T(8,128)(2,1)S(1)}, u32[]{:S(2)}, u32[]{:S(2)}) collective-permute-start(bf16[48,1408]{1,0:T(8,128)(2,1)S(1)} %collective-permute-done.4.refs_6_), channel_id=1, source_target_pairs={{0,14},{2,0},{4,2},{6,4},{8,6},{10,8},{12,10},{14,12},{1,15},{3,1}... | collective-permute-start | bytes 405512 | tf_op jit(solution)/shard_map/ppermute | solution.py:418
  47.5 0.1 fusion.4.extra
  47.6 4.8 %collective-permute-done.3.refs_4_ = bf16[48,1408]{1,0:T(8,128)(2,1)S(1)} collective-permute-done((bf16[48,1408]{1,0:T(8,128)(2,1)S(1)}, bf16[48,1408]{1,0:T(8,128)(2,1)S(1)}, u32[]{:S(2)}, u32[]{:S(2)}) %collective-permute-start.3) | collective-permute-done | bytes 135200 | tf_op jit(solution)/shard_map/ppermute | solution.py:418
  52.5 0.0 collective-permute-done.refs_1_
  52.5 0.0 collective-permute-done.6.refs_7_
  52.5 2.7 %collective-permute-done.2.refs_3_ = bf16[48,1408]{1,0:T(8,128)(2,1)S(1)} collective-permute-done((bf16[48,1408]{1,0:T(8,128)(2,1)S(1)}, bf16[48,1408]{1,0:T(8,128)(2,1)S(1)}, u32[]{:S(2)}, u32[]{:S(2)}) %collective-permute-start.2) | collective-permute-done | bytes 135200 | tf_op jit(solution)/shard_map/ppermute | solution.py:418
  55.1 0.0 collective-permute-done.5.refs_5_
  55.1 1.5 shard_map.133.mine
  56.6 0.0 copy-start.7
  56.6 1.9 %collective-permute-start.7 = (bf16[384,1408]{1,0:T(8,128)(2,1)S(1)}, bf16[384,1408]{1,0:T(8,128)(2,1)S(1)}, u32[]{:S(2)}, u32[]{:S(2)}) collective-permute-start(bf16[384,1408]{1,0:T(8,128)(2,1)S(1)} %shard_map.133.mine), channel_id=1, source_target_pairs={{0,1},{1,0},{2,3},{3,2},{4,5},{5,4},{6,7},{7,6},{8,9},{9,8},{10,11... | collective-permute-start | bytes 3244040 | tf_op jit(solution)/shard_map/ppermute | solution.py:432
  58.5 2.7 %collective-permute-done.7.other = bf16[384,1408]{1,0:T(8,128)(2,1)S(1)} collective-permute-done((bf16[384,1408]{1,0:T(8,128)(2,1)S(1)}, bf16[384,1408]{1,0:T(8,128)(2,1)S(1)}, u32[]{:S(2)}, u32[]{:S(2)}) %collective-permute-start.7) | collective-permute-done | bytes 1081376 | tf_op jit(solution)/shard_map/ppermute | solution.py:432
  61.2 0.0 copy-start.1
  61.2 5.0 %shard_map.134 = (bf16[16,64,128]{2,1,0:T(8,128)(2,1)}, bf16[512,768]{1,0:T(8,128)(2,1)}, f32[8,768]{1,0:T(8,128)}) custom-call(bf16[384,1408]{1,0:T(8,128)(2,1)S(1)} %shard_map.133.mine, bf16[384,1408]{1,0:T(8,128)(2,1)S(1)} %collective-permute-done.7.other, bf16[1408,384]{1,0:T(8,128)(2,1)S(1)} %shard_map.131.w, bf16[768,768]{1,0:T(8,128)(2,1)S(1)} %fusion.swap, ...), custom_call_target="tpu_custom_call" | custom-call | flops 1782579200 | bytes 8388608 | tf_op jit(solution)/shard_map/pallas_call | solution.py:230
  66.2 0.0 copy-done.1
  66.2 0.0 copy-start.4
  66.3 8.4 %all-to-all-start = ((bf16[16,64,128]{2,1,0:T(8,128)(2,1)}), bf16[16,64,128]{2,1,0:T(8,128)(2,1)S(1)}, u32[]{:S(2)}, u32[]{:S(2)}) async-start(bf16[16,64,128]{2,1,0:T(8,128)(2,1)} %get-tuple-element.28), calls=%async_computation | async-start | bytes 524288 | tf_op jit(solution)/shard_map/all_to_all | solution.py:410
  74.7 0.0 copy-done.7
  74.7 1.0 multiply_sine_fusion
  75.7 0.1 pad_maximum_fusion.table
  75.8 8.5 %all-to-all-done.came = bf16[16,64,128]{2,1,0:T(8,128)(2,1)S(1)} async-done(((bf16[16,64,128]{2,1,0:T(8,128)(2,1)}), bf16[16,64,128]{2,1,0:T(8,128)(2,1)S(1)}, u32[]{:S(2)}, u32[]{:S(2)}) %all-to-all-start) | async-done | bytes 262176 | tf_op jit(solution)/shard_map/all_to_all | solution.py:410
  84.3 0.0 all-gather.3.cloned.1.call-done
  84.3 0.0 copy-done.4
  84.3 0.0 copy-start.2
  84.3 0.0 copy-start.5
  84.3 0.0 copy-start.6
  84.3 6.8 %shard_map.135 = (bf16[256,512]{1,0:T(8,128)(2,1)}, bf16[48,512]{1,0:T(8,128)(2,1)S(1)}) custom-call(bf16[16,64,128]{2,1,0:T(8,128)(2,1)S(1)} %all-to-all-done.came, bf16[16,352,512]{2,1,0:T(8,128)(2,1)} %bitcast.22, bf16[256,512]{1,0:T(8,128)(2,1)} %bitcast.24, bf16[1,512]{1,0:T(2,128)(2,1)S(1)} %broadcast_in_dim.30.mask, f32[1,512]{1,0:T(1,128)S(1)} %bitcast.18, ...), custom_call_target="tpu_custom_call" | custom-call | flops 2411724800 | bytes 8388608 | tf_op jit(solution)/shard_map/pallas_call | solution.py:313
  91.2 18.6 %all_gather.11.dvis = bf16[768,512]{1,0:T(8,128)(2,1)S(1)} all-gather(bf16[48,512]{1,0:T(8,128)(2,1)S(1)} %get-tuple-element.31), channel_id=1, replica_groups=mesh['y'=8,'x'=4,'z'=8,'core'=2] {'z','core'}, dimensions={0}, use_global_device_ids=true | all-gather | bytes 835584 | tf_op jit(solution)/shard_map/all_gather | solution.py:480
  109.8 0.0 copy-done.2
  109.8 0.0 copy-done.5
  109.8 0.0 copy-done.6
  109.8 4.1 %shard_map.136 = bf16[3328,128]{1,0:T(8,128)(2,1)S(1)} custom-call(bf16[768,512]{1,0:T(8,128)(2,1)S(1)} %all_gather.11.dvis, bf16[96,512]{1,0:T(8,128)(2,1)S(1)} %get-tuple-element.32.w_oe, bf16[768,768]{1,0:T(8,128)(2,1)S(1)} %fusion.swap, bf16[512,768]{1,0:T(8,128)(2,1)S(1)} %copy-done.5, f32[8,768]{1,0:T(8,128)S(1)} %copy-done.6, ...), custom_call_target="tpu_custom_call" | custom-call | flops 2621440000 | bytes 8388608 | tf_op jit(solution)/shard_map/pallas_call | solution.py:372
  113.9 17.6 %all_to_all.25 = bf16[4,832,128]{2,1,0:T(8,128)(2,1)S(1)} all-to-all(bf16[4,832,128]{2,1,0:T(8,128)(2,1)S(1)} %bitcast.16), channel_id=1, replica_groups=mesh['y'=8,'x'=4,'z'=8,'core'=2] {'x'}, dimensions={0} | all-to-all | bytes 1703936 | tf_op jit(solution)/shard_map/all_to_all | solution.py:410
  131.5 0.2 reduce_sum.24
  131.7 16.6 %all_to_all.26 = bf16[8,104,128]{2,1,0:T(8,128)(2,1)S(1)} all-to-all(bf16[8,104,128]{2,1,0:T(8,128)(2,1)S(1)} %bitcast.19), channel_id=1, replica_groups=mesh['y'=8,'x'=4,'z'=8,'core'=2] {'y'}, dimensions={0} | all-to-all | bytes 425984 | tf_op jit(solution)/shard_map/all_to_all | solution.py:410
  148.4 12.4 %all_to_all.27 = bf16[8,104,128]{2,1,0:T(8,128)(2,1)S(1)} all-to-all(bf16[8,104,128]{2,1,0:T(8,128)(2,1)S(1)} %broadcast_in_dim.33), channel_id=1, replica_groups=mesh['y'=8,'x'=4,'z'=8,'core'=2] {'y'}, dimensions={0} | all-to-all | bytes 425984 | tf_op jit(solution)/shard_map/all_to_all | solution.py:410
  160.7 0.0 copy-start
  160.7 0.1 broadcast_in_dim.35
  160.8 12.4 %all_to_all.28 = bf16[4,832,128]{2,1,0:T(8,128)(2,1)S(1)} all-to-all(bf16[4,832,128]{2,1,0:T(8,128)(2,1)S(1)} %broadcast_in_dim.35), channel_id=1, replica_groups=mesh['y'=8,'x'=4,'z'=8,'core'=2] {'x'}, dimensions={0} | all-to-all | bytes 1703936 | tf_op jit(solution)/shard_map/all_to_all | solution.py:410
  173.2 0.0 copy-done
  173.2 1.5 shard_map.137
  (7 shorter events, 0.1 us)
Async XLA Ops:
  7.2 77.1 %all-gather.3.cloned.1.call-start = ((), (), s32[]{:S(2)}) async-start(), calls=%async_computation.5 | async-start | bytes 6127616 | tf_op jit(solution)/shard_map/all_gather | solution.py:458
  8.5 27.4 %copy-start.3 = (bf16[3,1408,88]{1,2,0:T(8,128)(2,1)S(1)}, bf16[3,1408,88]{1,2,0:T(8,128)(2,1)}, u32[]{:S(2)}) copy-start(bf16[3,1408,88]{1,2,0:T(8,128)(2,1)} %param.15) | copy-start | bytes 2230276
  17.7 19.1 %collective-permute-start.1 = (bf16[48,1408]{1,0:T(8,128)(2,1)S(1)}, bf16[48,1408]{1,0:T(8,128)(2,1)S(1)}, u32[]{:S(2)}, u32[]{:S(2)}) collective-permute-start(bf16[48,1408]{1,0:T(8,128)(2,1)S(1)} %get-tuple-element.20.refs_0_), channel_id=1, source_target_pairs={{0,4},{2,6},{4,8},{6,10},{8,12},{10,14},{12,0},{14,2},{1,5},{3,7},... | collective-permute-start | bytes 405512 | tf_op jit(solution)/shard_map/ppermute | solution.py:418
  23.8 21.8 %collective-permute-start.4 = (bf16[48,1408]{1,0:T(8,128)(2,1)S(1)}, bf16[48,1408]{1,0:T(8,128)(2,1)S(1)}, u32[]{:S(2)}, u32[]{:S(2)}) collective-permute-start(bf16[48,1408]{1,0:T(8,128)(2,1)S(1)} %get-tuple-element.20.refs_0_), channel_id=1, source_target_pairs={{0,12},{2,14},{4,0},{6,2},{8,4},{10,6},{12,8},{14,10},{1,13},{3,15... | collective-permute-start | bytes 405512 | tf_op jit(solution)/shard_map/ppermute | solution.py:418
  29.7 22.8 %collective-permute-start = (bf16[48,1408]{1,0:T(8,128)(2,1)S(1)}, bf16[48,1408]{1,0:T(8,128)(2,1)S(1)}, u32[]{:S(2)}, u32[]{:S(2)}) collective-permute-start(bf16[48,1408]{1,0:T(8,128)(2,1)S(1)} %get-tuple-element.20.refs_0_), channel_id=1, source_target_pairs={{0,2},{2,4},{4,6},{6,8},{8,10},{10,12},{12,14},{14,0},{1,3},{3,5},... | collective-permute-start | bytes 405512 | tf_op jit(solution)/shard_map/ppermute | solution.py:418
  31.6 20.9 %collective-permute-start.6 = (bf16[48,1408]{1,0:T(8,128)(2,1)S(1)}, bf16[48,1408]{1,0:T(8,128)(2,1)S(1)}, u32[]{:S(2)}, u32[]{:S(2)}) collective-permute-start(bf16[48,1408]{1,0:T(8,128)(2,1)S(1)} %get-tuple-element.20.refs_0_), channel_id=1, source_target_pairs={{0,14},{2,0},{4,2},{6,4},{8,6},{10,8},{12,10},{14,12},{1,15},{3,1}... | collective-permute-start | bytes 405512 | tf_op jit(solution)/shard_map/ppermute | solution.py:418
  36.8 15.7 %collective-permute-start.3 = (bf16[48,1408]{1,0:T(8,128)(2,1)S(1)}, bf16[48,1408]{1,0:T(8,128)(2,1)S(1)}, u32[]{:S(2)}, u32[]{:S(2)}) collective-permute-start(bf16[48,1408]{1,0:T(8,128)(2,1)S(1)} %collective-permute-done.1.refs_2_), channel_id=1, source_target_pairs={{0,4},{2,6},{4,8},{6,10},{8,12},{10,14},{12,0},{14,2},{1,5},{3,7},... | collective-permute-start | bytes 405512 | tf_op jit(solution)/shard_map/ppermute | solution.py:418
  40.4 14.7 %collective-permute-start.2 = (bf16[48,1408]{1,0:T(8,128)(2,1)S(1)}, bf16[48,1408]{1,0:T(8,128)(2,1)S(1)}, u32[]{:S(2)}, u32[]{:S(2)}) collective-permute-start(bf16[48,1408]{1,0:T(8,128)(2,1)S(1)} %collective-permute-done.1.refs_2_), channel_id=1, source_target_pairs={{0,2},{2,4},{4,6},{6,8},{8,10},{10,12},{12,14},{14,0},{1,3},{3,5},... | collective-permute-start | bytes 405512 | tf_op jit(solution)/shard_map/ppermute | solution.py:418
  45.6 9.5 %collective-permute-start.5 = (bf16[48,1408]{1,0:T(8,128)(2,1)S(1)}, bf16[48,1408]{1,0:T(8,128)(2,1)S(1)}, u32[]{:S(2)}, u32[]{:S(2)}) collective-permute-start(bf16[48,1408]{1,0:T(8,128)(2,1)S(1)} %collective-permute-done.4.refs_6_), channel_id=1, source_target_pairs={{0,14},{2,0},{4,2},{6,4},{8,6},{10,8},{12,10},{14,12},{1,15},{3,1}... | collective-permute-start | bytes 405512 | tf_op jit(solution)/shard_map/ppermute | solution.py:418
  56.6 18.1 %copy-start.7 = (bf16[512]{0:T(512)(128)(2,1)S(1)}, bf16[512]{0:T(512)(128)(2,1)}, u32[]{:S(2)}) copy-start(bf16[512]{0:T(512)(128)(2,1)} %param.18) | copy-start | bytes 3076
  56.6 4.6 %collective-permute-start.7 = (bf16[384,1408]{1,0:T(8,128)(2,1)S(1)}, bf16[384,1408]{1,0:T(8,128)(2,1)S(1)}, u32[]{:S(2)}, u32[]{:S(2)}) collective-permute-start(bf16[384,1408]{1,0:T(8,128)(2,1)S(1)} %shard_map.133.mine), channel_id=1, source_target_pairs={{0,1},{1,0},{2,3},{3,2},{4,5},{5,4},{6,7},{7,6},{8,9},{9,8},{10,11... | collective-permute-start | bytes 3244040 | tf_op jit(solution)/shard_map/ppermute | solution.py:432
  61.2 5.0 %copy-start.1 = (bf16[384,1408]{1,0:T(8,128)(2,1)}, bf16[384,1408]{1,0:T(8,128)(2,1)S(1)}, u32[]{:S(2)}) copy-start(bf16[384,1408]{1,0:T(8,128)(2,1)S(1)} %collective-permute-done.7.other) | copy-start | bytes 3244036
  66.2 18.1 %copy-start.4 = (f32[512]{0:T(512)S(1)}, f32[512]{0:T(512)}, u32[]{:S(2)}) copy-start(f32[512]{0:T(512)} %param.19) | copy-start | bytes 6148
  66.3 18.0 %all-to-all-start = ((bf16[16,64,128]{2,1,0:T(8,128)(2,1)}), bf16[16,64,128]{2,1,0:T(8,128)(2,1)S(1)}, u32[]{:S(2)}, u32[]{:S(2)}) async-start(bf16[16,64,128]{2,1,0:T(8,128)(2,1)} %get-tuple-element.28), calls=%async_computation | async-start | bytes 524288 | tf_op jit(solution)/shard_map/all_to_all | solution.py:410
  84.3 25.5 %copy-start.2 = (bf16[384,1408]{1,0:T(8,128)(2,1)S(1)}, bf16[384,1408]{1,0:T(8,128)(2,1)}, u32[]{:S(2)}) copy-start(bf16[384,1408]{1,0:T(8,128)(2,1)} %copy-done.1) | copy-start | bytes 3244036
  84.3 25.5 %copy-start.5 = (bf16[512,768]{1,0:T(8,128)(2,1)S(1)}, bf16[512,768]{1,0:T(8,128)(2,1)}, u32[]{:S(2)}) copy-start(bf16[512,768]{1,0:T(8,128)(2,1)} %get-tuple-element.33.saved) | copy-start | bytes 2359300
  84.3 25.5 %copy-start.6 = (f32[8,768]{1,0:T(8,128)S(1)}, f32[8,768]{1,0:T(8,128)}, u32[]{:S(2)}) copy-start(f32[8,768]{1,0:T(8,128)} %get-tuple-element.34.stats) | copy-start | bytes 73732
  160.7 12.5 %copy-start = (bf16[1408,512]{1,0:T(8,128)(2,1)S(1)}, bf16[1408,512]{1,0:T(8,128)(2,1)}, u32[]{:S(2)}) copy-start(bf16[1408,512]{1,0:T(8,128)(2,1)} %w_e2d.3) | copy-start | bytes 4325380
Sparse Core Ops, SparseCore 0:
  17.8 59.4 all-gather.2
